TPU v7x, 128 devices: a whole 4x4x4 slice. The times are simulated.
128 devices in a mesh: batch: 2 (over x_hi), blk: 16 (over x_lo, z, core), ulysses: 4 (over y).
Axes of the slice: x: 4 (x_hi: 2, x_lo: 2; x = x_hi * 2 + x_lo), y: 4, z: 4, core: 2. Of those that a mesh axis runs over, the one named last changes fastest.
Arguments:
- tokens: bfloat16 [16384, 768], P(('batch', 'blk', 'ulysses')), may hold values from -6 to 6
- stretch_order: int32 [2, 32], P('batch'), may hold values from 0 to 31, each once within a row
- ln_gain: bfloat16 [1, 1536], P(None, ('batch', 'blk', 'ulysses')), may hold values from 0.5 to 1.5
- ln_bias: bfloat16 [1, 1536], P(None, ('batch', 'blk', 'ulysses')), may hold values from -3 to 3
- w_qkv: bfloat16 [1, 768, 2304], P(None, ('batch', 'blk', 'ulysses')), may hold values from -0.21875 to 0.21875
- qv_bias: bfloat16 [1, 1536], P(None, ('batch', 'blk', 'ulysses')), may hold values from -4 to 4
- w_out: bfloat16 [1, 768, 768], P(None, ('batch', 'blk', 'ulysses')), may hold values from -0.875 to 0.875
- out_bias: bfloat16 [1, 768], P(None, ('batch', 'blk', 'ulysses')), may hold values from -3 to 3
- w_up: bfloat16 [1, 768, 3072], P(None, ('batch', 'blk', 'ulysses')), may hold values from -0.21875 to 0.21875
- up_bias: bfloat16 [1, 3072], P(None, ('batch', 'blk', 'ulysses')), may hold values from -4 to 4
- w_down: bfloat16 [1, 3072, 768], P(None, ('batch', 'blk', 'ulysses')), may hold values from -0.21875 to 0.21875
- down_bias: bfloat16 [1, 768], P(None, ('batch', 'blk', 'ulysses')), may hold values from -3 to 3
- cotangent: float32 [16384, 768], P(('batch', 'blk', 'ulysses')), may hold values from -6 to 6
Outputs:
- result: float32 [16384, 768], P(('batch', 'blk', 'ulysses'))
- d_tokens: float32 [16384, 768], P(('batch', 'blk', 'ulysses'))
- g_ln_gain: float32 [1, 1536], P(None, ('batch', 'blk', 'ulysses'))
- g_ln_bias: float32 [1, 1536], P(None, ('batch', 'blk', 'ulysses'))
- g_w_qkv: float32 [1, 768, 2304], P(None, ('batch', 'blk', 'ulysses'))
- g_qv_bias: float32 [1, 1536], P(None, ('batch', 'blk', 'ulysses'))
- g_w_out: float32 [1, 768, 768], P(None, ('batch', 'blk', 'ulysses'))
- g_out_bias: float32 [1, 768], P(None, ('batch', 'blk', 'ulysses'))
- g_w_up: float32 [1, 768, 3072], P(None, ('batch', 'blk', 'ulysses'))
- g_up_bias: float32 [1, 3072], P(None, ('batch', 'blk', 'ulysses'))
- g_w_down: float32 [1, 3072, 768], P(None, ('batch', 'blk', 'ulysses'))
- g_down_bias: float32 [1, 768], P(None, ('batch', 'blk', 'ulysses'))
Inputs may be any that keep to these rules, and one draw needn't show every extreme that they name: Each row of stretch_order is a permutation of the 32 stretches of 256 positions; stored rows 2 j * 256 to 2 (j + 1) * 256 - 1 of a sequence hold the stretches named at entries 2 j and 2 j + 1, in that order.
All inputs are finite; a program needn't handle non-finite values.
Results may differ from a plain program's by a relative error of at most 0.038.
Values may be sent and summed in bfloat16 or wider, within the bound.
No kernel may reach another device: no remote copies, remote signals or barrier semaphores. Data moves between devices by JAX's collectives and lax.ppermute only.
A program may use at most 256 MiB of HBM per device.

v0:
```python
import functools
import math

import jax
import jax.numpy as jnp
from jax import lax
from jax.experimental import pallas as pl
from jax.experimental.pallas import tpu as pltpu
from jax.sharding import PartitionSpec as P

HEADS = 12
HEAD_DIM = 64
NORM_EPS = 1e-05
FLOOR = -1e25
BELOW_FLOOR = -1e30
ALL = ("batch", "blk", "ulysses")
WIDE = ("batch", "blk")
BF16 = jnp.bfloat16
F32 = jnp.float32
NT = (((1,), (1,)), ((), ()))
VMEM_LIMIT = 60 * 1024 * 1024


def mm(a, b):
    return jnp.dot(a, b, preferred_element_type=F32)


def mm_nt(a, b):
    return lax.dot_general(a, b, NT, preferred_element_type=F32)


def mm_tn(a, b):
    return lax.dot_general(a, b, (((0,), (0,)), ((), ())), preferred_element_type=F32)


def allowed_tile(key_ranks, query_ranks, half, key_rows, query_cols):
    rows = lax.broadcasted_iota(jnp.int32, (key_rows, 1), 0)
    cols = lax.broadcasted_iota(jnp.int32, (1, query_cols), 1)

    def positions(index, ranks):
        if len(ranks) == 1:
            return ranks[0] * half + index
        return jnp.where(index < half, ranks[0] * half + index, (ranks[1] - 1) * half + index)

    return positions(rows, key_ranks) <= positions(cols, query_ranks)


def attend_kernel(
    ranks, own, qpad, kv, ctx_low, ctx, lse, v_turned, row_max, row_sum, total, *, half, heads
):
    step = pl.program_id(0)
    width = HEAD_DIM

    @pl.when(step == 0)
    def _():
        row_max[...] = jnp.full_like(row_max, FLOOR)
        row_sum[...] = jnp.zeros_like(row_sum)
        total[...] = jnp.zeros_like(total)

    key_ranks = (ranks[2 * step], ranks[2 * step + 1])
    low_rank = jnp.minimum(*key_ranks)
    high_rank = jnp.maximum(*key_ranks)
    v_turned[...] = kv[:, 128:].T

    def tile(part, masked):
        cols = slice(part * half, (part + 1) * half)
        if masked:
            allowed = allowed_tile(key_ranks, (own[part],), half, 2 * half, half)
        for h in range(heads):
            logits = mm_nt(kv[:, :256], qpad[h, cols, :])
            if masked:
                logits = jnp.where(allowed, logits, BELOW_FLOOR)
            old_max = row_max[h : h + 1, cols]
            new_max = jnp.maximum(old_max, jnp.max(logits, axis=0, keepdims=True))
            scale = jnp.exp(old_max - new_max)
            probs = jnp.exp(logits - new_max)
            row_max[h : h + 1, cols] = new_max
            row_sum[h : h + 1, cols] = row_sum[h : h + 1, cols] * scale + jnp.sum(
                probs, axis=0, keepdims=True
            )
            rows = slice(h * width, (h + 1) * width)
            values = v_turned[width * (h + 1) : width * (h + 2), :]
            total[rows, cols] = total[rows, cols] * scale + mm(values, probs.astype(BF16))

    for part in range(2):
        own_rank = own[part]

        @pl.when(high_rank < own_rank)
        def _():
            tile(part, False)

        @pl.when(jnp.logical_and(low_rank <= own_rank, own_rank <= high_rank))
        def _():
            tile(part, True)

    @pl.when(step == pl.num_programs(0) - 1)
    def _():
        for h in range(heads):
            rows = slice(h * width, (h + 1) * width)
            total[rows, :] = total[rows, :] / row_sum[h : h + 1, :]
        done = total[...].T
        ctx[...] = done
        ctx_low[...] = done.astype(BF16)
        lse[...] = row_max[...] + jnp.log(row_sum[...])


def query_grad_kernel(
    ranks, own, qpad, dpad, lse, delta, kv, d_query, k_turned, total, *, half, heads
):
    step = pl.program_id(0)
    width = HEAD_DIM

    @pl.when(step == 0)
    def _():
        total[...] = jnp.zeros_like(total)

    key_ranks = (ranks[2 * step], ranks[2 * step + 1])
    low_rank = jnp.minimum(*key_ranks)
    high_rank = jnp.maximum(*key_ranks)
    k_turned[...] = kv[:, :256].T

    def tile(part, masked):
        cols = slice(part * half, (part + 1) * half)
        if masked:
            allowed = allowed_tile(key_ranks, (own[part],), half, 2 * half, half)
        for h in range(heads):
            probs = jnp.exp(mm_nt(kv[:, :256], qpad[h, cols, :]) - lse[h : h + 1, cols])
            if masked:
                probs = jnp.where(allowed, probs, 0.0)
            d_probs = mm_nt(kv[:, 128:], dpad[h, cols, :])
            d_logits = (probs * (d_probs - delta[h : h + 1, cols])).astype(BF16)
            rows = slice(h * width, (h + 1) * width)
            total[rows, cols] += mm(k_turned[rows, :], d_logits)

    for part in range(2):
        own_rank = own[part]

        @pl.when(high_rank < own_rank)
        def _():
            tile(part, False)

        @pl.when(jnp.logical_and(low_rank <= own_rank, own_rank <= high_rank))
        def _():
            tile(part, True)

    @pl.when(step == pl.num_programs(0) - 1)
    def _():
        d_query[...] = (total[...] * (1.0 / math.sqrt(HEAD_DIM))).T.astype(BF16)


def key_grad_kernel(ranks, own, kpad, vpad, q_all, p_all, d_key, d_value, k_sum, v_sum, *, half, heads):
    step = pl.program_id(0)
    width = HEAD_DIM

    @pl.when(step == 0)
    def _():
        k_sum[...] = jnp.zeros_like(k_sum)
        v_sum[...] = jnp.zeros_like(v_sum)

    query_ranks = (ranks[2 * step], ranks[2 * step + 1])
    low_rank = jnp.minimum(*query_ranks)
    high_rank = jnp.maximum(*query_ranks)

    def tile(part, masked):
        rows = slice(part * half, (part + 1) * half)
        lane = lax.broadcasted_iota(jnp.int32, (2 * half, 256), 1)
        queries = q_all[...]
        packed = p_all[...]
        q_ext = jnp.where(lane < heads * width, queries, packed)
        if masked:
            allowed = allowed_tile((own[part],), query_ranks, half, half, 2 * half)
        k_new = jnp.zeros((half, 256), F32)
        v_new = jnp.zeros((half, 256), F32)
        zero = jnp.zeros_like(queries)
        for h in range(heads):
            here = jnp.logical_and(lane >= h * width, lane < (h + 1) * width)
            probs = jnp.exp(mm_nt(kpad[h, rows, :], q_ext))
            if masked:
                probs = jnp.where(allowed, probs, 0.0)
            d_probs = mm_nt(vpad[h, rows, :], packed)
            d_logits = (probs * d_probs).astype(BF16)
            k_new += mm(d_logits, jnp.where(here, queries, zero))
            v_new += mm(probs.astype(BF16), jnp.where(here, packed, zero))
        k_sum[rows, :] += k_new
        v_sum[rows, :] += v_new

    for part in range(2):
        own_rank = own[part]

        @pl.when(own_rank < low_rank)
        def _():
            tile(part, False)

        @pl.when(jnp.logical_and(low_rank <= own_rank, own_rank <= high_rank))
        def _():
            tile(part, True)

    @pl.when(step == pl.num_programs(0) - 1)
    def _():
        d_key[...] = k_sum[:, : heads * width].astype(BF16)
        d_value[...] = v_sum[:, : heads * width].astype(BF16)


def whole(shape):
    return pl.BlockSpec(shape, lambda i, *_: (0,) * len(shape))


def streamed(rows, cols):
    return pl.BlockSpec((rows, cols), lambda i, *_: (i, 0))


def cost(rows, keys, heads, products):
    area = rows * keys * heads
    return pl.CostEstimate(
        flops=2 * area * 256 * products, bytes_accessed=keys * 768, transcendentals=area
    )


def params():
    return pltpu.CompilerParams(
        dimension_semantics=("arbitrary",), vmem_limit_bytes=VMEM_LIMIT
    )


def attend(ranks, own, qpad, kv):
    heads, rows, _ = qpad.shape
    keys = kv.shape[0]
    width = heads * HEAD_DIM
    return pl.pallas_call(
        functools.partial(attend_kernel, half=rows // 2, heads=heads),
        out_shape=(
            jax.ShapeDtypeStruct((rows, width), BF16),
            jax.ShapeDtypeStruct((rows, width), F32),
            jax.ShapeDtypeStruct((8, rows), F32),
        ),
        grid_spec=pltpu.PrefetchScalarGridSpec(
            num_scalar_prefetch=2,
            grid=(keys // rows,),
            in_specs=[whole(qpad.shape), streamed(rows, kv.shape[1])],
            out_specs=[whole((rows, width)), whole((rows, width)), whole((8, rows))],
            scratch_shapes=[
                pltpu.VMEM((256, rows), BF16),
                pltpu.VMEM((8, rows), F32),
                pltpu.VMEM((8, rows), F32),
                pltpu.VMEM((width, rows), F32),
            ],
        ),
        compiler_params=params(),
        cost_estimate=cost(rows, keys, heads, 2),
        name="attend",
    )(ranks, own, qpad, kv)


def query_grad(ranks, own, qpad, dpad, lse, delta, kv):
    heads, rows, _ = qpad.shape
    keys = kv.shape[0]
    width = heads * HEAD_DIM
    return pl.pallas_call(
        functools.partial(query_grad_kernel, half=rows // 2, heads=heads),
        out_shape=jax.ShapeDtypeStruct((rows, width), BF16),
        grid_spec=pltpu.PrefetchScalarGridSpec(
            num_scalar_prefetch=2,
            grid=(keys // rows,),
            in_specs=[
                whole(qpad.shape),
                whole(dpad.shape),
                whole((8, rows)),
                whole((8, rows)),
                streamed(rows, kv.shape[1]),
            ],
            out_specs=whole((rows, width)),
            scratch_shapes=[pltpu.VMEM((256, rows), BF16), pltpu.VMEM((width, rows), F32)],
        ),
        compiler_params=params(),
        cost_estimate=cost(rows, keys, heads, 3),
        name="query_grad",
    )(ranks, own, qpad, dpad, lse, delta, kv)


def key_grad(ranks, own, kpad, vpad, q_all, p_all):
    heads, rows, _ = kpad.shape
    queries = q_all.shape[0]
    width = heads * HEAD_DIM
    return pl.pallas_call(
        functools.partial(key_grad_kernel, half=rows // 2, heads=heads),
        out_shape=(
            jax.ShapeDtypeStruct((rows, width), BF16),
            jax.ShapeDtypeStruct((rows, width), BF16),
        ),
        grid_spec=pltpu.PrefetchScalarGridSpec(
            num_scalar_prefetch=2,
            grid=(queries // rows,),
            in_specs=[
                whole(kpad.shape),
                whole(vpad.shape),
                streamed(rows, 256),
                streamed(rows, 256),
            ],
            out_specs=[whole((rows, width)), whole((rows, width))],
            scratch_shapes=[pltpu.VMEM((rows, 256), F32), pltpu.VMEM((rows, 256), F32)],
        ),
        compiler_params=params(),
        cost_estimate=cost(rows, queries, heads, 4),
        name="key_grad",
    )(ranks, own, kpad, vpad, q_all, p_all)


def weight_grads_kernel(h2, du, act, df, ctx, dc, out, g_out, *, owners):
    each = h2.shape[1] // owners
    few = ctx.shape[1] // owners
    chunk = h2.shape[1] // 2
    for i in range(2):
        cols = slice(i * chunk, (i + 1) * chunk)
        mine = slice(i * owners // 2, (i + 1) * owners // 2)
        shape = (owners // 2, each, du.shape[1])
        out[mine, :each, :] = mm_tn(h2[:, cols], du[...]).reshape(shape)
        out[mine, each : 2 * each, :] = mm_tn(act[:, cols], df[...]).reshape(shape)
    g_out[...] = mm_tn(ctx[...], dc[...])
    out[:, 2 * each :, :] = jnp.zeros((owners, out.shape[1] - 2 * each, out.shape[2]), F32)
    for w in range(owners):
        out[w, 2 * each : 2 * each + few, :] = g_out[w * few : (w + 1) * few, :]


def weight_grads(h2, du, act, df, ctx, dc, owners):
    width = du.shape[1]
    each = h2.shape[1] // owners
    rows = 2 * each + 8
    out = pl.pallas_call(
        functools.partial(weight_grads_kernel, owners=owners),
        out_shape=jax.ShapeDtypeStruct((owners, rows, width), F32),
        scratch_shapes=[pltpu.VMEM((ctx.shape[1], width), F32)],
        compiler_params=pltpu.CompilerParams(vmem_limit_bytes=VMEM_LIMIT),
        cost_estimate=pl.CostEstimate(
            flops=4 * h2.size * width, bytes_accessed=8 * owners * rows * width, transcendentals=0
        ),
        name="weight_grads",
    )(h2, du, act, df, ctx, dc)
    return out.reshape(owners * rows, width)


def normalized(values):
    mean = jnp.mean(values, axis=-1, keepdims=True)
    centered = values - mean
    spread = jnp.mean(centered * centered, axis=-1, keepdims=True)
    scale = lax.rsqrt(spread + NORM_EPS)
    return centered * scale, scale


def norm_back(grad, gain, normed, scale):
    e = grad * gain
    mean_e = jnp.mean(e, axis=-1, keepdims=True)
    mean_en = jnp.mean(e * normed, axis=-1, keepdims=True)
    return scale * (e - mean_e - normed * mean_en)


def gelu_tanh(values):
    return jax.nn.gelu(values, approximate=True)


def head_lanes(x, heads, first, ones_at=None):
    rows, width = x.shape
    wide = jnp.pad(x, ((0, 0), (first, 256 - width - first)))
    lane = lax.broadcasted_iota(jnp.int32, (heads, 1, 256), 2)
    head = lax.broadcasted_iota(jnp.int32, (heads, 1, 256), 0)
    start = first + head * HEAD_DIM
    here = jnp.logical_and(lane >= start, lane < start + HEAD_DIM)
    out = jnp.where(here, wide[None], jnp.zeros((), x.dtype))
    if ones_at is not None:
        at = ones_at + 3 * head
        out = jnp.where(jnp.logical_and(lane >= at, lane < at + 3), jnp.ones((), x.dtype), out)
    return out


def three_parts(x):
    high = lax.reduce_precision(x, 8, 7)
    mid = lax.reduce_precision(x - high, 8, 7)
    return jnp.stack([high, mid, x - high - mid], axis=-1).astype(BF16)


def to_all(x, axis="ulysses"):
    ways = lax.axis_size(axis)
    sent = jnp.broadcast_to(x[None], (ways,) + x.shape)
    return lax.all_to_all(sent, axis, split_axis=0, concat_axis=0, tiled=True)


def summed_at_owner(x, axis="ulysses"):
    ways = lax.axis_size(axis)
    sent = x.astype(BF16).reshape(ways, -1, x.shape[1])
    got = lax.all_to_all(sent, axis, split_axis=0, concat_axis=0, tiled=True)
    return jnp.sum(got.astype(F32), axis=0)


def on_device(
    tokens,
    stretch_order,
    ln_gain,
    ln_bias,
    w_qkv,
    qv_bias,
    w_out,
    out_bias,
    w_up,
    up_bias,
    w_down,
    down_bias,
    cotangent,
):
    own_rows, width = tokens.shape
    ways = lax.axis_size("ulysses")
    wide = lax.axis_size("batch") * lax.axis_size("blk")
    me = lax.axis_index("ulysses")
    rows = own_rows * ways
    heads = HEADS // ways
    part = width // ways
    held = w_qkv.shape[1]
    ff_held = w_down.shape[1]
    ff_part = ff_held * wide
    pair = 2 * held

    order = stretch_order[0]
    own = lax.dynamic_slice(order, (2 * lax.axis_index("blk"),), (2,))

    small = jnp.concatenate(
        [
            ln_gain,
            ln_bias,
            qv_bias,
            jnp.concatenate([out_bias, down_bias], axis=1),
            up_bias.reshape(2, pair),
        ],
        axis=0,
    )
    qkv_slices = w_qkv[0].reshape(held, 3, ways, part).transpose(2, 0, 1, 3).reshape(ways, held, 3 * part)
    up_slices = w_up[0].reshape(held, wide, ways, ff_held).transpose(2, 0, 1, 3).reshape(ways, held, ff_part)
    first = jnp.concatenate(
        [
            up_slices,
            jnp.broadcast_to(w_out[0][None], (ways, held, width)),
            qkv_slices,
            jnp.broadcast_to(small[None], (ways,) + small.shape),
            jnp.zeros((ways, held, 64 - pair), BF16),
        ],
        axis=2,
    )
    first = lax.all_to_all(first, "ulysses", split_axis=0, concat_axis=0, tiled=True)
    first = first.reshape(ways * held, -1)
    ffn = jnp.concatenate([first[:, : ff_part + width], w_down[0]], axis=1)
    ffn_all = lax.all_gather(ffn, WIDE, axis=0, tiled=True)
    filled = lax.all_gather(first[:, ff_part + width :], WIDE, axis=0, tiled=True)
    filled, tokens_late = lax.optimization_barrier((filled, tokens))
    x = to_all(tokens_late).reshape(rows, width).astype(F32)
    w_qkv_u = filled[:, : 3 * part]
    smalls = filled[:, 3 * part : 3 * part + pair].reshape(wide * ways, held, pair).astype(F32)
    gains = smalls[:, 0].reshape(-1)
    shifts = smalls[:, 1].reshape(-1)
    qv_all = smalls[:, 2].reshape(-1)
    out_bias_all = smalls[:, 3, :held].reshape(-1)
    down_bias_all = smalls[:, 3, held:].reshape(-1)
    up_bias_all = smalls[:, 4:].reshape(wide, ways, ff_held)
    up_bias_u = lax.dynamic_index_in_dim(up_bias_all, me, axis=1, keepdims=False).reshape(-1)
    bias_q = lax.dynamic_slice(qv_all, (me * part,), (part,))
    bias_v = lax.dynamic_slice(qv_all, (width + me * part,), (part,))

    n1, r1 = normalized(x)
    h1 = (n1 * gains[:width] + shifts[:width]).astype(BF16)
    proj_bias = jnp.concatenate([bias_q, jnp.zeros((part,), F32), bias_v])
    proj = (mm(h1, w_qkv_u) + proj_bias).astype(BF16)
    q_scaled = proj[:, :part] * jnp.asarray(1.0 / math.sqrt(HEAD_DIM), BF16)
    kv = proj[:, part:]
    kv_all = lax.all_gather(kv, "blk", axis=0, tiled=True)
    qpad = head_lanes(q_scaled, heads, 0)

    df_own = cotangent.astype(BF16)
    df_own, kv = lax.optimization_barrier((df_own, kv))
    df = to_all(df_own).reshape(rows, width)
    w_up_u = ffn_all[:, :ff_part]
    w_out_all = ffn_all[:, ff_part : ff_part + width]
    w_down_u = ffn_all[:, ff_part + width :]
    w_out_u = lax.dynamic_slice(w_out_all, (me * part, 0), (part, width))
    qpad, df, w_up_u, w_out_all, w_down_u, w_out_u = lax.optimization_barrier(
        (qpad, df, w_up_u, w_out_all, w_down_u, w_out_u)
    )
    q_wide = jnp.pad(q_scaled, ((0, 0), (0, 256 - part)))
    q_wide, kv_all = lax.optimization_barrier((q_wide, kv_all))
    q_all = lax.all_gather(q_wide, "blk", axis=0, tiled=True)

    ctx_low, ctx, lse = attend(order, own, qpad, kv_all)
    ctx_all = to_all(ctx_low)
    out = mm(ctx_all[0], w_out_all[:part])
    for u in range(1, ways):
        out += mm(ctx_all[u], w_out_all[u * part : (u + 1) * part])
    x2 = x + out + out_bias_all
    n2, r2 = normalized(x2)
    gain_two = gains[width:]
    h2 = (n2 * gain_two + shifts[width:]).astype(BF16)

    up = mm(h2, w_up_u) + up_bias_u
    act = gelu_tanh(up).astype(BF16)
    down = mm(act, w_down_u)
    d_act = mm_nt(df, w_down_u)
    _, gelu_pull = jax.vjp(gelu_tanh, up)
    du = gelu_pull(d_act)[0].astype(BF16)
    both = jnp.concatenate([mm_nt(du, w_up_u).astype(BF16), down.astype(BF16)], axis=1)
    both = summed_at_owner(both)
    dh2 = both[:, :width]

    def mine(a):
        return lax.dynamic_slice(a, (me * own_rows, 0), (own_rows, a.shape[1]))

    x2_own = mine(x2)
    result = both[:, width:] + x2_own + down_bias_all
    g_up_bias = jnp.sum(du.astype(F32), axis=0)
    g_down_bias = jnp.sum(df_own.astype(F32), axis=0)

    n2_own, r2_own = normalized(x2_own)
    dx2 = cotangent + norm_back(dh2, gain_two, n2_own, r2_own)
    g_gain_two = jnp.sum(dh2 * n2_own, axis=0)
    g_shift_two = jnp.sum(dh2, axis=0)
    dc_own, q_all = lax.optimization_barrier((dx2.astype(BF16), q_all))
    g_out_bias = jnp.sum(dc_own.astype(F32), axis=0)
    dc = to_all(dc_own).reshape(rows, width)
    dctx = mm_nt(dc, w_out_u).astype(BF16)
    early = weight_grads(h2, du, act, df, ctx_low, dc, wide)

    delta = jnp.sum((dctx.astype(F32) * ctx).reshape(rows, heads, HEAD_DIM), axis=2)
    lse_cols = lse[:heads].T
    packed = jnp.concatenate(
        [
            dctx,
            three_parts(-lse_cols).reshape(rows, 3 * heads),
            three_parts(-delta).reshape(rows, 3 * heads),
            jnp.zeros((rows, 256 - part - 6 * heads), BF16),
        ],
        axis=1,
    )
    packed_all = lax.all_gather(packed, "blk", axis=0, tiled=True)
    delta_rows = jnp.pad(delta.T, ((0, 8 - heads), (0, 0)))
    d_query = query_grad(order, own, qpad, head_lanes(dctx, heads, 64), lse, delta_rows, kv_all)
    kpad = head_lanes(kv[:, :part], heads, 0, part)
    vpad = head_lanes(kv[:, part:], heads, 0, part + 3 * heads)
    d_key, d_value = key_grad(order, own, kpad, vpad, q_all, packed_all)
    d_proj = jnp.concatenate([d_query, d_key, d_value], axis=1)
    dh1 = summed_at_owner(mm_nt(d_proj, w_qkv_u))
    g_w_qkv = mm_tn(h1, d_proj)
    n1_own, r1_own = normalized(tokens.astype(F32))
    d_tokens = dx2 + norm_back(dh1, gains[:width], n1_own, r1_own)
    g_gain_one = jnp.sum(dh1 * n1_own, axis=0)
    g_shift_one = jnp.sum(dh1, axis=0)

    early = lax.psum_scatter(early, WIDE, scatter_dimension=0, tiled=True)
    g_up_rows = early[:ff_held]
    o_w_down = early[ff_held : 2 * ff_held]
    out_rows = early[2 * ff_held : 2 * ff_held + held]
    count = wide * ways
    o_w_out = lax.ppermute(
        out_rows, ALL, [(w * ways + u, u * wide + w) for w in range(wide) for u in range(ways)]
    )

    d_sums = jnp.sum(d_proj.astype(F32), axis=0)
    g_qv = jnp.zeros((2, ways, part), F32)
    g_qv = lax.dynamic_update_slice(g_qv, d_sums[:part].reshape(1, 1, part), (0, me, 0))
    g_qv = lax.dynamic_update_slice(g_qv, d_sums[2 * part :].reshape(1, 1, part), (1, me, 0))
    g_up_full = jnp.zeros((wide, ways, ff_held), F32)
    g_up_full = lax.dynamic_update_slice(
        g_up_full, g_up_bias.reshape(wide, 1, ff_held), (0, me, 0)
    )
    small_grads = jnp.concatenate(
        [
            jnp.concatenate([g_gain_one, g_gain_two]).reshape(count, 1, pair),
            jnp.concatenate([g_shift_one, g_shift_two]).reshape(count, 1, pair),
            g_qv.reshape(count, 1, pair),
            jnp.concatenate(
                [g_out_bias.reshape(count, 1, held), g_down_bias.reshape(count, 1, held)], axis=2
            ),
            g_up_full.reshape(count, 2, pair),
        ],
        axis=1,
    ).reshape(count * held, pair)
    late = jnp.concatenate([g_w_qkv, jnp.pad(small_grads, ((0, 0), (0, 64 - pair)))], axis=1)
    late = summed_at_owner(late, WIDE)
    last = jnp.concatenate([late, g_up_rows], axis=1).reshape(ways, held, -1)
    last = lax.all_to_all(last, "ulysses", split_axis=0, concat_axis=0, tiled=True)
    o_w_qkv = last[:, :, : 3 * part].reshape(ways, held, 3, part).transpose(1, 2, 0, 3)
    o_small = jnp.sum(last[:, :, 3 * part : 3 * part + pair], axis=0)
    o_w_up = last[:, :, 3 * part + 64 :].reshape(ways, held, wide, ff_held).transpose(1, 2, 0, 3)
    return (
        result,
        d_tokens,
        o_small[0:1],
        o_small[1:2],
        o_w_qkv.reshape(1, held, 3 * width),
        o_small[2:3],
        o_w_out[None],
        o_small[3:4, :held],
        o_w_up.reshape(1, held, -1),
        o_small[4:6].reshape(1, ff_held),
        o_w_down[None],
        o_small[3:4, held:],
    )


def solution(mesh):
    rows = P(ALL, None)
    flat = P(None, ALL)
    deep = P(None, ALL, None)
    return jax.shard_map(
        on_device,
        mesh=mesh,
        in_specs=(
            rows, P("batch", None), flat, flat, deep, flat, deep, flat, deep, flat, deep, flat, rows,
        ),
        out_specs=(rows, rows, flat, flat, deep, flat, deep, flat, deep, flat, deep, flat),
        check_vma=False,
    )
```

profile of v0, /device:TPU:96, one launch (start us, length us, event | category | flops | bytes accessed | tf_op | source)
XLA Modules:
  0.0 445.3 jit_solution(4838013797640064748)
XLA Ops:
  7.2 1.1 reshape_squeeze.11
  10.1 1.3 reduce.13
  14.5 4.5 %all-to-all-start = ((bf16[4,6,2176]{2,1,0:T(8,128)(2,1)}), bf16[4,6,2176]{2,1,0:T(8,128)(2,1)S(1)}, u32[]{:S(2)}, u32[]{:S(2)}) async-start(bf16[4,6,2176]{2,1,0:T(8,128)(2,1)} %copy.251), calls=%async_computation | async-start | bytes 278528 | tf_op jit(solution)/shard_map/all_to_all | solution.py:445
  19.0 6.0 %all-to-all-done = bf16[4,6,2176]{2,1,0:T(8,128)(2,1)S(1)} async-done(((bf16[4,6,2176]{2,1,0:T(8,128)(2,1)}), bf16[4,6,2176]{2,1,0:T(8,128)(2,1)S(1)}, u32[]{:S(2)}, u32[]{:S(2)}) %all-to-all-start) | async-done | bytes 104480 | tf_op jit(solution)/shard_map/all_to_all | solution.py:445
  25.0 24.8 %all_gather.15 = bf16[768,640]{1,0:T(8,128)(2,1)S(1)} all-gather(bf16[24,640]{1,0:T(8,128)(2,1)S(1)} %slice.188), channel_id=1, replica_groups=mesh['batch'=2,'blk'=16,'ulysses'=4] {'batch','blk'}, dimensions={0}, use_global_device_ids=true | all-gather | bytes 1013760 | tf_op jit(solution)/shard_map/all_gather | solution.py:449
  51.4 3.5 all-to-all-start.1
  57.0 1.1 fusion.57
  59.5 8.5 %all-to-all-done.1 = bf16[4,128,768]{2,1,0:T(8,128)(2,1)S(1)} async-done(((bf16[4,128,768]{2,1,0:T(8,128)(2,1)}), bf16[4,128,768]{2,1,0:T(8,128)(2,1)S(1)}, u32[]{:S(2)}, u32[]{:S(2)}) %all-to-all-start.1) | async-done | bytes 786464 | tf_op jit(solution)/shard_map/all_to_all | solution.py:383
  76.0 4.2 all-to-all-start.2
  80.5 1.5 select_select_fusion
  82.0 29.9 %all-gather.7.cloned.1.call-done.kv = bf16[8192,384]{1,0:T(8,128)(2,1)} async-done(((bf16[512,384]{1,0:T(8,128)(2,1)}), bf16[8192,384]{1,0:T(8,128)(2,1)}) %all-gather.7.cloned.1.call-update) | async-done | bytes 6291472 | tf_op jit(solution)/shard_map/all_gather | solution.py:470
  111.9 49.0 %all-gather.5.cloned.1.call-done = bf16[768,2304]{1,0:T(8,128)(2,1)} async-done(((bf16[24,2304]{1,0:T(8,128)(2,1)}), bf16[768,2304]{1,0:T(8,128)(2,1)}) %all-gather.5.cloned.1.call-update) | async-done | bytes 3538960 | tf_op jit(solution)/shard_map/all_gather | solution.py:448
  160.9 3.6 fusion.55
  165.3 42.8 %attend.1 = (bf16[512,192]{1,0:T(8,128)(2,1)}, f32[512,192]{1,0:T(8,128)}, f32[8,512]{1,0:T(8,128)}) custom-call(s32[32]{0:T(128)} %bitcast.146, s32[2]{0:T(128)} %fusion.47.own, bf16[3,512,256]{2,1,0:T(8,128)(2,1)} %get-tuple-element.36.qpad, bf16[8192,384]{1,0:T(8,128)(2,1)} %all-gather.7.cloned.1.call-done.kv), custom_call_target="tpu_custom_call" | custom-call | flops 12884901888 | bytes 6291456 | tf_op jit(solution)/shard_map/attend/pallas_call | solution.py:229
  208.1 1.1 copy.257
  210.2 4.3 all-to-all-start.3
  214.8 1.1 fusion.56
  215.9 1.8 copy.258
  217.9 1.5 copy.259
  219.5 1.5 copy.260
  222.8 3.5 fusion.64
  226.3 1.3 fusion.34
  227.6 1.3 fusion.36
  229.0 1.3 fusion.32
  230.3 1.7 fusion.63
  233.8 2.4 convert_reduce_fusion.3
  238.8 1.3 pad_maximum_fusion
  240.1 4.9 %all-to-all-start.4 = ((bf16[4,128,1536]{2,1,0:T(8,128)(2,1)}), bf16[4,128,1536]{2,1,0:T(8,128)(2,1)S(1)}, u32[]{:S(2)}, u32[]{:S(2)}) async-start(bf16[4,128,1536]{2,1,0:T(8,128)(2,1)} %bitcast.131), calls=%async_computation.4 | async-start | bytes 3145728 | tf_op jit(solution)/shard_map/all_to_all | solution.py:389
  245.0 1.5 copy.262
  248.3 14.1 %all-to-all-done.4 = bf16[4,128,1536]{2,1,0:T(8,128)(2,1)S(1)} async-done(((bf16[4,128,1536]{2,1,0:T(8,128)(2,1)}), bf16[4,128,1536]{2,1,0:T(8,128)(2,1)S(1)}, u32[]{:S(2)}, u32[]{:S(2)}) %all-to-all-start.4) | async-done | bytes 1572896 | tf_op jit(solution)/shard_map/all_to_all | solution.py:389
  265.1 3.5 all-to-all-start.5
  269.0 9.1 %all-to-all-done.5 = bf16[4,128,768]{2,1,0:T(8,128)(2,1)S(1)} async-done(((bf16[4,128,768]{2,1,0:T(8,128)(2,1)}), bf16[4,128,768]{2,1,0:T(8,128)(2,1)S(1)}, u32[]{:S(2)}, u32[]{:S(2)}) %all-to-all-start.5) | async-done | bytes 786464 | tf_op jit(solution)/shard_map/all_to_all | solution.py:383
  280.5 6.3 %weight_grads.1 = f32[32,56,768]{2,1,0:T(8,128)} custom-call(bf16[512,768]{1,0:T(8,128)(2,1)} %copy-done.8, bf16[512,768]{1,0:T(8,128)(2,1)} %copy-done.18, bf16[512,768]{1,0:T(8,128)(2,1)} %copy-done.19, bf16[512,768]{1,0:T(8,128)(2,1)} %bitcast.6.df, bf16[512,192]{1,0:T(8,128)(2,1)} %get-tuple-element.38.ctx, bf16[512,768]{1,0:T(8,128)(2,1)} %bitcast.130), custom_call_target="tpu_custom_call" | custom-call | flops 1207959552 | bytes 11010048 | tf_op jit(solution)/shard_map/weight_grads/pallas_call | solution.py:328
  292.0 42.7 %query_grad.1 = bf16[512,192]{1,0:T(8,128)(2,1)} custom-call(s32[32]{0:T(128)} %bitcast.147, s32[2]{0:T(128)} %fusion.47.own, bf16[3,512,256]{2,1,0:T(8,128)(2,1)} %get-tuple-element.36.qpad, bf16[3,512,256]{2,1,0:T(8,128)(2,1)} %broadcast_select_fusion.dpad, f32[8,512]{1,0:T(8,128)} %get-tuple-element.44.lse, f32[8,512]{1,0:T(8,128)} %pad.26.delta, ...), custom_call_target="tpu_custom_call" | custom-call | flops 19327352832 | bytes 6291456 | tf_op jit(solution)/shard_map/query_grad/pallas_call | solution.py:258
  334.8 26.7 %key_grad.1 = (bf16[512,192]{1,0:T(8,128)(2,1)}, bf16[512,192]{1,0:T(8,128)(2,1)}) custom-call(s32[32]{0:T(128)} %bitcast.148, s32[2]{0:T(128)} %fusion.47.own, bf16[3,512,256]{2,1,0:T(8,128)(2,1)} %get-tuple-element.178.kpad, bf16[3,512,256]{2,1,0:T(8,128)(2,1)} %get-tuple-element.177.vpad, bf16[8192,256]{1,0:T(8,128)(2,1)} %all-gather.9.cloned.1.call-done.q_all, ...), custom_call_target="tpu_custom_call" | custom-call | flops 25769803776 | bytes 6291456 | tf_op jit(solution)/shard_map/key_grad/pallas_call | solution.py:284
  361.5 2.8 convolution_convert_fusion.3
  364.2 3.6 all-to-all-start.6
  370.0 1.9 convolution_convert_fusion
  371.9 5.4 %all-to-all-done.6 = bf16[4,128,768]{2,1,0:T(8,128)(2,1)S(1)} async-done(((bf16[4,128,768]{2,1,0:T(8,128)(2,1)}), bf16[4,128,768]{2,1,0:T(8,128)(2,1)S(1)}, u32[]{:S(2)}, u32[]{:S(2)}) %all-to-all-start.6) | async-done | bytes 786464 | tf_op jit(solution)/shard_map/all_to_all | solution.py:389
  379.0 1.1 pad_maximum_fusion.1
  380.1 9.6 %all-to-all-start.7 = ((bf16[32,24,640]{2,1,0:T(8,128)(2,1)}), bf16[32,24,640]{2,1,0:T(8,128)(2,1)S(1)}, u32[]{:S(2)}, u32[]{:S(2)}) async-start(bf16[32,24,640]{2,1,0:T(8,128)(2,1)} %pad_maximum_fusion.1), calls=%async_computation.7 | async-start | bytes 1966080 | tf_op jit(solution)/shard_map/all_to_all | solution.py:389
  389.7 20.0 %reduce-scatter.2.cloned.1.call-done = f32[56,768]{1,0:T(8,128)} async-done(((f32[1792,768]{1,0:T(8,128)}), f32[56,768]{1,0:T(8,128)}) %reduce-scatter.2.cloned.1.call-update) | async-done | bytes 172048 | tf_op jit(solution)/shard_map/reduce_scatter | solution.py:550
  410.5 3.6 collective-permute-start
  414.1 1.6 slice_bitcast_fusion.8
  415.7 3.9 collective-permute-done
  421.0 6.6 %all-to-all-start.8 = ((f32[4,6,1408]{2,1,0:T(8,128)}), f32[4,6,1408]{2,1,0:T(8,128)S(1)}, u32[]{:S(2)}, u32[]{:S(2)}) async-start(f32[4,6,1408]{2,1,0:T(8,128)} %reshape.405), calls=%async_computation.9 | async-start | bytes 360448 | tf_op jit(solution)/shard_map/all_to_all | solution.py:582
  428.6 5.3 %all-to-all-done.8 = f32[4,6,1408]{2,1,0:T(8,128)S(1)} async-done(((f32[4,6,1408]{2,1,0:T(8,128)}), f32[4,6,1408]{2,1,0:T(8,128)S(1)}, u32[]{:S(2)}, u32[]{:S(2)}) %all-to-all-start.8) | async-done | bytes 135200 | tf_op jit(solution)/shard_map/all_to_all | solution.py:582
  435.7 1.1 reshape.417
  (247 shorter events, 49.0 us)
Async XLA Ops:
  14.5 10.5 %all-to-all-start = ((bf16[4,6,2176]{2,1,0:T(8,128)(2,1)}), bf16[4,6,2176]{2,1,0:T(8,128)(2,1)S(1)}, u32[]{:S(2)}, u32[]{:S(2)}) async-start(bf16[4,6,2176]{2,1,0:T(8,128)(2,1)} %copy.251), calls=%async_computation | async-start | bytes 278528 | tf_op jit(solution)/shard_map/all_to_all | solution.py:445
  25.0 25.5 %copy-start.1 = (bf16[128,768]{1,0:T(8,128)(2,1)S(1)}, bf16[128,768]{1,0:T(8,128)(2,1)}, u32[]{:S(2)}) copy-start(bf16[128,768]{1,0:T(8,128)(2,1)} %param.13) | copy-start | bytes 589828
  49.8 19.1 %copy-start.4 = (bf16[768,640]{1,0:T(8,128)(2,1)}, bf16[768,640]{1,0:T(8,128)(2,1)S(1)}, u32[]{:S(2)}) copy-start(bf16[768,640]{1,0:T(8,128)(2,1)S(1)} %all_gather.15) | copy-start | bytes 2949124
  51.4 16.5 %all-to-all-start.1 = ((bf16[4,128,768]{2,1,0:T(8,128)(2,1)}), bf16[4,128,768]{2,1,0:T(8,128)(2,1)S(1)}, u32[]{:S(2)}, u32[]{:S(2)}) async-start(bf16[4,128,768]{2,1,0:T(8,128)(2,1)} %broadcast_in_dim.157), calls=%async_computation.1 | async-start | bytes 1572864 | tf_op jit(solution)/shard_map/all_to_all | solution.py:383
  54.9 57.0 %all-gather.7.cloned.1.call-start = ((), (), s32[]{:S(2)}) async-start(), calls=%async_computation.11 | async-start | bytes 6684672 | tf_op jit(solution)/shard_map/all_gather | solution.py:470
  69.0 2.8 copy-start.29
  70.7 1.7 copy-start.12
  70.7 1.8 copy-start.36
  71.6 3.3 copy-start.3
  71.7 89.2 %all-gather.5.cloned.1.call-start = ((), (), s32[]{:S(2)}) async-start(), calls=%async_computation.10 | async-start | bytes 3649536 | tf_op jit(solution)/shard_map/all_gather | solution.py:448
  72.4 3.6 copy-start.10
  74.9 5.6 %copy-start.9 = (bf16[512,256]{1,0:T(8,128)(2,1)}, bf16[512,256]{1,0:T(8,128)(2,1)S(1)}, u32[]{:S(2)}) copy-start(bf16[512,256]{1,0:T(8,128)(2,1)S(1)} %pad.24) | copy-start | bytes 786436
  75.1 5.4 %copy-start.35 = (pred[256]{0:T(512)(128)(4,1)S(1)}, pred[256]{0:T(512)(128)(4,1)}, u32[]{:S(2)}) copy-start(pred[256]{0:T(512)(128)(4,1)} %constant.92.clone.1) | copy-start | bytes 772
  76.0 89.2 %all-to-all-start.2 = ((bf16[4,128,768]{2,1,0:T(8,128)(2,1)}), bf16[4,128,768]{2,1,0:T(8,128)(2,1)}, u32[]{:S(2)}, u32[]{:S(2)}) async-start(bf16[4,128,768]{2,1,0:T(8,128)(2,1)} %broadcast_in_dim.161), calls=%async_computation.2 | async-start | bytes 1572864 | tf_op jit(solution)/shard_map/all_to_all | solution.py:383
  80.2 183.9 %all-gather.9.cloned.1.call-start = ((), (), s32[]{:S(2)}) async-start(), calls=%async_computation.12 | async-start | bytes 4456448 | tf_op jit(solution)/shard_map/all_gather | solution.py:485
  210.2 16.1 %all-to-all-start.3 = ((bf16[4,512,192]{1,2,0:T(8,128)(2,1)}), bf16[4,512,192]{1,2,0:T(8,128)(2,1)}, u32[]{:S(2)}, u32[]{:S(2)}) async-start(bf16[4,512,192]{1,2,0:T(8,128)(2,1)} %broadcast_in_dim.162), calls=%async_computation.3 | async-start | bytes 1572864 | tf_op jit(solution)/shard_map/all_to_all | solution.py:383
  232.0 1.4 copy-start.37
  232.3 1.5 copy-start.17
  232.3 1.5 copy-start.32
  233.8 2.4 copy-start.8
  236.2 1.2 copy-start.19
  236.2 1.8 copy-start.16
  240.1 4.9 %copy-start.14 = (f32[128,1,6]{1,0,2:T(8,128)S(1)}, f32[128,1,6]{1,0,2:T(8,128)}, u32[]{:S(2)}) copy-start(f32[128,1,6]{1,0,2:T(8,128)} %get-tuple-element.150) | copy-start | bytes 9220
  240.1 22.3 %all-to-all-start.4 = ((bf16[4,128,1536]{2,1,0:T(8,128)(2,1)}), bf16[4,128,1536]{2,1,0:T(8,128)(2,1)S(1)}, u32[]{:S(2)}, u32[]{:S(2)}) async-start(bf16[4,128,1536]{2,1,0:T(8,128)(2,1)} %bitcast.131), calls=%async_computation.4 | async-start | bytes 3145728 | tf_op jit(solution)/shard_map/all_to_all | solution.py:389
  248.3 15.0 %copy-start.13 = (f32[128,768]{1,0:T(8,128)S(1)}, f32[128,768]{1,0:T(8,128)}, u32[]{:S(2)}) copy-start(f32[128,768]{1,0:T(8,128)} %param.25) | copy-start | bytes 1179652
  264.2 4.6 %copy-start.33 = (f32[8,512]{1,0:T(8,128)S(1)}, f32[8,512]{1,0:T(8,128)}, u32[]{:S(2)}) copy-start(f32[8,512]{1,0:T(8,128)} %get-tuple-element.44.lse) | copy-start | bytes 49156
  264.2 13.9 %copy-start.15 = (bf16[192,768]{1,0:T(8,128)(2,1)S(1)}, bf16[192,768]{1,0:T(8,128)(2,1)}, u32[]{:S(2)}) copy-start(bf16[192,768]{1,0:T(8,128)(2,1)} %constant_dynamic-slice_fusion.1) | copy-start | bytes 884740
  264.2 13.9 %copy-start.21 = (f32[512,192]{1,0:T(8,128)S(1)}, f32[512,192]{1,0:T(8,128)}, u32[]{:S(2)}) copy-start(f32[512,192]{1,0:T(8,128)} %get-tuple-element.45) | copy-start | bytes 1179652
  265.1 13.0 %all-to-all-start.5 = ((bf16[4,128,768]{2,1,0:T(8,128)(2,1)}), bf16[4,128,768]{2,1,0:T(8,128)(2,1)S(1)}, u32[]{:S(2)}, u32[]{:S(2)}) async-start(bf16[4,128,768]{2,1,0:T(8,128)(2,1)} %broadcast_in_dim.164), calls=%async_computation.5 | async-start | bytes 1572864 | tf_op jit(solution)/shard_map/all_to_all | solution.py:383
  268.6 66.1 %all-gather.11.cloned.1.call-start = ((), (), s32[]{:S(2)}) async-start(), calls=%async_computation.13 | async-start | bytes 4456448 | tf_op jit(solution)/shard_map/all_gather | solution.py:536
  278.1 0.9 copy-start
  280.2 129.6 %reduce-scatter.2.cloned.1.call-start = ((), (), s32[]{:S(2)}) async-start(), calls=%async_computation.14 | async-start | bytes 5677056 | tf_op jit(solution)/shard_map/reduce_scatter | solution.py:550
  286.7 0.9 copy-start.2
  286.7 1.3 copy-start.11
  286.7 1.3 copy-start.7
  287.7 3.4 copy-start.30
  334.7 26.7 %copy-start.5 = (bf16[768,640]{1,0:T(8,128)(2,1)S(1)}, bf16[768,640]{1,0:T(8,128)(2,1)}, u32[]{:S(2)}) copy-start(bf16[768,640]{1,0:T(8,128)(2,1)} %copy-done.4) | copy-start | bytes 2949124
  334.7 26.7 %copy-start.22 = (bf16[512,192]{1,0:T(8,128)(2,1)S(1)}, bf16[512,192]{1,0:T(8,128)(2,1)}, u32[]{:S(2)}) copy-start(bf16[512,192]{1,0:T(8,128)(2,1)} %query_grad.1) | copy-start | bytes 589828
  364.2 4.4 copy-start.23
  364.2 4.4 copy-start.24
  364.2 13.1 %all-to-all-start.6 = ((bf16[4,128,768]{2,1,0:T(8,128)(2,1)}), bf16[4,128,768]{2,1,0:T(8,128)(2,1)S(1)}, u32[]{:S(2)}, u32[]{:S(2)}) async-start(bf16[4,128,768]{2,1,0:T(8,128)(2,1)} %bitcast.23), calls=%async_computation.6 | async-start | bytes 1572864 | tf_op jit(solution)/shard_map/all_to_all | solution.py:389
  371.9 6.3 %copy-start.28 = (bf16[64,1,12]{2,0,1:T(8,128)(2,1)S(1)}, bf16[64,1,12]{2,0,1:T(8,128)(2,1)}, u32[]{:S(2)}) copy-start(bf16[64,1,12]{2,0,1:T(8,128)(2,1)} %concatenate.69) | copy-start | bytes 4612
  371.9 6.3 %copy-start.25 = (bf16[128,2,12]{2,1,0:T(2,128)(2,1)S(1)}, bf16[128,2,12]{2,1,0:T(2,128)(2,1)}, u32[]{:S(2)}) copy-start(bf16[128,2,12]{2,1,0:T(2,128)(2,1)} %reshape.402) | copy-start | bytes 18436
  371.9 6.3 %copy-start.26 = (bf16[128,1,12]{2,1,0:T(2,128)(2,1)S(1)}, bf16[128,1,12]{2,1,0:T(2,128)(2,1)}, u32[]{:S(2)}) copy-start(bf16[128,1,12]{2,1,0:T(2,128)(2,1)} %copy.275) | copy-start | bytes 9220
  371.9 6.3 %copy-start.27 = (bf16[128,1,12]{2,1,0:T(2,128)(2,1)S(1)}, bf16[128,1,12]{2,1,0:T(2,128)(2,1)}, u32[]{:S(2)}) copy-start(bf16[128,1,12]{2,1,0:T(2,128)(2,1)} %reshape.414) | copy-start | bytes 9220
  380.1 40.1 %all-to-all-start.7 = ((bf16[32,24,640]{2,1,0:T(8,128)(2,1)}), bf16[32,24,640]{2,1,0:T(8,128)(2,1)S(1)}, u32[]{:S(2)}, u32[]{:S(2)}) async-start(bf16[32,24,640]{2,1,0:T(8,128)(2,1)} %pad_maximum_fusion.1), calls=%async_computation.7 | async-start | bytes 1966080 | tf_op jit(solution)/shard_map/all_to_all | solution.py:389
  410.5 9.0 %collective-permute-start = (f32[6,768]{1,0:T(8,128)S(1)}, f32[6,768]{1,0:T(8,128)S(1)}, u32[]{:S(2)}, u32[]{:S(2)}) collective-permute-start(f32[6,768]{1,0:T(8,128)S(1)} %slice.213), channel_id=1, source_target_pairs={{0,0},{1,32},{2,64},{3,96},{4,1},{5,33},{6,65},{7,97},{8,2},{9,34}... | collective-permute-start | bytes 55304 | tf_op jit(solution)/shard_map/ppermute | solution.py:555
  421.0 12.9 %all-to-all-start.8 = ((f32[4,6,1408]{2,1,0:T(8,128)}), f32[4,6,1408]{2,1,0:T(8,128)S(1)}, u32[]{:S(2)}, u32[]{:S(2)}) async-start(f32[4,6,1408]{2,1,0:T(8,128)} %reshape.405), calls=%async_computation.9 | async-start | bytes 360448 | tf_op jit(solution)/shard_map/all_to_all | solution.py:582
  (5 other events, 4.1 us)
Sparse Core Ops, SparseCore 0:
  71.8 40.0 all-gather.6
  114.8 46.0 all-gather.4
  162.6 36.8 all-gather.8
  280.3 36.3 all-gather.10
  320.3 89.3 reduce-scatter.1
where the time goes:
time: 453 us; the launch traced here: 445 us
  waiting for transfers between devices  151 us (33%)
  Pallas kernels  119 us (26%)
  local copies, waits for them, and re-layouts  51.2 us (11%)
  starting transfers between devices  48.9 us (11%)
  blocking collectives  24.8 us (5%)
  matrix products  18.9 us (4%)
  other arithmetic  16.6 us (4%)
  between operations  15.1 us (3%)
    all_gather x1, waiting for transfers between devices, on_device(): ffn_all = lax.all_gather(ffn, WIDE, axis=0, tiled=True)  49 us
    pallas_call x1, Pallas kernels, attend(): pl.pallas_call(functools.partial(attend_kernel, half=rows // 2, heads=hea...  42.8 us
    pallas_call x1, Pallas kernels, query_grad(): pl.pallas_call(functools.partial(query_grad_kernel, half=rows // 2, heads...  42.7 us
    all_gather x1, waiting for transfers between devices, on_device(): kv_all = lax.all_gather(kv, 'blk', axis=0, tiled=True)  29.9 us
    pallas_call x1, Pallas kernels, key_grad(): pl.pallas_call(functools.partial(key_grad_kernel, half=rows // 2, heads=h...  26.7 us
    all_gather x1, blocking collectives, on_device(): lax.all_gather(first[:, ff_part + width:], WIDE, axis=0, tiled=True)  24.8 us
    reduce_scatter x1, waiting for transfers between devices, on_device(): early = lax.psum_scatter(early, WIDE, scatter_dimension=0, tiled=True)  20 us
    all_to_all x3, waiting for transfers between devices, summed_at_owner(): got = lax.all_to_all(sent, axis, split_axis=0, concat_axis=0, tiled=True)  19.5 us
  transfers between devices with their start and end apart: 15, of which 10 were waited for; matrix products, arithmetic and copies ran while one was open for 14% of the time, Pallas kernels for 27%

commit v1 on v0

--- a/solution.py
+++ b/solution.py
@@ -6,15 +6,17 @@
 from jax import lax
 from jax.experimental import pallas as pl
 from jax.experimental.pallas import tpu as pltpu
-from jax.sharding import PartitionSpec as P
+from jax.sharding import Mesh, PartitionSpec as P
 
 HEADS = 12
 HEAD_DIM = 64
 NORM_EPS = 1e-05
 FLOOR = -1e25
 BELOW_FLOOR = -1e30
-ALL = ("batch", "blk", "ulysses")
-WIDE = ("batch", "blk")
+BLK = ("xlo", "z", "core")
+CHIPS = ("batch", "xlo", "z")
+WIDE = ("batch", "xlo", "z", "core")
+ALL = ("batch", "xlo", "z", "core", "ulysses")
 BF16 = jnp.bfloat16
 F32 = jnp.float32
 NT = (((1,), (1,)), ((), ()))
@@ -305,37 +307,132 @@
     )(ranks, own, kpad, vpad, q_all, p_all)
 
 
-def weight_grads_kernel(h2, du, act, df, ctx, dc, out, g_out, *, owners):
+def feed_forward_kernel(
+    me, x, ctx, df, vectors, w_up, w_out, w_down, x2_own, h2, act, du, dh2, down
+):
+    part = ctx.shape[2]
+    total = x[...].astype(F32) + vectors[2:3, :]
+    for u in range(ctx.shape[0]):
+        total += mm(ctx[u], w_out[u * part : (u + 1) * part, :])
+
+    @pl.when(pl.program_id(0) == me[0])
+    def _():
+        x2_own[...] = total
+
+    normed, _ = normalized(total)
+    h2_low = (normed * vectors[0:1, :] + vectors[1:2, :]).astype(BF16)
+    h2[...] = h2_low
+    up = mm(h2_low, w_up[...]) + vectors[3:4, :]
+    bend = math.sqrt(2.0 / math.pi)
+    square = up * up
+    turn = jnp.tanh(bend * (up + 0.044715 * square * up))
+    half = 0.5 * (1.0 + turn)
+    act_low = (up * half).astype(BF16)
+    act[...] = act_low
+    down[...] = mm(act_low, w_down[...]).astype(BF16)
+    slope = half + 0.5 * up * (1.0 - turn * turn) * (bend * (1.0 + 3 * 0.044715 * square))
+    du_low = (slope * mm_nt(df[...], w_down[...])).astype(BF16)
+    du[...] = du_low
+    dh2[...] = mm_nt(du_low, w_up[...]).astype(BF16)
+
+
+def feed_forward(me, x, ctx, df, vectors, weights):
+    rows, width = x.shape
+    ways, _, part = ctx.shape
+    step = rows // ways
+
+    def along(cols):
+        return pl.BlockSpec((step, cols), lambda i, *_: (i, 0))
+
+    def third(c):
+        return pl.BlockSpec((weights.shape[0], width), lambda i, *_: (0, c))
+
+    flat = jax.ShapeDtypeStruct((rows, width), BF16)
+    return pl.pallas_call(
+        feed_forward_kernel,
+        out_shape=(jax.ShapeDtypeStruct((step, width), F32), flat, flat, flat, flat, flat),
+        grid_spec=pltpu.PrefetchScalarGridSpec(
+            num_scalar_prefetch=1,
+            grid=(ways,),
+            in_specs=[
+                along(width),
+                pl.BlockSpec((ways, step, part), lambda i, *_: (0, i, 0)),
+                along(width),
+                whole(vectors.shape),
+                third(0),
+                third(1),
+                third(2),
+            ],
+            out_specs=[whole((step, width))] + [along(width)] * 5,
+        ),
+        compiler_params=params(),
+        cost_estimate=pl.CostEstimate(
+            flops=10 * rows * width * width, bytes_accessed=6 * width * width, transcendentals=rows * width
+        ),
+        name="feed_forward",
+    )(me, x, ctx, df, vectors, weights, weights, weights)
+
+
+def weight_grads_kernel(core, h2, du, act, df, ctx, dc, kept, sent, g_up, g_down, g_out):
+    chips, rows, width = kept.shape
+    owners = 2 * chips
     each = h2.shape[1] // owners
     few = ctx.shape[1] // owners
     chunk = h2.shape[1] // 2
     for i in range(2):
         cols = slice(i * chunk, (i + 1) * chunk)
-        mine = slice(i * owners // 2, (i + 1) * owners // 2)
-        shape = (owners // 2, each, du.shape[1])
-        out[mine, :each, :] = mm_tn(h2[:, cols], du[...]).reshape(shape)
-        out[mine, each : 2 * each, :] = mm_tn(act[:, cols], df[...]).reshape(shape)
+        g_up[cols, :] = mm_tn(h2[:, cols], du[...])
+        g_down[cols, :] = mm_tn(act[:, cols], df[...])
     g_out[...] = mm_tn(ctx[...], dc[...])
-    out[:, 2 * each :, :] = jnp.zeros((owners, out.shape[1] - 2 * each, out.shape[2]), F32)
-    for w in range(owners):
-        out[w, 2 * each : 2 * each + few, :] = g_out[w * few : (w + 1) * few, :]
-
-
-def weight_grads(h2, du, act, df, ctx, dc, owners):
+
+    def put(target, which):
+        target[:, 2 * each :, :] = jnp.zeros((chips, rows - 2 * each, width), target.dtype)
+        for g in range(chips):
+            w = 2 * g + which
+            target[g, :each, :] = g_up[w * each : (w + 1) * each, :].astype(target.dtype)
+            target[g, each : 2 * each, :] = g_down[w * each : (w + 1) * each, :].astype(target.dtype)
+            target[g, 2 * each : 2 * each + few, :] = g_out[w * few : (w + 1) * few, :].astype(
+                target.dtype
+            )
+
+    for which in range(2):
+
+        @pl.when(core[0] == which)
+        def _():
+            put(kept, which)
+            put(sent, 1 - which)
+
+
+def weight_grads(core, h2, du, act, df, ctx, dc, owners):
     width = du.shape[1]
-    each = h2.shape[1] // owners
-    rows = 2 * each + 8
-    out = pl.pallas_call(
-        functools.partial(weight_grads_kernel, owners=owners),
-        out_shape=jax.ShapeDtypeStruct((owners, rows, width), F32),
-        scratch_shapes=[pltpu.VMEM((ctx.shape[1], width), F32)],
-        compiler_params=pltpu.CompilerParams(vmem_limit_bytes=VMEM_LIMIT),
+    units = h2.shape[1]
+    rows = 2 * units // owners + 8
+    chips = owners // 2
+    arrays = (h2, du, act, df, ctx, dc)
+    kept, sent = pl.pallas_call(
+        weight_grads_kernel,
+        out_shape=(
+            jax.ShapeDtypeStruct((chips, rows, width), F32),
+            jax.ShapeDtypeStruct((chips, rows, width), BF16),
+        ),
+        grid_spec=pltpu.PrefetchScalarGridSpec(
+            num_scalar_prefetch=1,
+            grid=(1,),
+            in_specs=[whole(a.shape) for a in arrays],
+            out_specs=[whole((chips, rows, width))] * 2,
+            scratch_shapes=[
+                pltpu.VMEM((units, width), F32),
+                pltpu.VMEM((units, width), F32),
+                pltpu.VMEM((ctx.shape[1], width), F32),
+            ],
+        ),
+        compiler_params=params(),
         cost_estimate=pl.CostEstimate(
-            flops=4 * h2.size * width, bytes_accessed=8 * owners * rows * width, transcendentals=0
+            flops=4 * h2.size * width, bytes_accessed=6 * chips * rows * width, transcendentals=0
         ),
         name="weight_grads",
-    )(h2, du, act, df, ctx, dc)
-    return out.reshape(owners * rows, width)
+    )(core, *arrays)
+    return kept.reshape(chips * rows, width), sent.reshape(chips * rows, width)
 
 
 def normalized(values):
@@ -407,7 +504,7 @@
 ):
     own_rows, width = tokens.shape
     ways = lax.axis_size("ulysses")
-    wide = lax.axis_size("batch") * lax.axis_size("blk")
+    wide = lax.axis_size(WIDE)
     me = lax.axis_index("ulysses")
     rows = own_rows * ways
     heads = HEADS // ways
@@ -418,7 +515,7 @@
     pair = 2 * held
 
     order = stretch_order[0]
-    own = lax.dynamic_slice(order, (2 * lax.axis_index("blk"),), (2,))
+    own = lax.dynamic_slice(order, (2 * lax.axis_index(BLK),), (2,))
 
     small = jnp.concatenate(
         [
@@ -434,21 +531,38 @@
     up_slices = w_up[0].reshape(held, wide, ways, ff_held).transpose(2, 0, 1, 3).reshape(ways, held, ff_part)
     first = jnp.concatenate(
         [
-            up_slices,
-            jnp.broadcast_to(w_out[0][None], (ways, held, width)),
             qkv_slices,
             jnp.broadcast_to(small[None], (ways,) + small.shape),
-            jnp.zeros((ways, held, 64 - pair), BF16),
+            jnp.zeros((ways, held, width - 3 * part - pair), BF16),
         ],
         axis=2,
     )
-    first = lax.all_to_all(first, "ulysses", split_axis=0, concat_axis=0, tiled=True)
-    first = first.reshape(ways * held, -1)
-    ffn = jnp.concatenate([first[:, : ff_part + width], w_down[0]], axis=1)
-    ffn_all = lax.all_gather(ffn, WIDE, axis=0, tiled=True)
-    filled = lax.all_gather(first[:, ff_part + width :], WIDE, axis=0, tiled=True)
-    filled, tokens_late = lax.optimization_barrier((filled, tokens))
-    x = to_all(tokens_late).reshape(rows, width).astype(F32)
+    blank = jnp.zeros((ways, 8 - held, width), BF16)
+    sent = jnp.concatenate(
+        [
+            jnp.broadcast_to(tokens[None], (ways,) + tokens.shape),
+            first,
+            blank,
+            up_slices,
+            blank,
+            jnp.broadcast_to(w_out[0][None], (ways, held, width)),
+            blank,
+        ],
+        axis=1,
+    )
+    got = lax.all_to_all(sent, "ulysses", split_axis=0, concat_axis=0, tiled=True)
+    x = got[:, :own_rows].reshape(rows, width)
+    at = own_rows
+    piece = got[:, at : at + held, : 3 * part + 64].reshape(ways * held, 3 * part + 64)
+    filled = lax.all_gather(piece, WIDE, axis=0, tiled=True)
+    ffn = jnp.concatenate(
+        [
+            got[:, at + 8 : at + 8 + held].reshape(ways * held, width),
+            got[:, at + 16 : at + 16 + held].reshape(ways * held, width),
+            w_down[0],
+        ],
+        axis=1,
+    )
     w_qkv_u = filled[:, : 3 * part]
     smalls = filled[:, 3 * part : 3 * part + pair].reshape(wide * ways, held, pair).astype(F32)
     gains = smalls[:, 0].reshape(-1)
@@ -461,54 +575,35 @@
     bias_q = lax.dynamic_slice(qv_all, (me * part,), (part,))
     bias_v = lax.dynamic_slice(qv_all, (width + me * part,), (part,))
 
-    n1, r1 = normalized(x)
+    n1, r1 = normalized(x.astype(F32))
     h1 = (n1 * gains[:width] + shifts[:width]).astype(BF16)
     proj_bias = jnp.concatenate([bias_q, jnp.zeros((part,), F32), bias_v])
     proj = (mm(h1, w_qkv_u) + proj_bias).astype(BF16)
     q_scaled = proj[:, :part] * jnp.asarray(1.0 / math.sqrt(HEAD_DIM), BF16)
     kv = proj[:, part:]
-    kv_all = lax.all_gather(kv, "blk", axis=0, tiled=True)
+    kv_all = lax.all_gather(kv, BLK, axis=0, tiled=True)
     qpad = head_lanes(q_scaled, heads, 0)
 
     df_own = cotangent.astype(BF16)
     df_own, kv = lax.optimization_barrier((df_own, kv))
     df = to_all(df_own).reshape(rows, width)
-    w_up_u = ffn_all[:, :ff_part]
-    w_out_all = ffn_all[:, ff_part : ff_part + width]
-    w_down_u = ffn_all[:, ff_part + width :]
-    w_out_u = lax.dynamic_slice(w_out_all, (me * part, 0), (part, width))
-    qpad, df, w_up_u, w_out_all, w_down_u, w_out_u = lax.optimization_barrier(
-        (qpad, df, w_up_u, w_out_all, w_down_u, w_out_u)
-    )
+    qpad, df = lax.optimization_barrier((qpad, df))
+    ffn, kv_all = lax.optimization_barrier((ffn, kv_all))
+    ffn_all = lax.all_gather(ffn, WIDE, axis=0, tiled=True)
     q_wide = jnp.pad(q_scaled, ((0, 0), (0, 256 - part)))
-    q_wide, kv_all = lax.optimization_barrier((q_wide, kv_all))
-    q_all = lax.all_gather(q_wide, "blk", axis=0, tiled=True)
+    q_wide, ffn_all = lax.optimization_barrier((q_wide, ffn_all))
+    q_all = lax.all_gather(q_wide, BLK, axis=0, tiled=True)
 
     ctx_low, ctx, lse = attend(order, own, qpad, kv_all)
     ctx_all = to_all(ctx_low)
-    out = mm(ctx_all[0], w_out_all[:part])
-    for u in range(1, ways):
-        out += mm(ctx_all[u], w_out_all[u * part : (u + 1) * part])
-    x2 = x + out + out_bias_all
-    n2, r2 = normalized(x2)
     gain_two = gains[width:]
-    h2 = (n2 * gain_two + shifts[width:]).astype(BF16)
-
-    up = mm(h2, w_up_u) + up_bias_u
-    act = gelu_tanh(up).astype(BF16)
-    down = mm(act, w_down_u)
-    d_act = mm_nt(df, w_down_u)
-    _, gelu_pull = jax.vjp(gelu_tanh, up)
-    du = gelu_pull(d_act)[0].astype(BF16)
-    both = jnp.concatenate([mm_nt(du, w_up_u).astype(BF16), down.astype(BF16)], axis=1)
-    both = summed_at_owner(both)
-    dh2 = both[:, :width]
-
-    def mine(a):
-        return lax.dynamic_slice(a, (me * own_rows, 0), (own_rows, a.shape[1]))
-
-    x2_own = mine(x2)
-    result = both[:, width:] + x2_own + down_bias_all
+    vectors = jnp.stack(
+        [gain_two, shifts[width:], out_bias_all, up_bias_u] + [jnp.zeros((width,), F32)] * 4
+    )
+    x2_own, h2, act, du, dh2, down = feed_forward(me[None], x, ctx_all, df, vectors, ffn_all)
+    dh2 = summed_at_owner(dh2)
+    w_out_u = lax.dynamic_slice(ffn_all, (me * part, width), (part, width))
+    result = summed_at_owner(down) + x2_own + down_bias_all
     g_up_bias = jnp.sum(du.astype(F32), axis=0)
     g_down_bias = jnp.sum(df_own.astype(F32), axis=0)
 
@@ -520,7 +615,8 @@
     g_out_bias = jnp.sum(dc_own.astype(F32), axis=0)
     dc = to_all(dc_own).reshape(rows, width)
     dctx = mm_nt(dc, w_out_u).astype(BF16)
-    early = weight_grads(h2, du, act, df, ctx_low, dc, wide)
+    core = lax.axis_index("core")
+    early, early_sent = weight_grads(core[None], h2, du, act, df, ctx_low, dc, wide)
 
     delta = jnp.sum((dctx.astype(F32) * ctx).reshape(rows, heads, HEAD_DIM), axis=2)
     lse_cols = lse[:heads].T
@@ -533,7 +629,7 @@
         ],
         axis=1,
     )
-    packed_all = lax.all_gather(packed, "blk", axis=0, tiled=True)
+    packed_all = lax.all_gather(packed, BLK, axis=0, tiled=True)
     delta_rows = jnp.pad(delta.T, ((0, 8 - heads), (0, 0)))
     d_query = query_grad(order, own, qpad, head_lanes(dctx, heads, 64), lse, delta_rows, kv_all)
     kpad = head_lanes(kv[:, :part], heads, 0, part)
@@ -547,7 +643,8 @@
     g_gain_one = jnp.sum(dh1 * n1_own, axis=0)
     g_shift_one = jnp.sum(dh1, axis=0)
 
-    early = lax.psum_scatter(early, WIDE, scatter_dimension=0, tiled=True)
+    early = early + lax.ppermute(early_sent, "core", [(0, 1), (1, 0)]).astype(F32)
+    early = summed_at_owner(early, CHIPS)
     g_up_rows = early[:ff_held]
     o_w_down = early[ff_held : 2 * ff_held]
     out_rows = early[2 * ff_held : 2 * ff_held + held]
@@ -577,7 +674,11 @@
         axis=1,
     ).reshape(count * held, pair)
     late = jnp.concatenate([g_w_qkv, jnp.pad(small_grads, ((0, 0), (0, 64 - pair)))], axis=1)
-    late = summed_at_owner(late, WIDE)
+    late = late.reshape(wide // 2, 2, ways * held, late.shape[1])
+    late_sent = lax.dynamic_index_in_dim(late, 1 - core, axis=1, keepdims=False).astype(BF16)
+    late = lax.dynamic_index_in_dim(late, core, axis=1, keepdims=False)
+    late = late + lax.ppermute(late_sent, "core", [(0, 1), (1, 0)]).astype(F32)
+    late = summed_at_owner(late.reshape(-1, late.shape[2]), CHIPS)
     last = jnp.concatenate([late, g_up_rows], axis=1).reshape(ways, held, -1)
     last = lax.all_to_all(last, "ulysses", split_axis=0, concat_axis=0, tiled=True)
     o_w_qkv = last[:, :, : 3 * part].reshape(ways, held, 3, part).transpose(1, 2, 0, 3)
@@ -600,12 +701,16 @@
 
 
 def solution(mesh):
+    chips_z = mesh.shape["blk"] // 4
+    parts = Mesh(
+        mesh.devices.reshape(mesh.shape["batch"], 2, chips_z, 2, mesh.shape["ulysses"]), ALL
+    )
     rows = P(ALL, None)
     flat = P(None, ALL)
     deep = P(None, ALL, None)
     return jax.shard_map(
         on_device,
-        mesh=mesh,
+        mesh=parts,
         in_specs=(
             rows, P("batch", None), flat, flat, deep, flat, deep, flat, deep, flat, deep, flat, rows,
         ),

time: 453 us -> 478 us (1.055)
  the two profiles are of different devices: /device:TPU:96 before, /device:TPU:0 now
where the time goes in v1:
time: 478 us; the launch traced here: 469 us
  waiting for transfers between devices  163 us (34%)
  Pallas kernels  119 us (25%)
  starting transfers between devices  62.6 us (13%)
  local copies, waits for them, and re-layouts  52.9 us (11%)
  blocking collectives  26.3 us (6%)
  other arithmetic  22.9 us (5%)
  between operations  15.2 us (3%)
  matrix products  6.1 us (1%)
    all_gather x1, waiting for transfers between devices, on_device(): ffn_all = lax.all_gather(ffn, WIDE, axis=0, tiled=True)  48.1 us
    all_to_all x5, waiting for transfers between devices, summed_at_owner(): got = lax.all_to_all(sent, axis, split_axis=0, concat_axis=0, tiled=True)  40.6 us
    all_to_all x5, starting transfers between devices, summed_at_owner(): got = lax.all_to_all(sent, axis, split_axis=0, concat_axis=0, tiled=True)  37.2 us
    all_gather x1, waiting for transfers between devices, on_device(): kv_all = lax.all_gather(kv, BLK, axis=0, tiled=True)  36.2 us
    pallas_call x1, Pallas kernels, attend(): pl.pallas_call(functools.partial(attend_kernel, half=rows // 2, heads=hea...  35.9 us
    pallas_call x1, Pallas kernels, query_grad(): pl.pallas_call(functools.partial(query_grad_kernel, half=rows // 2, heads...  35.8 us
    pallas_call x1, Pallas kernels, key_grad(): pl.pallas_call(functools.partial(key_grad_kernel, half=rows // 2, heads=h...  30.5 us
    all_gather x1, blocking collectives, on_device(): filled = lax.all_gather(piece, WIDE, axis=0, tiled=True)  26.3 us
  transfers between devices with their start and end apart: 17, of which 11 were waited for; matrix products, arithmetic and copies ran while one was open for 11% of the time, Pallas kernels for 25%

profile of v1, /device:TPU:0, one launch (start us, length us, event | category | flops | bytes accessed | tf_op | source)
XLA Modules:
  0.0 468.6 jit_solution(7181969276678198987)
XLA Ops:
  7.7 1.3 reduce.11
  11.8 1.1 reshape_squeeze.12
  14.2 4.2 concatenate.55
  18.4 4.5 all-to-all-start
  22.9 13.9 %all-to-all-done = bf16[4,152,768]{2,1,0:T(8,128)(2,1)S(1)} async-done(((bf16[4,152,768]{2,1,0:T(8,128)(2,1)}), bf16[4,152,768]{2,1,0:T(8,128)(2,1)S(1)}, u32[]{:S(2)}, u32[]{:S(2)}) %all-to-all-start) | async-done | bytes 933920 | tf_op jit(solution)/shard_map/all_to_all | solution.py:553
  36.8 26.3 %all_gather.15 = bf16[768,640]{1,0:T(8,128)(2,1)S(1)} all-gather(bf16[24,640]{1,0:T(8,128)(2,1)S(1)} %reshape.382), channel_id=1, replica_groups=mesh['batch'=2,'xlo'=2,'z'=4,'core'=2,'ulysses'=4] {'batch','xlo','z','c..., dimensions={0}, use_global_device_ids=true | all-gather | bytes 1013760 | tf_op jit(solution)/shard_map/all_gather | solution.py:557
  65.1 1.1 fusion.40
  69.9 1.0 copy-done.17
  75.0 1.4 pad_maximum_fusion.2
  76.5 36.2 %all-gather.5.cloned.1.call-done.kv = bf16[8192,384]{1,0:T(8,128)(2,1)} async-done(((bf16[512,384]{1,0:T(8,128)(2,1)}), bf16[8192,384]{1,0:T(8,128)(2,1)}) %all-gather.5.cloned.1.call-update) | async-done | bytes 6291472 | tf_op jit(solution)/shard_map/all_gather | solution.py:584
  113.5 48.1 %all-gather.7.cloned.1.call-done.w_up.w_out.w_down = bf16[768,2304]{1,0:T(8,128)(2,1)} async-done(((bf16[24,2304]{1,0:T(8,128)(2,1)}), bf16[768,2304]{1,0:T(8,128)(2,1)}) %all-gather.7.cloned.1.call-update) | async-done | bytes 3538960 | tf_op jit(solution)/shard_map/all_gather | solution.py:592
  163.0 4.6 all-to-all-start.1
  168.4 1.5 select_select_fusion
  170.0 10.3 %all-to-all-done.1 = bf16[4,128,768]{2,1,0:T(8,128)(2,1)S(1)} async-done(((bf16[4,128,768]{2,1,0:T(8,128)(2,1)}), bf16[4,128,768]{2,1,0:T(8,128)(2,1)S(1)}, u32[]{:S(2)}, u32[]{:S(2)}) %all-to-all-start.1) | async-done | bytes 786464 | tf_op jit(solution)/shard_map/all_to_all | solution.py:480
  180.3 35.9 %attend.1 = (bf16[512,192]{1,0:T(8,128)(2,1)}, f32[512,192]{1,0:T(8,128)}, f32[8,512]{1,0:T(8,128)}) custom-call(s32[32]{0:T(128)} %bitcast.133, s32[2]{0:T(128)} %fusion.29.own, bf16[3,512,256]{2,1,0:T(8,128)(2,1)} %get-tuple-element.36.qpad, bf16[8192,384]{1,0:T(8,128)(2,1)} %all-gather.5.cloned.1.call-done.kv), custom_call_target="tpu_custom_call" | custom-call | flops 12884901888 | bytes 6291456 | tf_op jit(solution)/shard_map/attend/pallas_call | solution.py:231
  216.2 1.1 copy.223
  218.2 3.6 all-to-all-start.2
  222.1 2.1 copy.224
  225.0 1.1 copy.225
  228.0 1.8 copy.226
  231.9 1.3 copy.228.ctx
  233.1 11.1 %feed_forward.1 = (f32[128,768]{1,0:T(8,128)}, bf16[512,768]{1,0:T(8,128)(2,1)}, bf16[512,768]{1,0:T(8,128)(2,1)}, bf16[512,768]{1,0:T(8,128)(2,1)}, bf16[512,768]{1,0:T(8,128)(2,1)}, /*index=5*/bf16[512,768]{1,0:T(8,128)(2,1)}) custom-call(s32[1]{0:T(128)} %bitcast.me, bf16[512,768]{1,0:T(8,128)(2,1)} %bitcast.107, bf16[4,512,192]{2,1,0:T(8,128)(2,1)} %copy.228.ctx, ...), custom_call_target="tpu_custom_call" | custom-call | flops 3019898880 | bytes 3538944 | tf_op jit(solution)/shard_map/feed_forward/pallas_call | solution.py:351
  244.2 4.9 %all-to-all-start.3 = ((bf16[4,128,768]{2,1,0:T(8,128)(2,1)}), bf16[4,128,768]{2,1,0:T(8,128)(2,1)S(1)}, u32[]{:S(2)}, u32[]{:S(2)}) async-start(bf16[4,128,768]{2,1,0:T(8,128)(2,1)} %bitcast.118), calls=%async_computation.3 | async-start | bytes 1572864 | tf_op jit(solution)/shard_map/all_to_all | solution.py:486
  250.4 8.2 %all-to-all-done.3 = bf16[4,128,768]{2,1,0:T(8,128)(2,1)S(1)} async-done(((bf16[4,128,768]{2,1,0:T(8,128)(2,1)}), bf16[4,128,768]{2,1,0:T(8,128)(2,1)S(1)}, u32[]{:S(2)}, u32[]{:S(2)}) %all-to-all-start.3) | async-done | bytes 786464 | tf_op jit(solution)/shard_map/all_to_all | solution.py:486
  258.6 3.5 all-to-all-start.4
  263.2 8.4 %all-to-all-done.4 = bf16[4,128,768]{2,1,0:T(8,128)(2,1)S(1)} async-done(((bf16[4,128,768]{2,1,0:T(8,128)(2,1)}), bf16[4,128,768]{2,1,0:T(8,128)(2,1)S(1)}, u32[]{:S(2)}, u32[]{:S(2)}) %all-to-all-start.4) | async-done | bytes 786464 | tf_op jit(solution)/shard_map/all_to_all | solution.py:486
  274.1 3.5 all-to-all-start.5
  278.1 8.9 %all-to-all-done.5 = bf16[4,128,768]{2,1,0:T(8,128)(2,1)S(1)} async-done(((bf16[4,128,768]{2,1,0:T(8,128)(2,1)}), bf16[4,128,768]{2,1,0:T(8,128)(2,1)S(1)}, u32[]{:S(2)}, u32[]{:S(2)}) %all-to-all-start.5) | async-done | bytes 786464 | tf_op jit(solution)/shard_map/all_to_all | solution.py:480
  287.0 1.8 convert_multiply_fusion
  295.4 6.1 %weight_grads.1 = (f32[16,56,768]{2,1,0:T(8,128)}, bf16[16,56,768]{2,1,0:T(8,128)(2,1)}) custom-call(s32[1]{0:T(128)} %bitcast.32.core, bf16[512,768]{1,0:T(8,128)(2,1)} %get-tuple-element.54.h2, bf16[512,768]{1,0:T(8,128)(2,1)} %get-tuple-element.53.du, bf16[512,768]{1,0:T(8,128)(2,1)} %get-tuple-element.55.act, bf16[512,768]{1,0:T(8,128)(2,1)} %bitcast.111, ...), custom_call_target="tpu_custom_call" | custom-call | flops 1207959552 | bytes 4128768 | tf_op jit(solution)/shard_map/weight_grads/pallas_call | solution.py:412
  302.4 35.8 %query_grad.1 = bf16[512,192]{1,0:T(8,128)(2,1)} custom-call(s32[32]{0:T(128)} %bitcast.134, s32[2]{0:T(128)} %fusion.29.own, bf16[3,512,256]{2,1,0:T(8,128)(2,1)} %get-tuple-element.36.qpad, bf16[3,512,256]{2,1,0:T(8,128)(2,1)} %broadcast_select_fusion.dpad, f32[8,512]{1,0:T(8,128)} %get-tuple-element.47.lse, f32[8,512]{1,0:T(8,128)} %pad.25.delta, ...), custom_call_target="tpu_custom_call" | custom-call | flops 19327352832 | bytes 6291456 | tf_op jit(solution)/shard_map/query_grad/pallas_call | solution.py:260
  338.3 30.5 %key_grad.1 = (bf16[512,192]{1,0:T(8,128)(2,1)}, bf16[512,192]{1,0:T(8,128)(2,1)}) custom-call(s32[32]{0:T(128)} %bitcast.135, s32[2]{0:T(128)} %fusion.29.own, bf16[3,512,256]{2,1,0:T(8,128)(2,1)} %get-tuple-element.173.kpad, bf16[3,512,256]{2,1,0:T(8,128)(2,1)} %get-tuple-element.172.vpad, bf16[8192,256]{1,0:T(8,128)(2,1)} %all-gather.9.cloned.1.call-done.q_all, ...), custom_call_target="tpu_custom_call" | custom-call | flops 25769803776 | bytes 6291456 | tf_op jit(solution)/shard_map/key_grad/pallas_call | solution.py:286
  368.7 2.7 convolution_convert_fusion
  371.5 3.5 all-to-all-start.6
  375.0 3.2 fusion
  379.4 6.5 %all-to-all-done.6 = bf16[4,128,768]{2,1,0:T(8,128)(2,1)S(1)} async-done(((bf16[4,128,768]{2,1,0:T(8,128)(2,1)}), bf16[4,128,768]{2,1,0:T(8,128)(2,1)S(1)}, u32[]{:S(2)}, u32[]{:S(2)}) %all-to-all-start.6) | async-done | bytes 786464 | tf_op jit(solution)/shard_map/all_to_all | solution.py:486
  386.8 14.9 %all-to-all-start.8 = ((bf16[16,56,768]{2,1,0:T(8,128)(2,1)}), bf16[16,56,768]{2,1,0:T(8,128)(2,1)}, u32[]{:S(2)}, u32[]{:S(2)}) async-start(bf16[16,56,768]{2,1,0:T(8,128)(2,1)} %bitcast.35), calls=%async_computation.8 | async-start | bytes 2752512 | tf_op jit(solution)/shard_map/all_to_all | solution.py:486
  404.6 1.4 select_maximum_fusion
  406.0 1.9 copy.243
  408.7 4.9 %collective-permute-start = (bf16[16,24,640]{2,1,0:T(8,128)(2,1)}, bf16[16,24,640]{2,1,0:T(8,128)(2,1)}, u32[]{:S(2)}, u32[]{:S(2)}) collective-permute-start(bf16[16,24,640]{2,1,0:T(8,128)(2,1)} %fusion.7), channel_id=1, source_target_pairs={{0,4},{4,0},{1,5},{5,1},{2,6},{6,2},{3,7},{7,3},{8,12},{12,8},{9,1... | collective-permute-start | bytes 1474568 | tf_op jit(solution)/shard_map/ppermute | solution.py:680
  413.6 6.7 %all-to-all-done.8 = bf16[16,56,768]{2,1,0:T(8,128)(2,1)} async-done(((bf16[16,56,768]{2,1,0:T(8,128)(2,1)}), bf16[16,56,768]{2,1,0:T(8,128)(2,1)}, u32[]{:S(2)}, u32[]{:S(2)}) %all-to-all-start.8) | async-done | bytes 1376288 | tf_op jit(solution)/shard_map/all_to_all | solution.py:486
  420.3 1.5 convert_reduce_fusion
  422.5 1.9 fusion.4
  424.4 10.4 %all-to-all-start.7 = ((bf16[16,24,640]{2,1,0:T(8,128)(2,1)}), bf16[16,24,640]{2,1,0:T(8,128)(2,1)S(1)}, u32[]{:S(2)}, u32[]{:S(2)}) async-start(bf16[16,24,640]{2,1,0:T(8,128)(2,1)} %fusion.4), calls=%async_computation.7 | async-start | bytes 983040 | tf_op jit(solution)/shard_map/all_to_all | solution.py:486
  436.1 10.8 %all-to-all-done.7 = bf16[16,24,640]{2,1,0:T(8,128)(2,1)S(1)} async-done(((bf16[16,24,640]{2,1,0:T(8,128)(2,1)}), bf16[16,24,640]{2,1,0:T(8,128)(2,1)S(1)}, u32[]{:S(2)}, u32[]{:S(2)}) %all-to-all-start.7) | async-done | bytes 491552 | tf_op jit(solution)/shard_map/all_to_all | solution.py:486
  447.6 3.4 all-to-all-start.9
  451.9 5.3 %all-to-all-done.9 = f32[4,6,1408]{2,1,0:T(8,128)S(1)} async-done(((f32[4,6,1408]{2,1,0:T(8,128)}), f32[4,6,1408]{2,1,0:T(8,128)S(1)}, u32[]{:S(2)}, u32[]{:S(2)}) %all-to-all-start.9) | async-done | bytes 135200 | tf_op jit(solution)/shard_map/all_to_all | solution.py:683
  459.9 1.1 reshape.414
  (252 shorter events, 48.1 us)
Async XLA Ops:
  7.2 7.0 %copy-start.35 = (bf16[1,6,768]{2,1,0:T(8,128)(2,1)S(1)}, bf16[1,6,768]{2,1,0:T(8,128)(2,1)}, u32[]{:S(2)}) copy-start(bf16[1,6,768]{2,1,0:T(8,128)(2,1)} %param.19) | copy-start | bytes 27652
  18.4 18.4 %all-to-all-start = ((bf16[4,152,768]{2,1,0:T(8,128)(2,1)}), bf16[4,152,768]{2,1,0:T(8,128)(2,1)S(1)}, u32[]{:S(2)}, u32[]{:S(2)}) async-start(bf16[4,152,768]{2,1,0:T(8,128)(2,1)} %concatenate.55), calls=%async_computation | async-start | bytes 1867776 | tf_op jit(solution)/shard_map/all_to_all | solution.py:553
  22.9 89.7 %all-gather.5.cloned.1.call-start = ((), (), s32[]{:S(2)}) async-start(), calls=%async_computation.10 | async-start | bytes 6684672 | tf_op jit(solution)/shard_map/all_gather | solution.py:584
  67.7 1.8 copy-start.33
  69.4 1.5 copy-start.17
  69.5 2.2 copy-start
  71.7 90.0 %copy-start.12 = (f32[128,768]{1,0:T(8,128)S(1)}, f32[128,768]{1,0:T(8,128)}, u32[]{:S(2)}) copy-start(f32[128,768]{1,0:T(8,128)} %param.25) | copy-start | bytes 1179652
  72.7 89.0 %all-gather.7.cloned.1.call-start = ((), (), s32[]{:S(2)}) async-start(), calls=%async_computation.11 | async-start | bytes 3649536 | tf_op jit(solution)/shard_map/all_gather | solution.py:592
  112.7 160.4 %all-gather.9.cloned.1.call-start = ((), (), s32[]{:S(2)}) async-start(), calls=%async_computation.12 | async-start | bytes 4456448 | tf_op jit(solution)/shard_map/all_gather | solution.py:595
  161.7 5.9 %copy-start.39 = (s32[1,32]{1,0:T(1,128)S(1)}, s32[1,32]{1,0:T(1,128)}, u32[]{:S(2)}) copy-start(s32[1,32]{1,0:T(1,128)} %param.14) | copy-start | bytes 388
  161.7 6.5 %copy-start.3 = (bf16[512,384]{1,0:T(8,128)(2,1)S(1)}, bf16[512,384]{1,0:T(8,128)(2,1)}, u32[]{:S(2)}) copy-start(bf16[512,384]{1,0:T(8,128)(2,1)} %slice.152) | copy-start | bytes 1179652
  162.0 6.3 %copy-start.38 = (pred[256]{0:T(512)(128)(4,1)S(1)}, pred[256]{0:T(512)(128)(4,1)}, u32[]{:S(2)}) copy-start(pred[256]{0:T(512)(128)(4,1)} %constant.92.clone.1) | copy-start | bytes 772
  163.0 5.4 %copy-start.8 = (bf16[512,256]{1,0:T(8,128)(2,1)S(1)}, bf16[512,256]{1,0:T(8,128)(2,1)}, u32[]{:S(2)}) copy-start(bf16[512,256]{1,0:T(8,128)(2,1)} %pad.23) | copy-start | bytes 786436
  163.0 17.3 %all-to-all-start.1 = ((bf16[4,128,768]{2,1,0:T(8,128)(2,1)}), bf16[4,128,768]{2,1,0:T(8,128)(2,1)S(1)}, u32[]{:S(2)}, u32[]{:S(2)}) async-start(bf16[4,128,768]{2,1,0:T(8,128)(2,1)} %broadcast_in_dim.168), calls=%async_computation.1 | async-start | bytes 1572864 | tf_op jit(solution)/shard_map/all_to_all | solution.py:480
  180.3 35.9 %copy-start.4 = (bf16[4,128,768]{2,1,0:T(8,128)(2,1)}, bf16[4,128,768]{2,1,0:T(8,128)(2,1)S(1)}, u32[]{:S(2)}) copy-start(bf16[4,128,768]{2,1,0:T(8,128)(2,1)S(1)} %all-to-all-done.1) | copy-start | bytes 2359300
  218.2 6.9 %copy-start.11 = (f32[64,1,12]{1,0,2:T(8,128)S(1)}, f32[64,1,12]{1,0,2:T(8,128)}, u32[]{:S(2)}) copy-start(f32[64,1,12]{1,0,2:T(8,128)} %get-tuple-element.146) | copy-start | bytes 9220
  218.2 13.7 %all-to-all-start.2 = ((bf16[4,512,192]{1,2,0:T(8,128)(2,1)}), bf16[4,512,192]{1,2,0:T(8,128)(2,1)S(1)}, u32[]{:S(2)}, u32[]{:S(2)}) async-start(bf16[4,512,192]{1,2,0:T(8,128)(2,1)} %broadcast_in_dim.169), calls=%async_computation.2 | async-start | bytes 1572864 | tf_op jit(solution)/shard_map/all_to_all | solution.py:480
  244.2 4.9 %copy-start.28 = (f32[64,1,12]{2,0,1:T(8,128)S(1)}, f32[64,1,12]{2,0,1:T(8,128)}, u32[]{:S(2)}) copy-start(f32[64,1,12]{2,0,1:T(8,128)} %copy.224) | copy-start | bytes 9220
  244.2 6.0 %copy-start.1 = (f32[128,768]{1,0:T(8,128)S(1)}, f32[128,768]{1,0:T(8,128)}, u32[]{:S(2)}) copy-start(f32[128,768]{1,0:T(8,128)} %get-tuple-element.43) | copy-start | bytes 1179652
  244.2 14.4 %all-to-all-start.3 = ((bf16[4,128,768]{2,1,0:T(8,128)(2,1)}), bf16[4,128,768]{2,1,0:T(8,128)(2,1)S(1)}, u32[]{:S(2)}, u32[]{:S(2)}) async-start(bf16[4,128,768]{2,1,0:T(8,128)(2,1)} %bitcast.118), calls=%async_computation.3 | async-start | bytes 1572864 | tf_op jit(solution)/shard_map/all_to_all | solution.py:486
  258.6 13.0 %all-to-all-start.4 = ((bf16[4,128,768]{2,1,0:T(8,128)(2,1)}), bf16[4,128,768]{2,1,0:T(8,128)(2,1)S(1)}, u32[]{:S(2)}, u32[]{:S(2)}) async-start(bf16[4,128,768]{2,1,0:T(8,128)(2,1)} %bitcast.116), calls=%async_computation.4 | async-start | bytes 1572864 | tf_op jit(solution)/shard_map/all_to_all | solution.py:486
  262.3 9.8 %copy-start.13 = (f32[128,768]{1,0:T(8,128)S(1)}, f32[128,768]{1,0:T(8,128)}, u32[]{:S(2)}) copy-start(f32[128,768]{1,0:T(8,128)} %param.25) | copy-start | bytes 1179652
  263.2 8.9 %copy-start.15 = (f32[128,768]{1,0:T(8,128)S(1)}, f32[128,768]{1,0:T(8,128)}, u32[]{:S(2)}) copy-start(f32[128,768]{1,0:T(8,128)} %convert_reduce_fusion.7) | copy-start | bytes 1179652
  273.1 4.8 %copy-start.36 = (f32[8,512]{1,0:T(8,128)S(1)}, f32[8,512]{1,0:T(8,128)}, u32[]{:S(2)}) copy-start(f32[8,512]{1,0:T(8,128)} %get-tuple-element.47.lse) | copy-start | bytes 49156
  274.1 13.0 %all-to-all-start.5 = ((bf16[4,128,768]{2,1,0:T(8,128)(2,1)}), bf16[4,128,768]{2,1,0:T(8,128)(2,1)S(1)}, u32[]{:S(2)}, u32[]{:S(2)}) async-start(bf16[4,128,768]{2,1,0:T(8,128)(2,1)} %broadcast_in_dim.171), calls=%async_computation.5 | async-start | bytes 1572864 | tf_op jit(solution)/shard_map/all_to_all | solution.py:480
  277.6 60.7 %all-gather.11.cloned.1.call-start = ((), (), s32[]{:S(2)}) async-start(), calls=%async_computation.13 | async-start | bytes 4456448 | tf_op jit(solution)/shard_map/all_gather | solution.py:632
  287.0 2.0 copy-start.7
  288.8 1.5 copy-start.2
  288.8 2.3 copy-start.10
  289.0 2.3 copy-start.26
  301.5 73.5 %collective-permute-start.1 = (bf16[896,768]{1,0:T(8,128)(2,1)}, bf16[896,768]{1,0:T(8,128)(2,1)S(1)}, u32[]{:S(2)}, u32[]{:S(2)}) collective-permute-start(bf16[896,768]{1,0:T(8,128)(2,1)} %bitcast.132), channel_id=1, source_target_pairs={{0,4},{4,0},{1,5},{5,1},{2,6},{6,2},{3,7},{7,3},{8,12},{12,8},{9,1... | collective-permute-start | bytes 4128776 | tf_op jit(solution)/shard_map/ppermute | solution.py:646
  338.3 30.5 %copy-start.18 = (bf16[768,640]{1,0:T(8,128)(2,1)S(1)}, bf16[768,640]{1,0:T(8,128)(2,1)}, u32[]{:S(2)}) copy-start(bf16[768,640]{1,0:T(8,128)(2,1)} %copy-done.16) | copy-start | bytes 2949124
  338.3 30.5 %copy-start.19 = (bf16[512,192]{1,0:T(8,128)(2,1)S(1)}, bf16[512,192]{1,0:T(8,128)(2,1)}, u32[]{:S(2)}) copy-start(bf16[512,192]{1,0:T(8,128)(2,1)} %query_grad.1) | copy-start | bytes 589828
  371.5 14.4 %all-to-all-start.6 = ((bf16[4,128,768]{2,1,0:T(8,128)(2,1)}), bf16[4,128,768]{2,1,0:T(8,128)(2,1)S(1)}, u32[]{:S(2)}, u32[]{:S(2)}) async-start(bf16[4,128,768]{2,1,0:T(8,128)(2,1)} %bitcast.117), calls=%async_computation.6 | async-start | bytes 1572864 | tf_op jit(solution)/shard_map/all_to_all | solution.py:486
  375.0 3.3 copy-start.20
  375.0 3.2 copy-start.22
  375.0 3.2 copy-start.24
  378.5 23.2 %copy-start.21 = (bf16[512,192]{1,0:T(8,128)(2,1)S(1)}, bf16[512,192]{1,0:T(8,128)(2,1)}, u32[]{:S(2)}) copy-start(bf16[512,192]{1,0:T(8,128)(2,1)} %query_grad.1) | copy-start | bytes 589828
  378.5 23.2 %copy-start.23 = (bf16[512,192]{1,0:T(8,128)(2,1)S(1)}, bf16[512,192]{1,0:T(8,128)(2,1)}, u32[]{:S(2)}) copy-start(bf16[512,192]{1,0:T(8,128)(2,1)} %get-tuple-element.51) | copy-start | bytes 589828
  378.5 23.2 %copy-start.25 = (bf16[512,192]{1,0:T(8,128)(2,1)S(1)}, bf16[512,192]{1,0:T(8,128)(2,1)}, u32[]{:S(2)}) copy-start(bf16[512,192]{1,0:T(8,128)(2,1)} %get-tuple-element.52) | copy-start | bytes 589828
  386.8 33.5 %all-to-all-start.8 = ((bf16[16,56,768]{2,1,0:T(8,128)(2,1)}), bf16[16,56,768]{2,1,0:T(8,128)(2,1)}, u32[]{:S(2)}, u32[]{:S(2)}) async-start(bf16[16,56,768]{2,1,0:T(8,128)(2,1)} %bitcast.35), calls=%async_computation.8 | async-start | bytes 2752512 | tf_op jit(solution)/shard_map/all_to_all | solution.py:486
  401.7 1.5 copy-start.34
  401.7 1.5 copy-start.37
  408.7 13.8 %collective-permute-start = (bf16[16,24,640]{2,1,0:T(8,128)(2,1)}, bf16[16,24,640]{2,1,0:T(8,128)(2,1)}, u32[]{:S(2)}, u32[]{:S(2)}) collective-permute-start(bf16[16,24,640]{2,1,0:T(8,128)(2,1)} %fusion.7), channel_id=1, source_target_pairs={{0,4},{4,0},{1,5},{5,1},{2,6},{6,2},{3,7},{7,3},{8,12},{12,8},{9,1... | collective-permute-start | bytes 1474568 | tf_op jit(solution)/shard_map/ppermute | solution.py:680
  421.8 13.6 %collective-permute-start.2 = (f32[6,768]{1,0:T(8,128)S(1)}, f32[6,768]{1,0:T(8,128)S(1)}, u32[]{:S(2)}, u32[]{:S(2)}) collective-permute-start(f32[6,768]{1,0:T(8,128)S(1)} %slice.163), channel_id=1, source_target_pairs={{0,0},{1,32},{2,64},{3,96},{4,1},{5,33},{6,65},{7,97},{8,2},{9,34}... | collective-permute-start | bytes 55304 | tf_op jit(solution)/shard_map/ppermute | solution.py:652
  424.4 26.6 %copy-start.14 = (f32[128,768]{1,0:T(8,128)S(1)}, f32[128,768]{1,0:T(8,128)}, u32[]{:S(2)}) copy-start(f32[128,768]{1,0:T(8,128)} %get-tuple-element.141) | copy-start | bytes 1179652
  424.4 22.4 %all-to-all-start.7 = ((bf16[16,24,640]{2,1,0:T(8,128)(2,1)}), bf16[16,24,640]{2,1,0:T(8,128)(2,1)S(1)}, u32[]{:S(2)}, u32[]{:S(2)}) async-start(bf16[16,24,640]{2,1,0:T(8,128)(2,1)} %fusion.4), calls=%async_computation.7 | async-start | bytes 983040 | tf_op jit(solution)/shard_map/all_to_all | solution.py:486
  447.6 9.6 %all-to-all-start.9 = ((f32[4,6,1408]{2,1,0:T(8,128)}), f32[4,6,1408]{2,1,0:T(8,128)S(1)}, u32[]{:S(2)}, u32[]{:S(2)}) async-start(f32[4,6,1408]{2,1,0:T(8,128)} %reshape.404), calls=%async_computation.9 | async-start | bytes 360448 | tf_op jit(solution)/shard_map/all_to_all | solution.py:683
  (9 other events, 8.6 us)
Sparse Core Ops, SparseCore 0:
  72.8 39.8 all-gather.4
  115.0 46.6 all-gather.6
  163.4 36.7 all-gather.8
  290.4 46.5 all-gather.10

commit v2 on v1

v2 whole, which is shorter than its diff:
```python
import functools
import math

import jax
import jax.numpy as jnp
from jax import lax
from jax.experimental import pallas as pl
from jax.experimental.pallas import tpu as pltpu
from jax.sharding import Mesh, PartitionSpec as P

HEADS = 12
HEAD_DIM = 64
NORM_EPS = 1e-05
FLOOR = -1e25
HIGHEST_ABOVE = 60.0
LANES = 256
EXTRA = 64
BELOW_FLOOR = -1e30
BLK = ("xlo", "z", "core")
CHIPS = ("batch", "xlo", "z")
WIDE = ("batch", "xlo", "z", "core")
ALL = ("batch", "xlo", "z", "core", "ulysses")
BF16 = jnp.bfloat16
F32 = jnp.float32
NT = (((1,), (1,)), ((), ()))
VMEM_LIMIT = 60 * 1024 * 1024


def mm(a, b):
    return jnp.dot(a, b, preferred_element_type=F32)


def mm_nt(a, b):
    return lax.dot_general(a, b, NT, preferred_element_type=F32)


def mm_tn(a, b):
    return lax.dot_general(a, b, (((0,), (0,)), ((), ())), preferred_element_type=F32)


def stretch(index, half):
    return pl.ds(pl.multiple_of(index * half, half), half)


def lanes_of(rows):
    return lax.broadcasted_iota(jnp.int32, (rows, LANES), 1)


def ones_after(k, first):
    return jnp.where(lanes_of(k.shape[0]) < first, k, jnp.ones_like(k))


def ones_before(v):
    return jnp.where(lanes_of(v.shape[0]) < EXTRA, jnp.ones_like(v), v)


def three(x):
    high = x.astype(BF16).astype(F32)
    mid = (x - high).astype(BF16).astype(F32)
    return high, mid, x - high - mid


def causal(half, heads, keys_first):
    rows = lax.broadcasted_iota(jnp.int32, (heads * half, half), 0) & (half - 1)
    cols = lax.broadcasted_iota(jnp.int32, (heads * half, half), 1)
    return rows <= cols if keys_first else cols <= rows


def merged_heads(stacked, half, heads, first):
    lane = lanes_of(half)
    out = stacked[:half]
    for h in range(1, heads):
        out = jnp.where(lane < first + h * HEAD_DIM, out, stacked[h * half : (h + 1) * half])
    return out


def in_groups(first, count, tiles):
    def eight(i, _):
        tiles([first + 8 * i + j for j in range(8)])
        return 0

    lax.fori_loop(0, count // 8, eight, 0)
    for size in (4, 2, 1):

        @pl.when((count & size) != 0)
        def _():
            begin = first + (count & ~(2 * size - 1))
            tiles([begin + j for j in range(size)])


def one_ahead(items, produce, consume):
    ready = produce(items[0])
    for n, item in enumerate(items):
        now = ready
        if n + 1 < len(items):
            ready = produce(items[n + 1])
        consume(item, now)


def attend_kernel(
    slots, own, q_heads, kv, ctx_low, ctx, lse, shift, total, q_ext, top, *, half, heads
):
    deep = heads * half
    lane = lanes_of(deep)

    def one_half(part, _):
        rank_own = own[part]
        mask = causal(half, heads, False)
        here = stretch(slots[rank_own], half)
        scores = jnp.where(mask, mm_nt(q_heads[part], kv[here, :LANES]), BELOW_FLOOR)
        first = jnp.max(scores, axis=1, keepdims=True).astype(BF16).astype(F32)
        shift[...] = first
        q_ext[...] = jnp.where(lane == heads * HEAD_DIM, -first, q_heads[part].astype(F32)).astype(
            BF16
        )
        top[...] = jnp.zeros_like(top)
        total[...] = mm(jnp.exp(scores - first).astype(BF16), ones_before(kv[here, 128:]))

        def tiles(ranks):
            at = [stretch(slots[r], half) for r in ranks]
            added = [total[...], top[...]]

            def produce(a):
                return mm_nt(q_ext[...], ones_after(kv[a, :LANES], heads * HEAD_DIM))

            def consume(a, above):
                added[1] = jnp.maximum(added[1], jnp.max(above.reshape(deep // 8, 8, half), axis=0))
                added[0] += mm(jnp.exp(above).astype(BF16), ones_before(kv[a, 128:]))

            one_ahead(at, produce, consume)
            total[...] = added[0]
            top[...] = added[1]

        in_groups(0, rank_own, tiles)

        @pl.when(jnp.logical_not(jnp.max(top[...]) < HIGHEST_ABOVE))
        def _():
            shift[...] = jnp.full_like(shift, FLOOR)
            total[...] = jnp.zeros_like(total)

            def again(rank, _):
                a = stretch(slots[rank], half)
                allowed = jnp.logical_or(mask, rank < rank_own)
                scores = jnp.where(allowed, mm_nt(q_heads[part], kv[a, :LANES]), BELOW_FLOOR)
                new = jnp.maximum(shift[...], jnp.max(scores, axis=1, keepdims=True))
                total[...] = total[...] * jnp.exp(shift[...] - new) + mm(
                    jnp.exp(scores - new).astype(BF16), ones_before(kv[a, 128:])
                )
                shift[...] = new
                return 0

            lax.fori_loop(0, rank_own + 1, again, 0)

        row_sum = total[:, :1]
        lse[part] = shift[...] + jnp.log(row_sum)
        done = merged_heads(total[...] / row_sum, half, heads, EXTRA)
        rows = stretch(part, half)
        ctx[rows, :] = done
        ctx_low[rows, :] = done[:, EXTRA:].astype(BF16)
        return 0

    lax.fori_loop(0, 2, one_half, 0)


def query_grad_kernel(slots, own, q_ext, d_ext, kv, d_query, total, *, half, heads):
    def one_half(part, _):
        rank_own = own[part]
        total[...] = jnp.zeros_like(total)

        def tiles(ranks, mask=None):
            at = [stretch(slots[r], half) for r in ranks]
            added = [total[...]]

            def produce(a):
                return (
                    mm_nt(q_ext[part], ones_after(kv[a, :LANES], heads * HEAD_DIM)),
                    mm_nt(d_ext[part], ones_before(kv[a, 128:])),
                )

            def consume(a, ready):
                probs = jnp.exp(ready[0])
                if mask is not None:
                    probs = jnp.where(mask, probs, 0.0)
                added[0] += mm((probs * ready[1]).astype(BF16), kv[a, :LANES])

            one_ahead(at, produce, consume)
            total[...] = added[0]

        in_groups(0, rank_own, tiles)
        tiles([rank_own], causal(half, heads, False))
        done = merged_heads(total[...], half, heads, 0)[:, : heads * HEAD_DIM]
        d_query[stretch(part, half), :] = (done * (1.0 / math.sqrt(HEAD_DIM))).astype(BF16)
        return 0

    lax.fori_loop(0, 2, one_half, 0)


def key_grad_kernel(
    slots, own, k_heads, v_heads, q_all, p_all, d_key, d_value, k_sum, v_sum, *, half, heads
):
    count = slots.shape[0]
    lane = lanes_of(half)

    def one_half(part, _):
        rank_own = own[part]
        k_sum[...] = jnp.zeros_like(k_sum)
        v_sum[...] = jnp.zeros_like(v_sum)

        def tiles(ranks, mask=None):
            at = [stretch(slots[r], half) for r in ranks]
            added = [k_sum[...], v_sum[...]]

            def produce(a):
                return (
                    mm_nt(k_heads[part], jnp.where(lane < EXTRA, p_all[a, :], q_all[a, :])),
                    mm_nt(v_heads[part], p_all[a, :]),
                )

            def consume(a, ready):
                probs = jnp.exp(ready[0])
                if mask is not None:
                    probs = jnp.where(mask, probs, 0.0)
                added[1] += mm(probs.astype(BF16), p_all[a, :])
                added[0] += mm((probs * ready[1]).astype(BF16), q_all[a, :])

            one_ahead(at, produce, consume)
            k_sum[...], v_sum[...] = added

        tiles([rank_own], causal(half, heads, True))
        in_groups(rank_own + 1, count - 1 - rank_own, tiles)
        rows = stretch(part, half)
        d_key[rows, :] = merged_heads(k_sum[...], half, heads, EXTRA)[:, EXTRA:].astype(BF16)
        d_value[rows, :] = merged_heads(v_sum[...], half, heads, EXTRA)[:, EXTRA:].astype(BF16)
        return 0

    lax.fori_loop(0, 2, one_half, 0)


def prepare_kernel(dc, w_out, ctx, lse, q_heads, packed, q_ext, d_ext, *, half, heads):
    lane = lanes_of(half)
    d_ctx = mm_nt(dc[...], w_out[...]).astype(BF16)
    for part in range(2):
        rows = slice(part * half, (part + 1) * half)
        grads = d_ctx[rows, :]
        terms = grads.astype(F32) * ctx[rows, :]
        extra = grads.astype(F32)
        for h in range(heads):
            deep = slice(h * half, (h + 1) * half)
            first = EXTRA + h * HEAD_DIM
            here = jnp.logical_and(lane >= first, lane < first + HEAD_DIM)
            delta = jnp.sum(jnp.where(here, terms, 0.0), axis=1, keepdims=True)
            minus_lse = three(-lse[part, deep, :])
            minus_delta = three(-delta)
            q_new = q_heads[part, deep, :].astype(F32)
            d_new = jnp.where(here, grads.astype(F32), 0.0)
            for i in range(3):
                q_new = jnp.where(lane == heads * HEAD_DIM + i, minus_lse[i], q_new)
                d_new = jnp.where(lane == i, minus_delta[i], d_new)
                extra = jnp.where(lane == 3 * h + i, minus_lse[i], extra)
                extra = jnp.where(lane == 3 * (heads + h) + i, minus_delta[i], extra)
            q_ext[part, deep, :] = q_new.astype(BF16)
            d_ext[part, deep, :] = d_new.astype(BF16)
        packed[rows, :] = extra.astype(BF16)


def whole(shape):
    return pl.BlockSpec(shape, lambda i, *_: (0,) * len(shape))


def params():
    return pltpu.CompilerParams(
        dimension_semantics=("arbitrary",), vmem_limit_bytes=VMEM_LIMIT
    )


def cost(rows, keys, heads, products):
    area = rows * keys * heads
    return pl.CostEstimate(
        flops=2 * area * 256 * products, bytes_accessed=keys * 768, transcendentals=area
    )


def call(kernel, name, scalars, arrays, outs, scratch, estimate, **static):
    return pl.pallas_call(
        functools.partial(kernel, **static),
        out_shape=tuple(jax.ShapeDtypeStruct(s, t) for s, t in outs),
        grid_spec=pltpu.PrefetchScalarGridSpec(
            num_scalar_prefetch=len(scalars),
            grid=(1,),
            in_specs=[whole(a.shape) for a in arrays],
            out_specs=[whole(s) for s, _ in outs],
            scratch_shapes=[pltpu.VMEM(s, t) for s, t in scratch],
        ),
        compiler_params=params(),
        cost_estimate=estimate,
        name=name,
    )(*scalars, *arrays)


def attend(slots, own, q_heads, kv, heads):
    _, deep, _ = q_heads.shape
    half = deep // heads
    width = heads * HEAD_DIM
    return call(
        attend_kernel, "attend", (slots, own), (q_heads, kv),
        [((2 * half, width), BF16), ((2 * half, LANES), F32), ((2, deep, 1), F32)],
        [((deep, 1), F32), ((deep, LANES), F32), ((deep, LANES), BF16), ((8, half), F32)],
        cost(2 * half, kv.shape[0], heads, 2), half=half, heads=heads,
    )


def prepare(dc, w_out, ctx, lse, q_heads, heads):
    _, deep, _ = q_heads.shape
    half = deep // heads
    return call(
        prepare_kernel, "prepare", (), (dc, w_out, ctx, lse, q_heads),
        [((2 * half, LANES), BF16), (q_heads.shape, BF16), (q_heads.shape, BF16)], [],
        pl.CostEstimate(flops=2 * dc.size * LANES, bytes_accessed=4 * q_heads.size, transcendentals=0),
        half=half, heads=heads,
    )


def query_grad(slots, own, q_ext, d_ext, kv, heads):
    _, deep, _ = q_ext.shape
    half = deep // heads
    return call(
        query_grad_kernel, "query_grad", (slots, own), (q_ext, d_ext, kv),
        [((2 * half, heads * HEAD_DIM), BF16)], [((deep, LANES), F32)],
        cost(2 * half, kv.shape[0], heads, 3), half=half, heads=heads,
    )[0]


def key_grad(slots, own, k_heads, v_heads, q_all, p_all, heads):
    _, deep, _ = k_heads.shape
    half = deep // heads
    out = ((2 * half, heads * HEAD_DIM), BF16)
    return call(
        key_grad_kernel, "key_grad", (slots, own), (k_heads, v_heads, q_all, p_all),
        [out, out], [((deep, LANES), F32)] * 2,
        cost(2 * half, q_all.shape[0], heads, 4), half=half, heads=heads,
    )


def feed_forward_kernel(
    me, x, ctx, df, vectors, w_up, w_out, w_down, x2_own, h2, act, du, dh2, down
):
    part = ctx.shape[2]
    total = x[...].astype(F32) + vectors[2:3, :]
    for u in range(ctx.shape[0]):
        total += mm(ctx[u], w_out[u * part : (u + 1) * part, :])

    @pl.when(pl.program_id(0) == me[0])
    def _():
        x2_own[...] = total

    normed, _ = normalized(total)
    h2_low = (normed * vectors[0:1, :] + vectors[1:2, :]).astype(BF16)
    h2[...] = h2_low
    up = mm(h2_low, w_up[...]) + vectors[3:4, :]
    bend = math.sqrt(2.0 / math.pi)
    square = up * up
    turn = jnp.tanh(bend * (up + 0.044715 * square * up))
    half = 0.5 * (1.0 + turn)
    act_low = (up * half).astype(BF16)
    act[...] = act_low
    down[...] = mm(act_low, w_down[...]).astype(BF16)
    slope = half + 0.5 * up * (1.0 - turn * turn) * (bend * (1.0 + 3 * 0.044715 * square))
    du_low = (slope * mm_nt(df[...], w_down[...])).astype(BF16)
    du[...] = du_low
    dh2[...] = mm_nt(du_low, w_up[...]).astype(BF16)


def feed_forward(me, x, ctx, df, vectors, weights):
    rows, width = x.shape
    ways, _, part = ctx.shape
    step = rows // ways

    def along(cols):
        return pl.BlockSpec((step, cols), lambda i, *_: (i, 0))

    def third(c):
        return pl.BlockSpec((weights.shape[0], width), lambda i, *_: (0, c))

    flat = jax.ShapeDtypeStruct((rows, width), BF16)
    return pl.pallas_call(
        feed_forward_kernel,
        out_shape=(jax.ShapeDtypeStruct((step, width), F32), flat, flat, flat, flat, flat),
        grid_spec=pltpu.PrefetchScalarGridSpec(
            num_scalar_prefetch=1,
            grid=(ways,),
            in_specs=[
                along(width),
                pl.BlockSpec((ways, step, part), lambda i, *_: (0, i, 0)),
                along(width),
                whole(vectors.shape),
                third(0),
                third(1),
                third(2),
            ],
            out_specs=[whole((step, width))] + [along(width)] * 5,
        ),
        compiler_params=params(),
        cost_estimate=pl.CostEstimate(
            flops=10 * rows * width * width, bytes_accessed=6 * width * width, transcendentals=rows * width
        ),
        name="feed_forward",
    )(me, x, ctx, df, vectors, weights, weights, weights)


def weight_grads_kernel(core, h2, du, act, df, ctx, dc, kept, sent, g_up, g_down, g_out, *, deep):
    chips, rows, width = kept.shape
    owners = 2 * chips
    each = h2.shape[1] // owners
    few = ctx.shape[1] // owners
    chunk = h2.shape[1] // 2
    for i in range(2):
        cols = slice(i * chunk, (i + 1) * chunk)
        g_up[cols, :] = mm_tn(h2[:, cols], du[...])
        g_down[cols, :] = mm_tn(act[:, cols], df[...])
    g_out[...] = mm_tn(ctx[...], dc[...])

    def put(target, which):
        target[:, 2 * each :, :] = jnp.zeros((chips, rows - 2 * each, width), target.dtype)
        for g in range(chips):
            w = 2 * (g % (chips // deep) * deep + g // (chips // deep)) + which
            target[g, :each, :] = g_up[w * each : (w + 1) * each, :].astype(target.dtype)
            target[g, each : 2 * each, :] = g_down[w * each : (w + 1) * each, :].astype(target.dtype)
            target[g, 2 * each : 2 * each + few, :] = g_out[w * few : (w + 1) * few, :].astype(
                target.dtype
            )

    for which in range(2):

        @pl.when(core[0] == which)
        def _():
            put(kept, which)
            put(sent, 1 - which)


def weight_grads(core, h2, du, act, df, ctx, dc, owners, deep):
    width = du.shape[1]
    units = h2.shape[1]
    rows = 2 * units // owners + 8
    chips = owners // 2
    arrays = (h2, du, act, df, ctx, dc)
    kept, sent = pl.pallas_call(
        functools.partial(weight_grads_kernel, deep=deep),
        out_shape=(
            jax.ShapeDtypeStruct((chips, rows, width), F32),
            jax.ShapeDtypeStruct((chips, rows, width), BF16),
        ),
        grid_spec=pltpu.PrefetchScalarGridSpec(
            num_scalar_prefetch=1,
            grid=(1,),
            in_specs=[whole(a.shape) for a in arrays],
            out_specs=[whole((chips, rows, width))] * 2,
            scratch_shapes=[
                pltpu.VMEM((units, width), F32),
                pltpu.VMEM((units, width), F32),
                pltpu.VMEM((ctx.shape[1], width), F32),
            ],
        ),
        compiler_params=params(),
        cost_estimate=pl.CostEstimate(
            flops=4 * h2.size * width, bytes_accessed=6 * chips * rows * width, transcendentals=0
        ),
        name="weight_grads",
    )(core, *arrays)
    return kept, sent


def normalized(values):
    mean = jnp.mean(values, axis=-1, keepdims=True)
    centered = values - mean
    spread = jnp.mean(centered * centered, axis=-1, keepdims=True)
    scale = lax.rsqrt(spread + NORM_EPS)
    return centered * scale, scale


def norm_back(grad, gain, normed, scale):
    e = grad * gain
    mean_e = jnp.mean(e, axis=-1, keepdims=True)
    mean_en = jnp.mean(e * normed, axis=-1, keepdims=True)
    return scale * (e - mean_e - normed * mean_en)


def gelu_tanh(values):
    return jax.nn.gelu(values, approximate=True)


def head_lanes(x, heads, first, ones_at=None):
    rows, width = x.shape
    wide = jnp.pad(x, ((0, 0), (first, LANES - width - first))).reshape(2, 1, rows // 2, LANES)
    lane = lax.broadcasted_iota(jnp.int32, (1, heads, 1, LANES), 3)
    head = lax.broadcasted_iota(jnp.int32, (1, heads, 1, LANES), 1)
    start = first + head * HEAD_DIM
    here = jnp.logical_and(lane >= start, lane < start + HEAD_DIM)
    out = jnp.where(here, wide, jnp.zeros((), x.dtype))
    if ones_at is not None:
        at = ones_at + 3 * head
        out = jnp.where(jnp.logical_and(lane >= at, lane < at + 3), jnp.ones((), x.dtype), out)
    return out.reshape(2, heads * rows // 2, LANES)


def to_all(x, axis="ulysses"):
    ways = lax.axis_size(axis)
    sent = jnp.broadcast_to(x[None], (ways,) + x.shape)
    return lax.all_to_all(sent, axis, split_axis=0, concat_axis=0, tiled=True)


def summed_at_owner(x, axis="ulysses"):
    ways = lax.axis_size(axis)
    sent = x.astype(BF16).reshape(ways, -1, x.shape[1])
    got = lax.all_to_all(sent, axis, split_axis=0, concat_axis=0, tiled=True)
    return jnp.sum(got.astype(F32), axis=0)


def swapped(x, axis="core"):
    return lax.ppermute(x, axis, [(0, 1), (1, 0)])


def reduced(x, axis):
    ways = lax.axis_size(axis)
    me = lax.axis_index(axis)

    def rows_of(k):
        return lax.dynamic_index_in_dim(x, lax.rem(me + k, ways), axis=0, keepdims=False)

    got = [
        lax.ppermute(rows_of(k).astype(BF16), axis, [(i, (i + k) % ways) for i in range(ways)])
        for k in range(1, ways)
    ]
    total = rows_of(0)
    for g in got:
        total += g.astype(F32)
    return total


def on_device(
    tokens,
    stretch_order,
    ln_gain,
    ln_bias,
    w_qkv,
    qv_bias,
    w_out,
    out_bias,
    w_up,
    up_bias,
    w_down,
    down_bias,
    cotangent,
):
    own_rows, width = tokens.shape
    ways = lax.axis_size("ulysses")
    wide = lax.axis_size(WIDE)
    me = lax.axis_index("ulysses")
    rows = own_rows * ways
    heads = HEADS // ways
    part = width // ways
    held = w_qkv.shape[1]
    ff_held = w_down.shape[1]
    ff_part = ff_held * wide
    pair = 2 * held

    order = stretch_order[0]
    own = lax.dynamic_slice(order, (2 * lax.axis_index(BLK),), (2,))
    count = order.shape[0]
    index = jnp.arange(count, dtype=jnp.int32)
    slots = jnp.sum(jnp.where(order[None, :] == index[:, None], index[None, :], 0), axis=1)
    core = lax.axis_index("core")
    deep = lax.axis_size("z")
    flat = lax.axis_size(("batch", "xlo"))

    small = jnp.concatenate(
        [
            ln_gain,
            ln_bias,
            qv_bias,
            jnp.concatenate([out_bias, down_bias], axis=1),
            up_bias.reshape(2, pair),
        ],
        axis=0,
    )
    qkv_slices = w_qkv[0].reshape(held, 3, ways, part).transpose(2, 0, 1, 3).reshape(ways, held, 3 * part)
    up_slices = w_up[0].reshape(held, wide, ways, ff_held).transpose(2, 0, 1, 3).reshape(ways, held, ff_part)
    first = jnp.concatenate(
        [
            qkv_slices,
            jnp.broadcast_to(small[None], (ways,) + small.shape),
            jnp.zeros((ways, held, width - 3 * part - pair), BF16),
        ],
        axis=2,
    )
    blank = jnp.zeros((ways, 8 - held, width), BF16)
    sent = jnp.concatenate(
        [
            jnp.broadcast_to(tokens[None], (ways,) + tokens.shape),
            first,
            blank,
            up_slices,
            blank,
            jnp.broadcast_to(w_out[0][None], (ways, held, width)),
            blank,
        ],
        axis=1,
    )
    got = lax.all_to_all(sent, "ulysses", split_axis=0, concat_axis=0, tiled=True)
    x = got[:, :own_rows].reshape(rows, width)
    at = own_rows
    piece = got[:, at : at + held, : 3 * part + 64].reshape(ways * held, 3 * part + 64)
    filled = lax.all_gather(piece, WIDE, axis=0, tiled=True)
    ffn = jnp.concatenate(
        [
            got[:, at + 8 : at + 8 + held].reshape(ways * held, width),
            got[:, at + 16 : at + 16 + held].reshape(ways * held, width),
            w_down[0],
        ],
        axis=1,
    )
    w_qkv_u = filled[:, : 3 * part]
    smalls = filled[:, 3 * part : 3 * part + pair].reshape(wide * ways, held, pair).astype(F32)
    gains = smalls[:, 0].reshape(-1)
    shifts = smalls[:, 1].reshape(-1)
    qv_all = smalls[:, 2].reshape(-1)
    out_bias_all = smalls[:, 3, :held].reshape(-1)
    down_bias_all = smalls[:, 3, held:].reshape(-1)
    up_bias_all = smalls[:, 4:].reshape(wide, ways, ff_held)
    up_bias_u = lax.dynamic_index_in_dim(up_bias_all, me, axis=1, keepdims=False).reshape(-1)
    bias_q = lax.dynamic_slice(qv_all, (me * part,), (part,))
    bias_v = lax.dynamic_slice(qv_all, (width + me * part,), (part,))

    n1, r1 = normalized(x.astype(F32))
    h1 = (n1 * gains[:width] + shifts[:width]).astype(BF16)
    proj_bias = jnp.concatenate([bias_q, jnp.zeros((part,), F32), bias_v])
    proj = (mm(h1, w_qkv_u) + proj_bias).astype(BF16)
    q_scaled = proj[:, :part] * jnp.asarray(1.0 / math.sqrt(HEAD_DIM), BF16)
    kv = proj[:, part:]
    kv_all = lax.all_gather(kv, BLK, axis=0, tiled=True)
    q_heads = head_lanes(q_scaled, heads, 0)

    df_own = cotangent.astype(BF16)
    df_own, kv = lax.optimization_barrier((df_own, kv))
    df = to_all(df_own).reshape(rows, width)
    ffn, kv_all, df = lax.optimization_barrier((ffn, kv_all, df))
    ffn_all = lax.all_gather(ffn, WIDE, axis=0, tiled=True)

    ctx_low, ctx, lse = attend(slots, own, q_heads, kv_all, heads)
    ctx_all = to_all(ctx_low)
    q_wide = jnp.pad(q_scaled, ((0, 0), (EXTRA, 0)))
    q_wide, ctx_all = lax.optimization_barrier((q_wide, ctx_all))
    q_all = lax.all_gather(q_wide, BLK, axis=0, tiled=True)
    gain_two = gains[width:]
    vectors = jnp.stack(
        [gain_two, shifts[width:], out_bias_all, up_bias_u] + [jnp.zeros((width,), F32)] * 4
    )
    x2_own, h2, act, du, dh2, down = feed_forward(me[None], x, ctx_all, df, vectors, ffn_all)
    dh2 = summed_at_owner(dh2)
    w_out_u = lax.dynamic_slice(ffn_all, (me * part, width), (part, width))
    g_up_bias = jnp.sum(du.astype(F32), axis=0)
    g_down_bias = jnp.sum(df_own.astype(F32), axis=0)

    n2_own, r2_own = normalized(x2_own)
    dx2 = cotangent + norm_back(dh2, gain_two, n2_own, r2_own)
    g_gain_two = jnp.sum(dh2 * n2_own, axis=0)
    g_shift_two = jnp.sum(dh2, axis=0)
    dc_own, q_all = lax.optimization_barrier((dx2.astype(BF16), q_all))
    g_out_bias = jnp.sum(dc_own.astype(F32), axis=0)
    dc = to_all(dc_own).reshape(rows, width)

    w_out_wide = jnp.pad(w_out_u, ((EXTRA, 0), (0, 0)))
    packed, q_ext, d_ext = prepare(dc, w_out_wide, ctx, lse, q_heads, heads)
    packed_all = lax.all_gather(packed, BLK, axis=0, tiled=True)
    down, packed = lax.optimization_barrier((down, packed))
    result = summed_at_owner(down) + x2_own + down_bias_all
    early, early_sent = weight_grads(core[None], h2, du, act, df, ctx_low, dc, wide, deep)
    early = early + swapped(early_sent).astype(F32)
    early, q_ext = lax.optimization_barrier((early, q_ext))
    early = reduced(early.reshape(deep, flat * early.shape[1], width), "z")
    d_query = query_grad(slots, own, q_ext, d_ext, kv_all, heads)
    early, packed_all = lax.optimization_barrier((early, packed_all))
    early = reduced(early.reshape(flat, -1, width), ("batch", "xlo"))
    k_heads = head_lanes(kv[:, :part], heads, EXTRA, 0)
    v_heads = head_lanes(kv[:, part:], heads, EXTRA, 3 * heads)
    d_key, d_value = key_grad(slots, own, k_heads, v_heads, q_all, packed_all, heads)
    d_proj = jnp.concatenate([d_query, d_key, d_value], axis=1)
    dh1 = summed_at_owner(mm_nt(d_proj, w_qkv_u))
    g_w_qkv = mm_tn(h1, d_proj)
    n1_own, r1_own = normalized(tokens.astype(F32))
    d_tokens = dx2 + norm_back(dh1, gains[:width], n1_own, r1_own)
    g_gain_one = jnp.sum(dh1 * n1_own, axis=0)
    g_shift_one = jnp.sum(dh1, axis=0)

    g_up_rows = early[:ff_held]
    o_w_down = early[ff_held : 2 * ff_held]
    out_rows = early[2 * ff_held : 2 * ff_held + held]
    owners = wide * ways
    o_w_out = lax.ppermute(
        out_rows, ALL, [(w * ways + u, u * wide + w) for w in range(wide) for u in range(ways)]
    )

    d_sums = jnp.sum(d_proj.astype(F32), axis=0)
    g_qv = jnp.zeros((2, ways, part), F32)
    g_qv = lax.dynamic_update_slice(g_qv, d_sums[:part].reshape(1, 1, part), (0, me, 0))
    g_qv = lax.dynamic_update_slice(g_qv, d_sums[2 * part :].reshape(1, 1, part), (1, me, 0))
    g_up_full = jnp.zeros((wide, ways, ff_held), F32)
    g_up_full = lax.dynamic_update_slice(
        g_up_full, g_up_bias.reshape(wide, 1, ff_held), (0, me, 0)
    )
    small_grads = jnp.concatenate(
        [
            jnp.concatenate([g_gain_one, g_gain_two]).reshape(owners, 1, pair),
            jnp.concatenate([g_shift_one, g_shift_two]).reshape(owners, 1, pair),
            g_qv.reshape(owners, 1, pair),
            jnp.concatenate(
                [g_out_bias.reshape(owners, 1, held), g_down_bias.reshape(owners, 1, held)], axis=2
            ),
            g_up_full.reshape(owners, 2, pair),
        ],
        axis=1,
    ).reshape(owners * held, pair)
    late = jnp.concatenate([g_w_qkv, jnp.pad(small_grads, ((0, 0), (0, 64 - pair)))], axis=1)
    late = late.reshape(flat, deep, 2, ways * held, late.shape[1]).transpose(2, 1, 0, 3, 4)
    late_sent = lax.dynamic_index_in_dim(late, 1 - core, axis=0, keepdims=False).astype(BF16)
    late = lax.dynamic_index_in_dim(late, core, axis=0, keepdims=False)
    late = late + swapped(late_sent).astype(F32)
    late = reduced(late.reshape(deep, flat * ways * held, -1), "z")
    late = reduced(late.reshape(flat, ways * held, -1), ("batch", "xlo"))
    last = jnp.concatenate([late, g_up_rows], axis=1).reshape(ways, held, -1)
    last = lax.all_to_all(last, "ulysses", split_axis=0, concat_axis=0, tiled=True)
    o_w_qkv = last[:, :, : 3 * part].reshape(ways, held, 3, part).transpose(1, 2, 0, 3)
    o_small = jnp.sum(last[:, :, 3 * part : 3 * part + pair], axis=0)
    o_w_up = last[:, :, 3 * part + 64 :].reshape(ways, held, wide, ff_held).transpose(1, 2, 0, 3)
    return (
        result,
        d_tokens,
        o_small[0:1],
        o_small[1:2],
        o_w_qkv.reshape(1, held, 3 * width),
        o_small[2:3],
        o_w_out[None],
        o_small[3:4, :held],
        o_w_up.reshape(1, held, -1),
        o_small[4:6].reshape(1, ff_held),
        o_w_down[None],
        o_small[3:4, held:],
    )


def solution(mesh):
    chips_z = mesh.shape["blk"] // 4
    parts = Mesh(
        mesh.devices.reshape(mesh.shape["batch"], 2, chips_z, 2, mesh.shape["ulysses"]), ALL
    )
    rows = P(ALL, None)
    flat = P(None, ALL)
    deep = P(None, ALL, None)
    return jax.shard_map(
        on_device,
        mesh=parts,
        in_specs=(
            rows, P("batch", None), flat, flat, deep, flat, deep, flat, deep, flat, deep, flat, rows,
        ),
        out_specs=(rows, rows, flat, flat, deep, flat, deep, flat, deep, flat, deep, flat),
        check_vma=False,
    )
```

time: 478 us -> 396 us (0.83)
  Pallas kernels: 119 us -> 74.5 us
  waiting for transfers between devices: 163 us -> 120 us
  blocking collectives: 26.3 us -> 40 us
    pallas_call x4 -> x5, Pallas kernels: 108 us -> 63.5 us  [the longest x4 57.4 us: call(): pl.pallas_call(functools.partial(kernel, **static), out_shape=tuple((jax....]
    all_gather x1, waiting for transfers between devices: 48.1 us -> 10.1 us  [on_device(): ffn_all = lax.all_gather(ffn, WIDE, axis=0, tiled=True)]
    ppermute x2 -> x14, starting transfers between devices: 4.88 us -> 30.2 us  [the longest x12 29.9 us: reduced(): lax.ppermute(rows_of(k).astype(BF16), axis, [(i, (i + k) % ways) for i in...]
    all_to_all x5 -> x3, starting transfers between devices: 37.2 us -> 12.2 us  [summed_at_owner(): got = lax.all_to_all(sent, axis, split_axis=0, concat_axis=0, tiled=True)]
    all_to_all x5 -> x3, waiting for transfers between devices: 40.6 us -> 23.1 us  [summed_at_owner(): got = lax.all_to_all(sent, axis, split_axis=0, concat_axis=0, tiled=True)]
    all_gather x1, waiting for transfers between devices: 36.2 us -> 22.4 us  [on_device(): kv_all = lax.all_gather(kv, BLK, axis=0, tiled=True)]
    all_to_all x0 -> x1, blocking collectives: none -> 13.7 us  [to_all(): return lax.all_to_all(sent, axis, split_axis=0, concat_axis=0, tiled=True)]
    ppermute x2 -> x14, waiting for transfers between devices: 0.01 us -> 13.4 us  [the longest x12 13.4 us: reduced(): lax.ppermute(rows_of(k).astype(BF16), axis, [(i, (i + k) % ways) for i in...]
  transfers between devices with their start and end apart: 17 -> 26, of which waited for: 11 -> 16; matrix products, arithmetic and copies ran while one was open for 11% -> 12% of each run, Pallas kernels for 25% -> 12%
where the time goes in v2:
time: 396 us; the launch traced here: 391 us
  waiting for transfers between devices  120 us (30%)
  Pallas kernels  74.5 us (19%)
  starting transfers between devices  61.5 us (16%)
  local copies, waits for them, and re-layouts  50.7 us (13%)
  blocking collectives  40 us (10%)
  other arithmetic  23.6 us (6%)
  between operations  14.9 us (4%)
  matrix products  5.45 us (1%)
    pallas_call x4, Pallas kernels, call(): pl.pallas_call(functools.partial(kernel, **static), out_shape=tuple((jax....  57.4 us
    ppermute x12, starting transfers between devices, reduced(): lax.ppermute(rows_of(k).astype(BF16), axis, [(i, (i + k) % ways) for i in...  29.9 us
    all_gather x1, blocking collectives, on_device(): filled = lax.all_gather(piece, WIDE, axis=0, tiled=True)  26.3 us
    all_to_all x2, waiting for transfers between devices, to_all(): return lax.all_to_all(sent, axis, split_axis=0, concat_axis=0, tiled=True)  23.1 us
    all_to_all x3, waiting for transfers between devices, summed_at_owner(): got = lax.all_to_all(sent, axis, split_axis=0, concat_axis=0, tiled=True)  23.1 us
    all_gather x1, waiting for transfers between devices, on_device(): kv_all = lax.all_gather(kv, BLK, axis=0, tiled=True)  22.4 us
    all_to_all x1, waiting for transfers between devices, on_device(): lax.all_to_all(sent, 'ulysses', split_axis=0, concat_axis=0, tiled=True)  13.9 us
    all_to_all x1, blocking collectives, to_all(): return lax.all_to_all(sent, axis, split_axis=0, concat_axis=0, tiled=True)  13.7 us
  transfers between devices with their start and end apart: 26, of which 16 were waited for; matrix products, arithmetic and copies ran while one was open for 12% of the time, Pallas kernels for 12%

profile of v2, /device:TPU:0, one launch (start us, length us, event | category | flops | bytes accessed | tf_op | source)
XLA Modules:
  0.0 391.0 jit_solution(9712081863498037638)
XLA Ops:
  14.2 4.2 %concatenate.52 = bf16[4,152,768]{2,1,0:T(8,128)(2,1)} concatenate(bf16[4,128,768]{2,1,0:T(8,128)(2,1)S(1)} %broadcast_in_dim.186, bf16[4,6,768]{2,1,0:T(8,128)(2,1)S(1)} %copy.199, bf16[4,2,768]{2,1,0:T(2,128)(2,1)S(1)} %broadcast_in_dim.189, bf16[4,6,768]{2,1,0:T(8,128)(2,1)S(1)} %reshape.400, bf16[4,2,768]{2,1,0:T(2,128)(2,1)S(1)} %broadcast_in_dim.189, ...), dimensions={1} | concatenate | bytes 1867776 | tf_op jit(solution)/shard_map/concatenate | solution.py:596
  18.4 4.5 %all-to-all-start = ((bf16[4,152,768]{2,1,0:T(8,128)(2,1)}), bf16[4,152,768]{2,1,0:T(8,128)(2,1)S(1)}, u32[]{:S(2)}, u32[]{:S(2)}) async-start(bf16[4,152,768]{2,1,0:T(8,128)(2,1)} %concatenate.52), calls=%async_computation | async-start | bytes 1867776 | tf_op jit(solution)/shard_map/all_to_all | solution.py:608
  22.9 13.9 %all-to-all-done = bf16[4,152,768]{2,1,0:T(8,128)(2,1)S(1)} async-done(((bf16[4,152,768]{2,1,0:T(8,128)(2,1)}), bf16[4,152,768]{2,1,0:T(8,128)(2,1)S(1)}, u32[]{:S(2)}, u32[]{:S(2)}) %all-to-all-start) | async-done | bytes 933920 | tf_op jit(solution)/shard_map/all_to_all | solution.py:608
  36.8 26.3 %all_gather.15 = bf16[768,640]{1,0:T(8,128)(2,1)S(1)} all-gather(bf16[24,640]{1,0:T(8,128)(2,1)S(1)} %reshape.371), channel_id=1, replica_groups=mesh['batch'=2,'xlo'=2,'z'=4,'core'=2,'ulysses'=4] {'batch','xlo','z','c..., dimensions={0}, use_global_device_ids=true | all-gather | bytes 1013760 | tf_op jit(solution)/shard_map/all_gather | solution.py:612
  66.6 1.5 copy.203
  68.2 1.5 copy.202
  76.7 3.5 all-to-all-start.1
  81.0 12.3 %all-to-all-done.1 = bf16[4,128,768]{2,1,0:T(8,128)(2,1)S(1)} async-done(((bf16[4,128,768]{2,1,0:T(8,128)(2,1)}), bf16[4,128,768]{2,1,0:T(8,128)(2,1)S(1)}, u32[]{:S(2)}, u32[]{:S(2)}) %all-to-all-start.1) | async-done | bytes 786464 | tf_op jit(solution)/shard_map/all_to_all | solution.py:508
  93.3 22.4 %all-gather.5.cloned.1.call-done.kv = bf16[8192,384]{1,0:T(8,128)(2,1)} async-done(((bf16[512,384]{1,0:T(8,128)(2,1)}), bf16[8192,384]{1,0:T(8,128)(2,1)}) %all-gather.5.cloned.1.call-update) | async-done | bytes 6291472 | tf_op jit(solution)/shard_map/all_gather | solution.py:639
  120.1 13.7 %attend.1 = (bf16[512,192]{1,0:T(8,128)(2,1)}, f32[512,256]{1,0:T(8,128)}, f32[2,768,1]{2,1,0:T(8,128)}) custom-call(s32[32]{0:T(128)} %select_reduce_fusion.slots, s32[2]{0:T(128)} %fusion.43.own, bf16[2,768,256]{2,1,0:T(8,128)(2,1)} %bitcast_select_fusion.2.q_heads, bf16[8192,384]{1,0:T(8,128)(2,1)} %all-gather.5.cloned.1.call-done.kv), custom_call_target="tpu_custom_call" | custom-call | flops 12884901888 | bytes 6291456 | tf_op jit(solution)/shard_map/attend/pallas_call | solution.py:284
  134.9 13.7 %all_to_all.40 = bf16[4,512,192]{1,2,0:T(8,128)(2,1)S(1)} all-to-all(bf16[4,512,192]{1,2,0:T(8,128)(2,1)S(1)} %broadcast_in_dim.203), channel_id=1, replica_groups=mesh['batch'=2,'xlo'=2,'z'=4,'core'=2,'ulysses'=4] {'ulysses'}, dimensions={0} | all-to-all | bytes 1572864 | tf_op jit(solution)/shard_map/all_to_all | solution.py:508
  154.6 10.1 %all-gather.7.cloned.1.call-done.w_up.w_out.w_down = bf16[768,2304]{1,0:T(8,128)(2,1)} async-done(((bf16[24,2304]{1,0:T(8,128)(2,1)}), bf16[768,2304]{1,0:T(8,128)(2,1)}) %all-gather.7.cloned.1.call-update) | async-done | bytes 3538960 | tf_op jit(solution)/shard_map/all_gather | solution.py:646
  164.7 11.1 %feed_forward.1 = (f32[128,768]{1,0:T(8,128)}, bf16[512,768]{1,0:T(8,128)(2,1)}, bf16[512,768]{1,0:T(8,128)(2,1)}, bf16[512,768]{1,0:T(8,128)(2,1)}, bf16[512,768]{1,0:T(8,128)(2,1)}, /*index=5*/bf16[512,768]{1,0:T(8,128)(2,1)}) custom-call(s32[1]{0:T(128)} %bitcast.me, bf16[512,768]{1,0:T(8,128)(2,1)} %bitcast.141, bf16[4,512,192]{2,1,0:T(8,128)(2,1)} %copy.211.ctx, ...), custom_call_target="tpu_custom_call" | custom-call | flops 3019898880 | bytes 3538944 | tf_op jit(solution)/shard_map/feed_forward/pallas_call | solution.py:385
  175.7 4.4 %all-to-all-start.3 = ((bf16[4,128,768]{2,1,0:T(8,128)(2,1)}), bf16[4,128,768]{2,1,0:T(8,128)(2,1)S(1)}, u32[]{:S(2)}, u32[]{:S(2)}) async-start(bf16[4,128,768]{2,1,0:T(8,128)(2,1)} %bitcast.157), calls=%async_computation.3 | async-start | bytes 1572864 | tf_op jit(solution)/shard_map/all_to_all | solution.py:514
  180.6 12.3 %all-to-all-done.3 = bf16[4,128,768]{2,1,0:T(8,128)(2,1)S(1)} async-done(((bf16[4,128,768]{2,1,0:T(8,128)(2,1)}), bf16[4,128,768]{2,1,0:T(8,128)(2,1)S(1)}, u32[]{:S(2)}, u32[]{:S(2)}) %all-to-all-start.3) | async-done | bytes 786464 | tf_op jit(solution)/shard_map/all_to_all | solution.py:514
  194.4 9.0 %all-gather.9.cloned.1.call-done.q_all = bf16[8192,256]{1,0:T(8,128)(2,1)} async-done(((bf16[512,256]{1,0:T(8,128)(2,1)}), bf16[8192,256]{1,0:T(8,128)(2,1)}) %all-gather.9.cloned.1.call-update) | async-done | bytes 4194320 | tf_op jit(solution)/shard_map/all_gather | solution.py:652
  204.4 4.4 %all-to-all-start.4 = ((bf16[4,128,768]{2,1,0:T(8,128)(2,1)}), bf16[4,128,768]{2,1,0:T(8,128)(2,1)S(1)}, u32[]{:S(2)}, u32[]{:S(2)}) async-start(bf16[4,128,768]{2,1,0:T(8,128)(2,1)} %broadcast_in_dim.204), calls=%async_computation.4 | async-start | bytes 1572864 | tf_op jit(solution)/shard_map/all_to_all | solution.py:508
  210.6 10.8 %all-to-all-done.4 = bf16[4,128,768]{2,1,0:T(8,128)(2,1)S(1)} async-done(((bf16[4,128,768]{2,1,0:T(8,128)(2,1)}), bf16[4,128,768]{2,1,0:T(8,128)(2,1)S(1)}, u32[]{:S(2)}, u32[]{:S(2)}) %all-to-all-start.4) | async-done | bytes 786464 | tf_op jit(solution)/shard_map/all_to_all | solution.py:508
  222.4 4.4 %prepare.1 = (bf16[512,256]{1,0:T(8,128)(2,1)}, bf16[2,768,256]{2,1,0:T(8,128)(2,1)}, bf16[2,768,256]{2,1,0:T(8,128)(2,1)}) custom-call(bf16[512,768]{1,0:T(8,128)(2,1)} %bitcast.146, bf16[256,768]{1,0:T(8,128)(2,1)} %pad.24.w_out, f32[512,256]{1,0:T(8,128)} %get-tuple-element.53.ctx, f32[2,768,1]{2,1,0:T(8,128)} %get-tuple-element.54.lse, ...), custom_call_target="tpu_custom_call" | custom-call | flops 201326592 | bytes 1572864 | tf_op jit(solution)/shard_map/prepare/pallas_call | solution.py:284
  227.7 6.1 %weight_grads.1 = (f32[16,56,768]{2,1,0:T(8,128)}, bf16[16,56,768]{2,1,0:T(8,128)(2,1)}) custom-call(s32[1]{0:T(128)} %bitcast.17.core, bf16[512,768]{1,0:T(8,128)(2,1)} %get-tuple-element.57.h2, bf16[512,768]{1,0:T(8,128)(2,1)} %get-tuple-element.58.du, bf16[512,768]{1,0:T(8,128)(2,1)} %get-tuple-element.59.act, bf16[512,768]{1,0:T(8,128)(2,1)} %bitcast.145, ...), custom_call_target="tpu_custom_call" | custom-call | flops 1207959552 | bytes 4128768 | tf_op jit(solution)/shard_map/weight_grads/pallas_call | solution.py:446
  234.0 3.5 all-to-all-start.5
  239.3 1.6 fusion.5
  243.1 7.5 %all-to-all-done.5 = bf16[4,128,768]{2,1,0:T(8,128)(2,1)S(1)} async-done(((bf16[4,128,768]{2,1,0:T(8,128)(2,1)}), bf16[4,128,768]{2,1,0:T(8,128)(2,1)S(1)}, u32[]{:S(2)}, u32[]{:S(2)}) %all-to-all-start.5) | async-done | bytes 786464 | tf_op jit(solution)/shard_map/all_to_all | solution.py:514
  251.5 2.5 convert_add_fusion
  255.0 1.7 collective-permute-start.3
  256.7 1.9 collective-permute-start.2
  258.6 15.4 %query_grad.1 = bf16[512,192]{1,0:T(8,128)(2,1)} custom-call(s32[32]{0:T(128)} %select_reduce_fusion.slots, s32[2]{0:T(128)} %fusion.43.own, bf16[2,768,256]{2,1,0:T(8,128)(2,1)} %get-tuple-element.63.q_ext, bf16[2,768,256]{2,1,0:T(8,128)(2,1)} %get-tuple-element.64.d_ext, bf16[8192,384]{1,0:T(8,128)(2,1)} %all-gather.5.cloned.1.call-done.kv), custom_call_target="tpu_custom_call" | custom-call | flops 19327352832 | bytes 6291456 | tf_op jit(solution)/shard_map/query_grad/pallas_call | solution.py:284
  274.0 1.7 collective-permute-done.1
  275.7 2.1 fusion.8
  277.8 23.9 %key_grad.1 = (bf16[512,192]{1,0:T(8,128)(2,1)}, bf16[512,192]{1,0:T(8,128)(2,1)}) custom-call(s32[32]{0:T(128)} %select_reduce_fusion.slots, s32[2]{0:T(128)} %fusion.43.own, bf16[2,768,256]{2,1,0:T(8,128)(2,1)} %get-tuple-element.181.k_heads, bf16[2,768,256]{2,1,0:T(8,128)(2,1)} %get-tuple-element.180.v_heads, ...), custom_call_target="tpu_custom_call" | custom-call | flops 25769803776 | bytes 6291456 | tf_op jit(solution)/shard_map/key_grad/pallas_call | solution.py:284
  301.7 2.8 convolution_convert_fusion
  304.5 4.3 %all-to-all-start.6 = ((bf16[4,128,768]{2,1,0:T(8,128)(2,1)}), bf16[4,128,768]{2,1,0:T(8,128)(2,1)}, u32[]{:S(2)}, u32[]{:S(2)}) async-start(bf16[4,128,768]{2,1,0:T(8,128)(2,1)} %bitcast.30), calls=%async_computation.6 | async-start | bytes 1572864 | tf_op jit(solution)/shard_map/all_to_all | solution.py:514
  308.9 1.8 fusion.31
  310.7 2.0 collective-permute-start.11
  313.2 1.9 fusion.45
  315.1 3.3 all-to-all-done.6
  318.4 1.5 convert_reduce_fusion
  323.4 1.4 select_maximum_fusion
  324.8 1.9 copy.220
  331.2 17.2 %collective-permute-start.7 = (bf16[96,640]{1,0:T(8,128)(2,1)S(1)}, bf16[96,640]{1,0:T(8,128)(2,1)S(1)}, u32[]{:S(2)}, u32[]{:S(2)}) collective-permute-start(bf16[96,640]{1,0:T(8,128)(2,1)S(1)} %get-tuple-element.160), channel_id=1, source_target_pairs={{0,24},{8,0},{16,8},{24,16},{1,25},{9,1},{17,9},{25,17},{2,26},{10... | collective-permute-start | bytes 368648 | tf_op jit(solution)/shard_map/ppermute | solution.py:530
  349.4 3.1 collective-permute-done.7
  352.5 2.5 collective-permute-done.6
  356.0 4.5 %collective-permute-start.10 = (bf16[24,640]{1,0:T(8,128)(2,1)S(1)}, bf16[24,640]{1,0:T(8,128)(2,1)S(1)}, u32[]{:S(2)}, u32[]{:S(2)}) collective-permute-start(bf16[24,640]{1,0:T(8,128)(2,1)S(1)} %get-tuple-element.178), channel_id=1, source_target_pairs={{0,96},{32,0},{64,32},{96,64},{1,97},{33,1},{65,33},{97,65},{2,98}... | collective-permute-start | bytes 92168 | tf_op jit(solution)/shard_map/ppermute | solution.py:530
  360.5 1.6 collective-permute-start.9
  362.2 3.7 collective-permute-done.9
  365.9 1.3 collective-permute-done.8
  368.0 5.6 %all-to-all-start.7 = ((f32[4,6,1408]{2,1,0:T(8,128)}), f32[4,6,1408]{2,1,0:T(8,128)S(1)}, u32[]{:S(2)}, u32[]{:S(2)}) async-start(f32[4,6,1408]{2,1,0:T(8,128)} %reshape.393), calls=%async_computation.7 | async-start | bytes 360448 | tf_op jit(solution)/shard_map/all_to_all | solution.py:730
  374.5 5.3 %all-to-all-done.7 = f32[4,6,1408]{2,1,0:T(8,128)S(1)} async-done(((f32[4,6,1408]{2,1,0:T(8,128)}), f32[4,6,1408]{2,1,0:T(8,128)S(1)}, u32[]{:S(2)}, u32[]{:S(2)}) %all-to-all-start.7) | async-done | bytes 135200 | tf_op jit(solution)/shard_map/all_to_all | solution.py:730
  (248 shorter events, 58.3 us)
Async XLA Ops:
  7.2 7.0 %copy-start.24 = (bf16[1,6,768]{2,1,0:T(8,128)(2,1)S(1)}, bf16[1,6,768]{2,1,0:T(8,128)(2,1)}, u32[]{:S(2)}) copy-start(bf16[1,6,768]{2,1,0:T(8,128)(2,1)} %param.19) | copy-start | bytes 27652
  18.4 18.4 %all-to-all-start = ((bf16[4,152,768]{2,1,0:T(8,128)(2,1)}), bf16[4,152,768]{2,1,0:T(8,128)(2,1)S(1)}, u32[]{:S(2)}, u32[]{:S(2)}) async-start(bf16[4,152,768]{2,1,0:T(8,128)(2,1)} %concatenate.52), calls=%async_computation | async-start | bytes 1867776 | tf_op jit(solution)/shard_map/all_to_all | solution.py:608
  22.9 92.8 %all-gather.5.cloned.1.call-start = ((), (), s32[]{:S(2)}) async-start(), calls=%async_computation.8 | async-start | bytes 6684672 | tf_op jit(solution)/shard_map/all_gather | solution.py:639
  73.0 2.7 copy-start.9
  75.8 4.6 %copy-start.23 = (bf16[1,24,768]{2,1,0:T(8,128)(2,1)S(1)}, bf16[1,24,768]{2,1,0:T(8,128)(2,1)}, u32[]{:S(2)}) copy-start(bf16[1,24,768]{2,1,0:T(8,128)(2,1)} %param.23) | copy-start | bytes 110596
  75.8 40.2 %copy-start.28 = (s32[1,32]{1,0:T(1,128)S(1)}, s32[1,32]{1,0:T(1,128)}, u32[]{:S(2)}) copy-start(s32[1,32]{1,0:T(1,128)} %param.14) | copy-start | bytes 388
  76.7 16.5 %all-to-all-start.1 = ((bf16[4,128,768]{2,1,0:T(8,128)(2,1)}), bf16[4,128,768]{2,1,0:T(8,128)(2,1)S(1)}, u32[]{:S(2)}, u32[]{:S(2)}) async-start(bf16[4,128,768]{2,1,0:T(8,128)(2,1)} %broadcast_in_dim.202), calls=%async_computation.1 | async-start | bytes 1572864 | tf_op jit(solution)/shard_map/all_to_all | solution.py:508
  80.2 84.5 %all-gather.7.cloned.1.call-start = ((), (), s32[]{:S(2)}) async-start(), calls=%async_computation.9 | async-start | bytes 3649536 | tf_op jit(solution)/shard_map/all_gather | solution.py:646
  93.3 40.5 %copy-start.6 = (bf16[4,128,768]{2,1,0:T(8,128)(2,1)}, bf16[4,128,768]{2,1,0:T(8,128)(2,1)S(1)}, u32[]{:S(2)}) copy-start(bf16[4,128,768]{2,1,0:T(8,128)(2,1)S(1)} %all-to-all-done.1) | copy-start | bytes 2359300
  115.7 87.7 %all-gather.9.cloned.1.call-start = ((), (), s32[]{:S(2)}) async-start(), calls=%async_computation.10 | async-start | bytes 4456448 | tf_op jit(solution)/shard_map/all_gather | solution.py:652
  134.9 14.0 %copy-start.8 = (f32[64,1,12]{1,0,2:T(8,128)S(1)}, f32[64,1,12]{1,0,2:T(8,128)}, u32[]{:S(2)}) copy-start(f32[64,1,12]{1,0,2:T(8,128)} %get-tuple-element.167) | copy-start | bytes 9220
  175.7 4.5 %copy-start = (f32[128,768]{1,0:T(8,128)S(1)}, f32[128,768]{1,0:T(8,128)}, u32[]{:S(2)}) copy-start(f32[128,768]{1,0:T(8,128)} %get-tuple-element.49) | copy-start | bytes 1179652
  175.7 17.1 %all-to-all-start.3 = ((bf16[4,128,768]{2,1,0:T(8,128)(2,1)}), bf16[4,128,768]{2,1,0:T(8,128)(2,1)S(1)}, u32[]{:S(2)}, u32[]{:S(2)}) async-start(bf16[4,128,768]{2,1,0:T(8,128)(2,1)} %bitcast.157), calls=%async_computation.3 | async-start | bytes 1572864 | tf_op jit(solution)/shard_map/all_to_all | solution.py:514
  180.2 13.3 %copy-start.10 = (f32[128,768]{1,0:T(8,128)S(1)}, f32[128,768]{1,0:T(8,128)}, u32[]{:S(2)}) copy-start(f32[128,768]{1,0:T(8,128)} %param.25) | copy-start | bytes 1179652
  204.4 17.1 %all-to-all-start.4 = ((bf16[4,128,768]{2,1,0:T(8,128)(2,1)}), bf16[4,128,768]{2,1,0:T(8,128)(2,1)S(1)}, u32[]{:S(2)}, u32[]{:S(2)}) async-start(bf16[4,128,768]{2,1,0:T(8,128)(2,1)} %broadcast_in_dim.204), calls=%async_computation.4 | async-start | bytes 1572864 | tf_op jit(solution)/shard_map/all_to_all | solution.py:508
  208.8 69.0 %all-gather.11.cloned.1.call-start = ((), (), s32[]{:S(2)}) async-start(), calls=%async_computation.11 | async-start | bytes 4456448 | tf_op jit(solution)/shard_map/all_gather | solution.py:673
  222.4 4.5 %copy-start.4 = (bf16[128,768]{1,0:T(8,128)(2,1)S(1)}, bf16[128,768]{1,0:T(8,128)(2,1)}, u32[]{:S(2)}) copy-start(bf16[128,768]{1,0:T(8,128)(2,1)} %param.13) | copy-start | bytes 589828
  233.8 3.7 copy-start.5
  233.8 17.7 %collective-permute-start = (bf16[16,56,768]{2,1,0:T(8,128)(2,1)}, bf16[16,56,768]{2,1,0:T(8,128)(2,1)}, u32[]{:S(2)}, u32[]{:S(2)}) collective-permute-start(bf16[16,56,768]{2,1,0:T(8,128)(2,1)} %get-tuple-element.61), channel_id=1, source_target_pairs={{0,4},{4,0},{1,5},{5,1},{2,6},{6,2},{3,7},{7,3},{8,12},{12,8},{9,1... | collective-permute-start | bytes 4128776 | tf_op jit(solution)/shard_map/ppermute | solution.py:519
  234.0 16.6 %all-to-all-start.5 = ((bf16[4,128,768]{2,1,0:T(8,128)(2,1)}), bf16[4,128,768]{2,1,0:T(8,128)(2,1)S(1)}, u32[]{:S(2)}, u32[]{:S(2)}) async-start(bf16[4,128,768]{2,1,0:T(8,128)(2,1)} %bitcast.16), calls=%async_computation.5 | async-start | bytes 1572864 | tf_op jit(solution)/shard_map/all_to_all | solution.py:514
  255.0 19.0 %collective-permute-start.3 = (bf16[224,768]{1,0:T(8,128)(2,1)}, bf16[224,768]{1,0:T(8,128)(2,1)S(1)}, u32[]{:S(2)}, u32[]{:S(2)}) collective-permute-start(bf16[224,768]{1,0:T(8,128)(2,1)} %get-tuple-element.157), channel_id=1, source_target_pairs={{0,24},{8,0},{16,8},{24,16},{1,25},{9,1},{17,9},{25,17},{2,26},{10... | collective-permute-start | bytes 1032200 | tf_op jit(solution)/shard_map/ppermute | solution.py:530
  256.7 17.3 %collective-permute-start.2 = (bf16[224,768]{1,0:T(8,128)(2,1)}, bf16[224,768]{1,0:T(8,128)(2,1)}, u32[]{:S(2)}, u32[]{:S(2)}) collective-permute-start(bf16[224,768]{1,0:T(8,128)(2,1)} %get-tuple-element.158), channel_id=1, source_target_pairs={{0,16},{8,24},{16,0},{24,8},{1,17},{9,25},{17,1},{25,9},{2,18},{10... | collective-permute-start | bytes 1032200 | tf_op jit(solution)/shard_map/ppermute | solution.py:530
  258.6 17.1 %collective-permute-start.1 = (bf16[224,768]{1,0:T(8,128)(2,1)}, bf16[224,768]{1,0:T(8,128)(2,1)}, u32[]{:S(2)}, u32[]{:S(2)}) collective-permute-start(bf16[224,768]{1,0:T(8,128)(2,1)} %get-tuple-element.156), channel_id=1, source_target_pairs={{0,8},{8,16},{16,24},{24,0},{1,9},{9,17},{17,25},{25,1},{2,10},{10... | collective-permute-start | bytes 1032200 | tf_op jit(solution)/shard_map/ppermute | solution.py:530
  277.8 23.9 %copy-start.15 = (bf16[768,640]{1,0:T(8,128)(2,1)S(1)}, bf16[768,640]{1,0:T(8,128)(2,1)}, u32[]{:S(2)}) copy-start(bf16[768,640]{1,0:T(8,128)(2,1)} %copy-done.13) | copy-start | bytes 2949124
  277.8 23.9 %copy-start.16 = (bf16[512,192]{1,0:T(8,128)(2,1)S(1)}, bf16[512,192]{1,0:T(8,128)(2,1)}, u32[]{:S(2)}) copy-start(bf16[512,192]{1,0:T(8,128)(2,1)} %query_grad.1) | copy-start | bytes 589828
  304.5 8.2 %copy-start.17 = (bf16[512,192]{1,0:T(8,128)(2,1)S(1)}, bf16[512,192]{1,0:T(8,128)(2,1)}, u32[]{:S(2)}) copy-start(bf16[512,192]{1,0:T(8,128)(2,1)} %get-tuple-element.69) | copy-start | bytes 589828
  304.5 8.2 %copy-start.18 = (bf16[512,192]{1,0:T(8,128)(2,1)S(1)}, bf16[512,192]{1,0:T(8,128)(2,1)}, u32[]{:S(2)}) copy-start(bf16[512,192]{1,0:T(8,128)(2,1)} %get-tuple-element.70) | copy-start | bytes 589828
  304.5 8.6 %copy-start.3 = (bf16[512,768]{1,0:T(8,128)(2,1)S(1)}, bf16[512,768]{1,0:T(8,128)(2,1)}, u32[]{:S(2)}) copy-start(bf16[512,768]{1,0:T(8,128)(2,1)} %copy-done.2) | copy-start | bytes 2359300
  304.5 13.9 %all-to-all-start.6 = ((bf16[4,128,768]{2,1,0:T(8,128)(2,1)}), bf16[4,128,768]{2,1,0:T(8,128)(2,1)}, u32[]{:S(2)}, u32[]{:S(2)}) async-start(bf16[4,128,768]{2,1,0:T(8,128)(2,1)} %bitcast.30), calls=%async_computation.6 | async-start | bytes 1572864 | tf_op jit(solution)/shard_map/all_to_all | solution.py:514
  310.7 17.2 %collective-permute-start.13 = (bf16[56,768]{1,0:T(8,128)(2,1)}, bf16[56,768]{1,0:T(8,128)(2,1)}, u32[]{:S(2)}, u32[]{:S(2)}) collective-permute-start(bf16[56,768]{1,0:T(8,128)(2,1)} %get-tuple-element.171), channel_id=1, source_target_pairs={{0,96},{32,0},{64,32},{96,64},{1,97},{33,1},{65,33},{97,65},{2,98}... | collective-permute-start | bytes 258056 | tf_op jit(solution)/shard_map/ppermute | solution.py:530
  310.7 17.2 %collective-permute-start.12 = (bf16[56,768]{1,0:T(8,128)(2,1)}, bf16[56,768]{1,0:T(8,128)(2,1)}, u32[]{:S(2)}, u32[]{:S(2)}) collective-permute-start(bf16[56,768]{1,0:T(8,128)(2,1)} %get-tuple-element.172), channel_id=1, source_target_pairs={{0,64},{32,96},{64,0},{96,32},{1,65},{33,97},{65,1},{97,33},{2,66}... | collective-permute-start | bytes 258056 | tf_op jit(solution)/shard_map/ppermute | solution.py:530
  310.7 17.2 %collective-permute-start.11 = (bf16[56,768]{1,0:T(8,128)(2,1)}, bf16[56,768]{1,0:T(8,128)(2,1)}, u32[]{:S(2)}, u32[]{:S(2)}) collective-permute-start(bf16[56,768]{1,0:T(8,128)(2,1)} %get-tuple-element.170), channel_id=1, source_target_pairs={{0,32},{32,64},{64,96},{96,0},{1,33},{33,65},{65,97},{97,1},{2,34}... | collective-permute-start | bytes 258056 | tf_op jit(solution)/shard_map/ppermute | solution.py:530
  313.2 6.7 %copy-start.25 = (f32[128]{0:T(128)S(1)}, f32[128]{0:T(128)}, u32[]{:S(2)}) copy-start(f32[128]{0:T(128)} %add_rsqrt_fusion) | copy-start | bytes 1540
  315.1 5.8 %copy-start.21 = (f32[64,1,12]{2,0,1:T(8,128)S(1)}, f32[64,1,12]{2,0,1:T(8,128)}, u32[]{:S(2)}) copy-start(f32[64,1,12]{2,0,1:T(8,128)} %concatenate.57) | copy-start | bytes 9220
  315.1 5.8 %copy-start.22 = (f32[64,1,12]{2,0,1:T(8,128)S(1)}, f32[64,1,12]{2,0,1:T(8,128)}, u32[]{:S(2)}) copy-start(f32[64,1,12]{2,0,1:T(8,128)} %concatenate.60) | copy-start | bytes 9220
  324.8 2.3 copy-start.12
  326.8 4.2 %collective-permute-start.4 = (bf16[4,4,24,640]{3,2,0,1:T(8,128)(2,1)S(1)}, bf16[4,4,24,640]{3,2,0,1:T(8,128)(2,1)S(1)}, u32[]{:S(2)}, u32[]{:S(2)}) collective-permute-start(bf16[4,4,24,640]{3,2,0,1:T(8,128)(2,1)S(1)} %fusion.9), channel_id=1, source_target_pairs={{0,4},{4,0},{1,5},{5,1},{2,6},{6,2},{3,7},{7,3},{8,12},{12,8},{9,1... | collective-permute-start | bytes 1474568 | tf_op jit(solution)/shard_map/ppermute | solution.py:519
  329.0 1.3 collective-permute-start.14
  331.1 18.3 %copy-start.27 = (f32[128]{0:T(128)S(1)}, f32[128]{0:T(128)}, u32[]{:S(2)}) copy-start(f32[128]{0:T(128)} %get-tuple-element.151) | copy-start | bytes 1540
  331.1 31.1 %copy-start.26 = (f32[128]{0:T(128)S(1)}, f32[128]{0:T(128)}, u32[]{:S(2)}) copy-start(f32[128]{0:T(128)} %get-tuple-element.152) | copy-start | bytes 1540
  331.2 42.4 %copy-start.11 = (f32[128,768]{1,0:T(8,128)S(1)}, f32[128,768]{1,0:T(8,128)}, u32[]{:S(2)}) copy-start(f32[128,768]{1,0:T(8,128)} %get-tuple-element.155) | copy-start | bytes 1179652
  331.2 21.3 %collective-permute-start.7 = (bf16[96,640]{1,0:T(8,128)(2,1)S(1)}, bf16[96,640]{1,0:T(8,128)(2,1)S(1)}, u32[]{:S(2)}, u32[]{:S(2)}) collective-permute-start(bf16[96,640]{1,0:T(8,128)(2,1)S(1)} %get-tuple-element.160), channel_id=1, source_target_pairs={{0,24},{8,0},{16,8},{24,16},{1,25},{9,1},{17,9},{25,17},{2,26},{10... | collective-permute-start | bytes 368648 | tf_op jit(solution)/shard_map/ppermute | solution.py:530
  348.4 6.6 %collective-permute-start.6 = (bf16[96,640]{1,0:T(8,128)(2,1)S(1)}, bf16[96,640]{1,0:T(8,128)(2,1)S(1)}, u32[]{:S(2)}, u32[]{:S(2)}) collective-permute-start(bf16[96,640]{1,0:T(8,128)(2,1)S(1)} %get-tuple-element.161), channel_id=1, source_target_pairs={{0,16},{8,24},{16,0},{24,8},{1,17},{9,25},{17,1},{25,9},{2,18},{10... | collective-permute-start | bytes 368648 | tf_op jit(solution)/shard_map/ppermute | solution.py:530
  348.4 7.5 %collective-permute-start.5 = (bf16[96,640]{1,0:T(8,128)(2,1)S(1)}, bf16[96,640]{1,0:T(8,128)(2,1)S(1)}, u32[]{:S(2)}, u32[]{:S(2)}) collective-permute-start(bf16[96,640]{1,0:T(8,128)(2,1)S(1)} %get-tuple-element.159), channel_id=1, source_target_pairs={{0,8},{8,16},{16,24},{24,0},{1,9},{9,17},{17,25},{25,1},{2,10},{10... | collective-permute-start | bytes 368648 | tf_op jit(solution)/shard_map/ppermute | solution.py:530
  356.0 6.2 %collective-permute-start.10 = (bf16[24,640]{1,0:T(8,128)(2,1)S(1)}, bf16[24,640]{1,0:T(8,128)(2,1)S(1)}, u32[]{:S(2)}, u32[]{:S(2)}) collective-permute-start(bf16[24,640]{1,0:T(8,128)(2,1)S(1)} %get-tuple-element.178), channel_id=1, source_target_pairs={{0,96},{32,0},{64,32},{96,64},{1,97},{33,1},{65,33},{97,65},{2,98}... | collective-permute-start | bytes 92168 | tf_op jit(solution)/shard_map/ppermute | solution.py:530
  360.5 5.4 %collective-permute-start.9 = (bf16[24,640]{1,0:T(8,128)(2,1)S(1)}, bf16[24,640]{1,0:T(8,128)(2,1)S(1)}, u32[]{:S(2)}, u32[]{:S(2)}) collective-permute-start(bf16[24,640]{1,0:T(8,128)(2,1)S(1)} %get-tuple-element.179), channel_id=1, source_target_pairs={{0,64},{32,96},{64,0},{96,32},{1,65},{33,97},{65,1},{97,33},{2,66}... | collective-permute-start | bytes 92168 | tf_op jit(solution)/shard_map/ppermute | solution.py:530
  362.2 5.1 %collective-permute-start.8 = (bf16[24,640]{1,0:T(8,128)(2,1)S(1)}, bf16[24,640]{1,0:T(8,128)(2,1)S(1)}, u32[]{:S(2)}, u32[]{:S(2)}) collective-permute-start(bf16[24,640]{1,0:T(8,128)(2,1)S(1)} %get-tuple-element.177), channel_id=1, source_target_pairs={{0,32},{32,64},{64,96},{96,0},{1,33},{33,65},{65,97},{97,1},{2,34}... | collective-permute-start | bytes 92168 | tf_op jit(solution)/shard_map/ppermute | solution.py:530
  368.0 11.9 %all-to-all-start.7 = ((f32[4,6,1408]{2,1,0:T(8,128)}), f32[4,6,1408]{2,1,0:T(8,128)S(1)}, u32[]{:S(2)}, u32[]{:S(2)}) async-start(f32[4,6,1408]{2,1,0:T(8,128)} %reshape.393), calls=%async_computation.7 | async-start | bytes 360448 | tf_op jit(solution)/shard_map/all_to_all | solution.py:730
  (7 other events, 9.0 us)
Sparse Core Ops, SparseCore 0:
  75.8 39.8 all-gather.4
  118.0 46.6 all-gather.6
  166.4 36.9 all-gather.8
  226.9 36.7 all-gather.10

commit v3 on v2

--- a/solution.py
+++ b/solution.py
@@ -17,7 +17,6 @@
 EXTRA = 64
 BELOW_FLOOR = -1e30
 BLK = ("xlo", "z", "core")
-CHIPS = ("batch", "xlo", "z")
 WIDE = ("batch", "xlo", "z", "core")
 ALL = ("batch", "xlo", "z", "core", "ulysses")
 BF16 = jnp.bfloat16
@@ -156,7 +155,7 @@
         done = merged_heads(total[...] / row_sum, half, heads, EXTRA)
         rows = stretch(part, half)
         ctx[rows, :] = done
-        ctx_low[rows, :] = done[:, EXTRA:].astype(BF16)
+        ctx_low[:, rows] = done.T[EXTRA:, :].astype(BF16)
         return 0
 
     lax.fori_loop(0, 2, one_half, 0)
@@ -303,7 +302,7 @@
     width = heads * HEAD_DIM
     return call(
         attend_kernel, "attend", (slots, own), (q_heads, kv),
-        [((2 * half, width), BF16), ((2 * half, LANES), F32), ((2, deep, 1), F32)],
+        [((width, 2 * half), BF16), ((2 * half, LANES), F32), ((2, deep, 1), F32)],
         [((deep, 1), F32), ((deep, LANES), F32), ((deep, LANES), BF16), ((8, half), F32)],
         cost(2 * half, kv.shape[0], heads, 2), half=half, heads=heads,
     )
@@ -344,10 +343,7 @@
 def feed_forward_kernel(
     me, x, ctx, df, vectors, w_up, w_out, w_down, x2_own, h2, act, du, dh2, down
 ):
-    part = ctx.shape[2]
-    total = x[...].astype(F32) + vectors[2:3, :]
-    for u in range(ctx.shape[0]):
-        total += mm(ctx[u], w_out[u * part : (u + 1) * part, :])
+    total = x[...].astype(F32) + vectors[2:3, :] + mm_tn(ctx[...], w_out[...])
 
     @pl.when(pl.program_id(0) == me[0])
     def _():
@@ -363,110 +359,96 @@
     half = 0.5 * (1.0 + turn)
     act_low = (up * half).astype(BF16)
     act[...] = act_low
-    down[...] = mm(act_low, w_down[...]).astype(BF16)
+    down[...] = mm(act_low, w_down[...])
     slope = half + 0.5 * up * (1.0 - turn * turn) * (bend * (1.0 + 3 * 0.044715 * square))
     du_low = (slope * mm_nt(df[...], w_down[...])).astype(BF16)
     du[...] = du_low
     dh2[...] = mm_nt(du_low, w_up[...]).astype(BF16)
 
 
-def feed_forward(me, x, ctx, df, vectors, weights):
-    rows, width = x.shape
-    ways, _, part = ctx.shape
+def feed_forward(me, both, ctx, vectors, weights, ways):
+    rows = both.shape[0]
+    width = both.shape[1] // 2
     step = rows // ways
 
-    def along(cols):
-        return pl.BlockSpec((step, cols), lambda i, *_: (i, 0))
+    def along(c):
+        return pl.BlockSpec((step, width), lambda i, *_: (i, c))
 
     def third(c):
         return pl.BlockSpec((weights.shape[0], width), lambda i, *_: (0, c))
 
     flat = jax.ShapeDtypeStruct((rows, width), BF16)
+    wide = jax.ShapeDtypeStruct((rows, width), F32)
     return pl.pallas_call(
         feed_forward_kernel,
-        out_shape=(jax.ShapeDtypeStruct((step, width), F32), flat, flat, flat, flat, flat),
+        out_shape=(jax.ShapeDtypeStruct((step, width), F32), flat, flat, flat, flat, wide),
         grid_spec=pltpu.PrefetchScalarGridSpec(
             num_scalar_prefetch=1,
             grid=(ways,),
             in_specs=[
-                along(width),
-                pl.BlockSpec((ways, step, part), lambda i, *_: (0, i, 0)),
-                along(width),
+                along(0),
+                pl.BlockSpec((width, step), lambda i, *_: (0, i)),
+                along(1),
                 whole(vectors.shape),
                 third(0),
                 third(1),
                 third(2),
             ],
-            out_specs=[whole((step, width))] + [along(width)] * 5,
+            out_specs=[whole((step, width))] + [along(0)] * 5,
         ),
         compiler_params=params(),
         cost_estimate=pl.CostEstimate(
             flops=10 * rows * width * width, bytes_accessed=6 * width * width, transcendentals=rows * width
         ),
         name="feed_forward",
-    )(me, x, ctx, df, vectors, weights, weights, weights)
-
-
-def weight_grads_kernel(core, h2, du, act, df, ctx, dc, kept, sent, g_up, g_down, g_out, *, deep):
-    chips, rows, width = kept.shape
-    owners = 2 * chips
+    )(me, both, ctx, both, vectors, weights, weights, weights)
+
+
+def weight_grads_kernel(h2, du, act, df, ctx, dc, out, g_out):
+    owners, rows, width = out.shape
     each = h2.shape[1] // owners
-    few = ctx.shape[1] // owners
+    few = ctx.shape[0] // owners
     chunk = h2.shape[1] // 2
     for i in range(2):
         cols = slice(i * chunk, (i + 1) * chunk)
-        g_up[cols, :] = mm_tn(h2[:, cols], du[...])
-        g_down[cols, :] = mm_tn(act[:, cols], df[...])
-    g_out[...] = mm_tn(ctx[...], dc[...])
-
-    def put(target, which):
-        target[:, 2 * each :, :] = jnp.zeros((chips, rows - 2 * each, width), target.dtype)
-        for g in range(chips):
-            w = 2 * (g % (chips // deep) * deep + g // (chips // deep)) + which
-            target[g, :each, :] = g_up[w * each : (w + 1) * each, :].astype(target.dtype)
-            target[g, each : 2 * each, :] = g_down[w * each : (w + 1) * each, :].astype(target.dtype)
-            target[g, 2 * each : 2 * each + few, :] = g_out[w * few : (w + 1) * few, :].astype(
-                target.dtype
-            )
-
-    for which in range(2):
-
-        @pl.when(core[0] == which)
-        def _():
-            put(kept, which)
-            put(sent, 1 - which)
-
-
-def weight_grads(core, h2, du, act, df, ctx, dc, owners, deep):
-    width = du.shape[1]
+        mine = slice(i * owners // 2, (i + 1) * owners // 2)
+        shape = (owners // 2, each, width)
+        out[mine, :each, :] = mm_tn(h2[:, cols], du[...]).reshape(shape)
+        out[mine, each : 2 * each, :] = mm_tn(act[:, cols], df[...]).reshape(shape)
+    g_out[...] = mm(ctx[...], dc[...])
+    out[:, 2 * each :, :] = jnp.zeros((owners, rows - 2 * each, width), F32)
+    for w in range(owners):
+        out[w, 2 * each : 2 * each + few, :] = g_out[w * few : (w + 1) * few, :]
+
+
+def weight_grads(h2, du, act, both, ctx, dc, owners):
+    count, width = du.shape
     units = h2.shape[1]
-    rows = 2 * units // owners + 8
-    chips = owners // 2
-    arrays = (h2, du, act, df, ctx, dc)
-    kept, sent = pl.pallas_call(
-        functools.partial(weight_grads_kernel, deep=deep),
-        out_shape=(
-            jax.ShapeDtypeStruct((chips, rows, width), F32),
-            jax.ShapeDtypeStruct((chips, rows, width), BF16),
-        ),
+    shape = (owners, 2 * units // owners + 8, width)
+    out = pl.pallas_call(
+        weight_grads_kernel,
+        out_shape=jax.ShapeDtypeStruct(shape, F32),
         grid_spec=pltpu.PrefetchScalarGridSpec(
-            num_scalar_prefetch=1,
+            num_scalar_prefetch=0,
             grid=(1,),
-            in_specs=[whole(a.shape) for a in arrays],
-            out_specs=[whole((chips, rows, width))] * 2,
-            scratch_shapes=[
-                pltpu.VMEM((units, width), F32),
-                pltpu.VMEM((units, width), F32),
-                pltpu.VMEM((ctx.shape[1], width), F32),
+            in_specs=[
+                whole(h2.shape),
+                whole(du.shape),
+                whole(act.shape),
+                pl.BlockSpec((count, width), lambda i, *_: (0, 1)),
+                whole(ctx.shape),
+                whole(dc.shape),
             ],
+            out_specs=whole(shape),
+            scratch_shapes=[pltpu.VMEM((ctx.shape[0], width), F32)],
         ),
         compiler_params=params(),
         cost_estimate=pl.CostEstimate(
-            flops=4 * h2.size * width, bytes_accessed=6 * chips * rows * width, transcendentals=0
+            flops=4 * h2.size * width, bytes_accessed=8 * units * width, transcendentals=0
         ),
         name="weight_grads",
-    )(core, *arrays)
-    return kept, sent
+    )(h2, du, act, both, ctx, dc)
+    return out.reshape(shape[0] * shape[1], width)
 
 
 def normalized(values):
@@ -513,10 +495,6 @@
     sent = x.astype(BF16).reshape(ways, -1, x.shape[1])
     got = lax.all_to_all(sent, axis, split_axis=0, concat_axis=0, tiled=True)
     return jnp.sum(got.astype(F32), axis=0)
-
-
-def swapped(x, axis="core"):
-    return lax.ppermute(x, axis, [(0, 1), (1, 0)])
 
 
 def reduced(x, axis):
@@ -568,9 +546,6 @@
     count = order.shape[0]
     index = jnp.arange(count, dtype=jnp.int32)
     slots = jnp.sum(jnp.where(order[None, :] == index[:, None], index[None, :], 0), axis=1)
-    core = lax.axis_index("core")
-    deep = lax.axis_size("z")
-    flat = lax.axis_size(("batch", "xlo"))
 
     small = jnp.concatenate(
         [
@@ -584,6 +559,8 @@
     )
     qkv_slices = w_qkv[0].reshape(held, 3, ways, part).transpose(2, 0, 1, 3).reshape(ways, held, 3 * part)
     up_slices = w_up[0].reshape(held, wide, ways, ff_held).transpose(2, 0, 1, 3).reshape(ways, held, ff_part)
+    df_own = cotangent.astype(BF16)
+    both = lax.all_gather(jnp.concatenate([tokens, df_own], axis=1), "ulysses", axis=0, tiled=True)
     first = jnp.concatenate(
         [
             qkv_slices,
@@ -593,27 +570,15 @@
         axis=2,
     )
     blank = jnp.zeros((ways, 8 - held, width), BF16)
-    sent = jnp.concatenate(
-        [
-            jnp.broadcast_to(tokens[None], (ways,) + tokens.shape),
-            first,
-            blank,
-            up_slices,
-            blank,
-            jnp.broadcast_to(w_out[0][None], (ways, held, width)),
-            blank,
-        ],
-        axis=1,
-    )
+    wide_out = jnp.broadcast_to(w_out[0][None], (ways, held, width))
+    sent = jnp.concatenate([first, blank, up_slices, blank, wide_out, blank], axis=1)
     got = lax.all_to_all(sent, "ulysses", split_axis=0, concat_axis=0, tiled=True)
-    x = got[:, :own_rows].reshape(rows, width)
-    at = own_rows
-    piece = got[:, at : at + held, : 3 * part + 64].reshape(ways * held, 3 * part + 64)
+    piece = got[:, :held, : 3 * part + 64].reshape(ways * held, 3 * part + 64)
     filled = lax.all_gather(piece, WIDE, axis=0, tiled=True)
     ffn = jnp.concatenate(
         [
-            got[:, at + 8 : at + 8 + held].reshape(ways * held, width),
-            got[:, at + 16 : at + 16 + held].reshape(ways * held, width),
+            got[:, 8 : 8 + held].reshape(ways * held, width),
+            got[:, 16 : 16 + held].reshape(ways * held, width),
             w_down[0],
         ],
         axis=1,
@@ -630,7 +595,7 @@
     bias_q = lax.dynamic_slice(qv_all, (me * part,), (part,))
     bias_v = lax.dynamic_slice(qv_all, (width + me * part,), (part,))
 
-    n1, r1 = normalized(x.astype(F32))
+    n1, _ = normalized(both[:, :width].astype(F32))
     h1 = (n1 * gains[:width] + shifts[:width]).astype(BF16)
     proj_bias = jnp.concatenate([bias_q, jnp.zeros((part,), F32), bias_v])
     proj = (mm(h1, w_qkv_u) + proj_bias).astype(BF16)
@@ -639,14 +604,11 @@
     kv_all = lax.all_gather(kv, BLK, axis=0, tiled=True)
     q_heads = head_lanes(q_scaled, heads, 0)
 
-    df_own = cotangent.astype(BF16)
-    df_own, kv = lax.optimization_barrier((df_own, kv))
-    df = to_all(df_own).reshape(rows, width)
-    ffn, kv_all, df = lax.optimization_barrier((ffn, kv_all, df))
+    ffn, kv_all = lax.optimization_barrier((ffn, kv_all))
     ffn_all = lax.all_gather(ffn, WIDE, axis=0, tiled=True)
 
     ctx_low, ctx, lse = attend(slots, own, q_heads, kv_all, heads)
-    ctx_all = to_all(ctx_low)
+    ctx_all = to_all(ctx_low).reshape(width, rows)
     q_wide = jnp.pad(q_scaled, ((0, 0), (EXTRA, 0)))
     q_wide, ctx_all = lax.optimization_barrier((q_wide, ctx_all))
     q_all = lax.all_gather(q_wide, BLK, axis=0, tiled=True)
@@ -654,8 +616,13 @@
     vectors = jnp.stack(
         [gain_two, shifts[width:], out_bias_all, up_bias_u] + [jnp.zeros((width,), F32)] * 4
     )
-    x2_own, h2, act, du, dh2, down = feed_forward(me[None], x, ctx_all, df, vectors, ffn_all)
+    x2_own, h2, act, du, dh2, down = feed_forward(
+        me[None], both, ctx_all, vectors, ffn_all, ways
+    )
     dh2 = summed_at_owner(dh2)
+    ctx_rows = lax.dynamic_index_in_dim(
+        ctx_all.reshape(wide, ways, held, rows), me, axis=1, keepdims=False
+    ).reshape(part, rows)
     w_out_u = lax.dynamic_slice(ffn_all, (me * part, width), (part, width))
     g_up_bias = jnp.sum(du.astype(F32), axis=0)
     g_down_bias = jnp.sum(df_own.astype(F32), axis=0)
@@ -664,41 +631,33 @@
     dx2 = cotangent + norm_back(dh2, gain_two, n2_own, r2_own)
     g_gain_two = jnp.sum(dh2 * n2_own, axis=0)
     g_shift_two = jnp.sum(dh2, axis=0)
-    dc_own, q_all = lax.optimization_barrier((dx2.astype(BF16), q_all))
+    dc_own = dx2.astype(BF16)
     g_out_bias = jnp.sum(dc_own.astype(F32), axis=0)
     dc = to_all(dc_own).reshape(rows, width)
+    dc, q_all = lax.optimization_barrier((dc, q_all))
 
     w_out_wide = jnp.pad(w_out_u, ((EXTRA, 0), (0, 0)))
     packed, q_ext, d_ext = prepare(dc, w_out_wide, ctx, lse, q_heads, heads)
     packed_all = lax.all_gather(packed, BLK, axis=0, tiled=True)
     down, packed = lax.optimization_barrier((down, packed))
-    result = summed_at_owner(down) + x2_own + down_bias_all
-    early, early_sent = weight_grads(core[None], h2, du, act, df, ctx_low, dc, wide, deep)
-    early = early + swapped(early_sent).astype(F32)
-    early, q_ext = lax.optimization_barrier((early, q_ext))
-    early = reduced(early.reshape(deep, flat * early.shape[1], width), "z")
+    result = reduced(down.reshape(ways, own_rows, width), "ulysses") + x2_own + down_bias_all
+    early = weight_grads(h2, du, act, both, ctx_rows, dc, wide)
     d_query = query_grad(slots, own, q_ext, d_ext, kv_all, heads)
-    early, packed_all = lax.optimization_barrier((early, packed_all))
-    early = reduced(early.reshape(flat, -1, width), ("batch", "xlo"))
+    early, packed_all, d_query = lax.optimization_barrier((early, packed_all, d_query))
+    early = lax.psum_scatter(early, WIDE, scatter_dimension=0, tiled=True)
     k_heads = head_lanes(kv[:, :part], heads, EXTRA, 0)
     v_heads = head_lanes(kv[:, part:], heads, EXTRA, 3 * heads)
     d_key, d_value = key_grad(slots, own, k_heads, v_heads, q_all, packed_all, heads)
     d_proj = jnp.concatenate([d_query, d_key, d_value], axis=1)
-    dh1 = summed_at_owner(mm_nt(d_proj, w_qkv_u))
+    dh1_terms = mm_nt(d_proj, w_qkv_u)
+    dh1 = summed_at_owner(dh1_terms)
     g_w_qkv = mm_tn(h1, d_proj)
     n1_own, r1_own = normalized(tokens.astype(F32))
     d_tokens = dx2 + norm_back(dh1, gains[:width], n1_own, r1_own)
-    g_gain_one = jnp.sum(dh1 * n1_own, axis=0)
-    g_shift_one = jnp.sum(dh1, axis=0)
-
-    g_up_rows = early[:ff_held]
-    o_w_down = early[ff_held : 2 * ff_held]
-    out_rows = early[2 * ff_held : 2 * ff_held + held]
+    g_gain_one = jnp.sum(dh1_terms * n1, axis=0)
+    g_shift_one = jnp.sum(dh1_terms, axis=0)
+
     owners = wide * ways
-    o_w_out = lax.ppermute(
-        out_rows, ALL, [(w * ways + u, u * wide + w) for w in range(wide) for u in range(ways)]
-    )
-
     d_sums = jnp.sum(d_proj.astype(F32), axis=0)
     g_qv = jnp.zeros((2, ways, part), F32)
     g_qv = lax.dynamic_update_slice(g_qv, d_sums[:part].reshape(1, 1, part), (0, me, 0))
@@ -720,13 +679,8 @@
         axis=1,
     ).reshape(owners * held, pair)
     late = jnp.concatenate([g_w_qkv, jnp.pad(small_grads, ((0, 0), (0, 64 - pair)))], axis=1)
-    late = late.reshape(flat, deep, 2, ways * held, late.shape[1]).transpose(2, 1, 0, 3, 4)
-    late_sent = lax.dynamic_index_in_dim(late, 1 - core, axis=0, keepdims=False).astype(BF16)
-    late = lax.dynamic_index_in_dim(late, core, axis=0, keepdims=False)
-    late = late + swapped(late_sent).astype(F32)
-    late = reduced(late.reshape(deep, flat * ways * held, -1), "z")
-    late = reduced(late.reshape(flat, ways * held, -1), ("batch", "xlo"))
-    last = jnp.concatenate([late, g_up_rows], axis=1).reshape(ways, held, -1)
+    late = summed_at_owner(late, WIDE)
+    last = jnp.concatenate([late, early[:ff_held]], axis=1).reshape(ways, held, -1)
     last = lax.all_to_all(last, "ulysses", split_axis=0, concat_axis=0, tiled=True)
     o_w_qkv = last[:, :, : 3 * part].reshape(ways, held, 3, part).transpose(1, 2, 0, 3)
     o_small = jnp.sum(last[:, :, 3 * part : 3 * part + pair], axis=0)
@@ -738,11 +692,11 @@
         o_small[1:2],
         o_w_qkv.reshape(1, held, 3 * width),
         o_small[2:3],
-        o_w_out[None],
+        early[None, 2 * ff_held : 2 * ff_held + held],
         o_small[3:4, :held],
         o_w_up.reshape(1, held, -1),
         o_small[4:6].reshape(1, ff_held),
-        o_w_down[None],
+        early[None, ff_held : 2 * ff_held],
         o_small[3:4, held:],
     )
 

time: 396 us -> 356 us (0.90)
  starting transfers between devices: 61.5 us -> 37.2 us
  local copies, waits for them, and re-layouts: 50.7 us -> 36.7 us
    ppermute x12 -> x3, starting transfers between devices: 29.9 us -> 5.03 us  [reduced(): lax.ppermute(rows_of(k).astype(BF16), axis, [(i, (i + k) % ways) for i in...]
    all_gather x1, waiting for transfers between devices: 22.4 us -> 39.2 us  [on_device(): kv_all = lax.all_gather(kv, BLK, axis=0, tiled=True)]
    all_gather x1, waiting for transfers between devices: 0.01 us -> 15.5 us  [on_device(): packed_all = lax.all_gather(packed, BLK, axis=0, tiled=True)]
    all_to_all x2 -> x1, waiting for transfers between devices: 23.1 us -> 9.73 us  [to_all(): return lax.all_to_all(sent, axis, split_axis=0, concat_axis=0, tiled=True)]
    ppermute x12 -> x3, waiting for transfers between devices: 13.4 us -> 0.01 us  [reduced(): lax.ppermute(rows_of(k).astype(BF16), axis, [(i, (i + k) % ways) for i in...]
    all_gather x1, waiting for transfers between devices: 9.02 us -> 0.01 us  [on_device(): q_all = lax.all_gather(q_wide, BLK, axis=0, tiled=True)]
    all_to_all x1, waiting for transfers between devices: 13.9 us -> 6.06 us  [on_device(): lax.all_to_all(sent, 'ulysses', split_axis=0, concat_axis=0, tiled=True)]
    all_to_all x3, starting transfers between devices: 12.2 us -> 19.4 us  [summed_at_owner(): got = lax.all_to_all(sent, axis, split_axis=0, concat_axis=0, tiled=True)]
  transfers between devices with their start and end apart: 26 -> 15, of which waited for: 16 -> 10; matrix products, arithmetic and copies ran while one was open for 12% -> 14% of each run, Pallas kernels for 12% -> 19%
where the time goes in v3:
time: 356 us; the launch traced here: 351 us
  waiting for transfers between devices  121 us (34%)
  Pallas kernels  72.8 us (20%)
  blocking collectives  40 us (11%)
  starting transfers between devices  37.2 us (10%)
  local copies, waits for them, and re-layouts  36.7 us (10%)
  other arithmetic  20.4 us (6%)
  between operations  15.4 us (4%)
  matrix products  7.33 us (2%)
    pallas_call x4, Pallas kernels, call(): pl.pallas_call(functools.partial(kernel, **static), out_shape=tuple((jax....  55.9 us
    all_gather x1, waiting for transfers between devices, on_device(): kv_all = lax.all_gather(kv, BLK, axis=0, tiled=True)  39.2 us
    all_to_all x3, waiting for transfers between devices, summed_at_owner(): got = lax.all_to_all(sent, axis, split_axis=0, concat_axis=0, tiled=True)  27.8 us
    all_gather x1, blocking collectives, on_device(): filled = lax.all_gather(piece, WIDE, axis=0, tiled=True)  26.3 us
    all_to_all x3, starting transfers between devices, summed_at_owner(): got = lax.all_to_all(sent, axis, split_axis=0, concat_axis=0, tiled=True)  19.4 us
    all_gather x1, waiting for transfers between devices, on_device(): packed_all = lax.all_gather(packed, BLK, axis=0, tiled=True)  15.5 us
    all_gather x1, waiting for transfers between devices, on_device(): ffn_all = lax.all_gather(ffn, WIDE, axis=0, tiled=True)  13.9 us
    all_to_all x1, blocking collectives, to_all(): return lax.all_to_all(sent, axis, split_axis=0, concat_axis=0, tiled=True)  13.7 us
  transfers between devices with their start and end apart: 15, of which 10 were waited for; matrix products, arithmetic and copies ran while one was open for 14% of the time, Pallas kernels for 19%

profile of v3, /device:TPU:0, one launch (start us, length us, event | category | flops | bytes accessed | tf_op | source)
XLA Modules:
  0.0 351.1 jit_solution(7695250248674822439)
XLA Ops:
  7.3 1.1 fusion.39
  8.4 1.7 pad_maximum_fusion.2
  13.3 4.5 %all-to-all-start = ((bf16[4,24,768]{2,1,0:T(8,128)(2,1)}), bf16[4,24,768]{2,1,0:T(8,128)(2,1)S(1)}, u32[]{:S(2)}, u32[]{:S(2)}) async-start(bf16[4,24,768]{2,1,0:T(8,128)(2,1)} %copy.213), calls=%async_computation | async-start | bytes 294912 | tf_op jit(solution)/shard_map/all_to_all | solution.py:575
  17.8 6.1 %all-to-all-done = bf16[4,24,768]{2,1,0:T(8,128)(2,1)S(1)} async-done(((bf16[4,24,768]{2,1,0:T(8,128)(2,1)}), bf16[4,24,768]{2,1,0:T(8,128)(2,1)S(1)}, u32[]{:S(2)}, u32[]{:S(2)}) %all-to-all-start) | async-done | bytes 147488 | tf_op jit(solution)/shard_map/all_to_all | solution.py:575
  23.9 26.3 %all_gather.19 = bf16[768,640]{1,0:T(8,128)(2,1)S(1)} all-gather(bf16[24,640]{1,0:T(8,128)(2,1)S(1)} %reshape.344), channel_id=1, replica_groups=mesh['batch'=2,'xlo'=2,'z'=4,'core'=2,'ulysses'=4] {'batch','xlo','z','c..., dimensions={0}, use_global_device_ids=true | all-gather | bytes 1013760 | tf_op jit(solution)/shard_map/all_gather | solution.py:577
  54.2 1.4 convert_reduce_fusion.1
  55.7 1.5 fusion.7
  58.2 1.0 slice.151
  59.9 39.2 %all-gather.8.cloned.1.call-done.kv = bf16[8192,384]{1,0:T(8,128)(2,1)} async-done(((bf16[512,384]{1,0:T(8,128)(2,1)}), bf16[8192,384]{1,0:T(8,128)(2,1)}) %all-gather.8.cloned.1.call-update) | async-done | bytes 6291472 | tf_op jit(solution)/shard_map/all_gather | solution.py:604
  102.4 1.0 bitcast_select_fusion.2.q_heads
  103.4 11.3 %attend.1 = (bf16[192,512]{1,0:T(8,128)(2,1)}, f32[512,256]{1,0:T(8,128)}, f32[2,768,1]{2,1,0:T(8,128)}) custom-call(s32[32]{0:T(128)} %select_reduce_fusion.slots, s32[2]{0:T(128)} %fusion.34.own, bf16[2,768,256]{2,1,0:T(8,128)(2,1)} %bitcast_select_fusion.2.q_heads, bf16[8192,384]{1,0:T(8,128)(2,1)} %all-gather.8.cloned.1.call-done.kv), custom_call_target="tpu_custom_call" | custom-call | flops 12884901888 | bytes 6291456 | tf_op jit(solution)/shard_map/attend/pallas_call | solution.py:283
  114.7 1.0 broadcast_in_dim.186
  115.7 13.7 %all_to_all.35 = bf16[4,192,512]{2,1,0:T(8,128)(2,1)} all-to-all(bf16[4,192,512]{2,1,0:T(8,128)(2,1)S(1)} %broadcast_in_dim.186), channel_id=1, replica_groups=mesh['batch'=2,'xlo'=2,'z'=4,'core'=2,'ulysses'=4] {'ulysses'}, dimensions={0} | all-to-all | bytes 1572864 | tf_op jit(solution)/shard_map/all_to_all | solution.py:490
  130.9 1.0 fusion.40
  134.8 13.9 %all-gather.10.cloned.1.call-done.w_up.w_out.w_down = bf16[768,2304]{1,0:T(8,128)(2,1)} async-done(((bf16[24,2304]{1,0:T(8,128)(2,1)}), bf16[768,2304]{1,0:T(8,128)(2,1)}) %all-gather.10.cloned.1.call-update) | async-done | bytes 3538960 | tf_op jit(solution)/shard_map/all_gather | solution.py:608
  148.7 10.7 %feed_forward.1 = (f32[128,768]{1,0:T(8,128)}, bf16[512,768]{1,0:T(8,128)(2,1)}, bf16[512,768]{1,0:T(8,128)(2,1)}, bf16[512,768]{1,0:T(8,128)(2,1)}, bf16[512,768]{1,0:T(8,128)(2,1)}, /*index=5*/f32[512,768]{1,0:T(8,128)}) custom-call(s32[1]{0:T(128)} %bitcast.me, bf16[512,1536]{1,0:T(8,128)(2,1)} %all-gather.6.cloned.1.call-done.x.df, ...), custom_call_target="tpu_custom_call" | custom-call | flops 3019898880 | bytes 3538944 | tf_op jit(solution)/shard_map/feed_forward/pallas_call | solution.py:382
  159.4 4.4 %all-to-all-start.2 = ((bf16[4,128,768]{2,1,0:T(8,128)(2,1)}), bf16[4,128,768]{2,1,0:T(8,128)(2,1)S(1)}, u32[]{:S(2)}, u32[]{:S(2)}) async-start(bf16[4,128,768]{2,1,0:T(8,128)(2,1)} %bitcast.99), calls=%async_computation.2 | async-start | bytes 1572864 | tf_op jit(solution)/shard_map/all_to_all | solution.py:496
  164.2 12.2 %all-to-all-done.2 = bf16[4,128,768]{2,1,0:T(8,128)(2,1)S(1)} async-done(((bf16[4,128,768]{2,1,0:T(8,128)(2,1)}), bf16[4,128,768]{2,1,0:T(8,128)(2,1)S(1)}, u32[]{:S(2)}, u32[]{:S(2)}) %all-to-all-start.2) | async-done | bytes 786464 | tf_op jit(solution)/shard_map/all_to_all | solution.py:496
  176.9 1.0 fusion.38
  177.8 0.9 broadcast_in_dim.187
  178.7 3.5 all-to-all-start.3
  182.5 1.0 constant_dynamic-slice_fusion.2
  184.3 9.7 %all-to-all-done.3 = bf16[4,128,768]{2,1,0:T(8,128)(2,1)S(1)} async-done(((bf16[4,128,768]{2,1,0:T(8,128)(2,1)}), bf16[4,128,768]{2,1,0:T(8,128)(2,1)S(1)}, u32[]{:S(2)}, u32[]{:S(2)}) %all-to-all-start.3) | async-done | bytes 786464 | tf_op jit(solution)/shard_map/all_to_all | solution.py:490
  194.9 4.4 %prepare.1 = (bf16[512,256]{1,0:T(8,128)(2,1)}, bf16[2,768,256]{2,1,0:T(8,128)(2,1)}, bf16[2,768,256]{2,1,0:T(8,128)(2,1)}) custom-call(bf16[512,768]{1,0:T(8,128)(2,1)} %bitcast.89, bf16[256,768]{1,0:T(8,128)(2,1)} %pad.25.w_out, f32[512,256]{1,0:T(8,128)} %get-tuple-element.45.ctx, f32[2,768,1]{2,1,0:T(8,128)} %get-tuple-element.46.lse, ...), custom_call_target="tpu_custom_call" | custom-call | flops 201326592 | bytes 1572864 | tf_op jit(solution)/shard_map/prepare/pallas_call | solution.py:283
  200.5 6.2 %weight_grads.1 = f32[32,56,768]{2,1,0:T(8,128)} custom-call(bf16[512,768]{1,0:T(8,128)(2,1)} %get-tuple-element.49.h2, bf16[512,768]{1,0:T(8,128)(2,1)} %get-tuple-element.50.du, bf16[512,768]{1,0:T(8,128)(2,1)} %get-tuple-element.51.act, bf16[512,1536]{1,0:T(8,128)(2,1)} %all-gather.6.cloned.1.call-done.x.df, bf16[192,512]{1,0:T(8,128)(2,1)} %reshape.353.ctx, ...), custom_call_target="tpu_custom_call" | custom-call | flops 1207959552 | bytes 4718592 | tf_op jit(solution)/shard_map/weight_grads/pallas_call | solution.py:428
  206.7 12.2 %query_grad.1 = bf16[512,192]{1,0:T(8,128)(2,1)} custom-call(s32[32]{0:T(128)} %select_reduce_fusion.slots, s32[2]{0:T(128)} %fusion.34.own, bf16[2,768,256]{2,1,0:T(8,128)(2,1)} %get-tuple-element.52.q_ext, bf16[2,768,256]{2,1,0:T(8,128)(2,1)} %get-tuple-element.53.d_ext, bf16[8192,384]{1,0:T(8,128)(2,1)} %all-gather.8.cloned.1.call-done.kv), custom_call_target="tpu_custom_call" | custom-call | flops 19327352832 | bytes 6291456 | tf_op jit(solution)/shard_map/query_grad/pallas_call | solution.py:283
  218.9 15.5 %all-gather.14.cloned.1.call-done.p_all = bf16[8192,256]{1,0:T(8,128)(2,1)} async-done(((bf16[512,256]{1,0:T(8,128)(2,1)}), bf16[8192,256]{1,0:T(8,128)(2,1)}) %all-gather.14.cloned.1.call-update) | async-done | bytes 4194320 | tf_op jit(solution)/shard_map/all_gather | solution.py:641
  238.5 1.5 fusion.12
  242.2 2.1 fusion.27
  244.3 1.5 collective-permute-start
  245.8 1.8 collective-permute-start.2
  247.5 1.8 collective-permute-start.1
  249.3 27.9 %key_grad.1 = (bf16[512,192]{1,0:T(8,128)(2,1)}, bf16[512,192]{1,0:T(8,128)(2,1)}) custom-call(s32[32]{0:T(128)} %select_reduce_fusion.slots, s32[2]{0:T(128)} %fusion.34.own, bf16[2,768,256]{2,1,0:T(8,128)(2,1)} %get-tuple-element.172.k_heads, bf16[2,768,256]{2,1,0:T(8,128)(2,1)} %get-tuple-element.171.v_heads, ...), custom_call_target="tpu_custom_call" | custom-call | flops 25769803776 | bytes 6291456 | tf_op jit(solution)/shard_map/key_grad/pallas_call | solution.py:283
  277.3 3.4 fusion.37
  280.7 3.6 %all-to-all-start.4 = ((bf16[4,128,768]{2,1,0:T(8,128)(2,1)}), bf16[4,128,768]{2,1,0:T(8,128)(2,1)S(1)}, u32[]{:S(2)}, u32[]{:S(2)}) async-start(bf16[4,128,768]{2,1,0:T(8,128)(2,1)} %bitcast.98), calls=%async_computation.4 | async-start | bytes 1572864 | tf_op jit(solution)/shard_map/all_to_all | solution.py:496
  284.6 1.3 convert_reduce_fusion.5
  286.1 3.0 convolution_convert_fusion
  290.3 1.5 copy.225
  291.9 1.1 pad_maximum_fusion
  293.8 11.3 %all-to-all-start.5 = ((bf16[32,24,640]{2,1,0:T(8,128)(2,1)}), bf16[32,24,640]{2,1,0:T(8,128)(2,1)S(1)}, u32[]{:S(2)}, u32[]{:S(2)}) async-start(bf16[32,24,640]{2,1,0:T(8,128)(2,1)} %pad_maximum_fusion), calls=%async_computation.5 | async-start | bytes 1966080 | tf_op jit(solution)/shard_map/all_to_all | solution.py:496
  305.2 2.1 fusion.26
  307.8 14.7 %all-to-all-done.5 = bf16[32,24,640]{2,1,0:T(8,128)(2,1)S(1)} async-done(((bf16[32,24,640]{2,1,0:T(8,128)(2,1)}), bf16[32,24,640]{2,1,0:T(8,128)(2,1)S(1)}, u32[]{:S(2)}, u32[]{:S(2)}) %all-to-all-start.5) | async-done | bytes 983072 | tf_op jit(solution)/shard_map/all_to_all | solution.py:496
  322.6 4.4 %reduce-scatter.2.cloned.1.call-done = f32[56,768]{1,0:T(8,128)} async-done(((f32[1792,768]{1,0:T(8,128)}), f32[56,768]{1,0:T(8,128)}) %reduce-scatter.2.cloned.1.call-update) | async-done | bytes 172048 | tf_op jit(solution)/shard_map/reduce_scatter | solution.py:647
  327.0 1.6 slice_bitcast_fusion
  329.3 4.1 %all-to-all-start.6 = ((f32[4,6,1408]{2,1,0:T(8,128)}), f32[4,6,1408]{2,1,0:T(8,128)S(1)}, u32[]{:S(2)}, u32[]{:S(2)}) async-start(f32[4,6,1408]{2,1,0:T(8,128)} %reshape.364), calls=%async_computation.7 | async-start | bytes 360448 | tf_op jit(solution)/shard_map/all_to_all | solution.py:684
  333.4 0.9 fusion.21
  334.9 4.7 %all-to-all-done.6 = f32[4,6,1408]{2,1,0:T(8,128)S(1)} async-done(((f32[4,6,1408]{2,1,0:T(8,128)}), f32[4,6,1408]{2,1,0:T(8,128)S(1)}, u32[]{:S(2)}, u32[]{:S(2)}) %all-to-all-start.6) | async-done | bytes 135200 | tf_op jit(solution)/shard_map/all_to_all | solution.py:684
  342.9 1.1 reshape.374
  (247 shorter events, 33.6 us)
Async XLA Ops:
  7.2 3.4 copy-start.39
  7.2 4.2 %copy-start.20 = (bf16[1,6,2304]{2,1,0:T(8,128)(2,1)S(1)}, bf16[1,6,2304]{2,1,0:T(8,128)(2,1)}, u32[]{:S(2)}) copy-start(bf16[1,6,2304]{2,1,0:T(8,128)(2,1)} %param.17) | copy-start | bytes 82948
  7.2 4.4 %copy-start.15 = (bf16[1,6,3072]{2,1,0:T(8,128)(2,1)S(1)}, bf16[1,6,3072]{2,1,0:T(8,128)(2,1)}, u32[]{:S(2)}) copy-start(bf16[1,6,3072]{2,1,0:T(8,128)(2,1)} %param.21) | copy-start | bytes 110596
  7.2 5.1 %copy-start.40 = (bf16[1,6]{1,0:T(2,128)(2,1)S(1)}, bf16[1,6]{1,0:T(2,128)(2,1)}, u32[]{:S(2)}) copy-start(bf16[1,6]{1,0:T(2,128)(2,1)} %param.24) | copy-start | bytes 40
  7.2 5.1 %copy-start.41 = (bf16[1,6]{1,0:T(2,128)(2,1)S(1)}, bf16[1,6]{1,0:T(2,128)(2,1)}, u32[]{:S(2)}) copy-start(bf16[1,6]{1,0:T(2,128)(2,1)} %param.20) | copy-start | bytes 40
  7.2 5.1 %copy-start.38 = (bf16[1,12]{1,0:T(2,128)(2,1)S(1)}, bf16[1,12]{1,0:T(2,128)(2,1)}, u32[]{:S(2)}) copy-start(bf16[1,12]{1,0:T(2,128)(2,1)} %param.18) | copy-start | bytes 76
  7.2 5.1 %copy-start.37 = (bf16[1,12]{1,0:T(2,128)(2,1)S(1)}, bf16[1,12]{1,0:T(2,128)(2,1)}, u32[]{:S(2)}) copy-start(bf16[1,12]{1,0:T(2,128)(2,1)} %param.16) | copy-start | bytes 76
  7.3 5.1 %copy-start.36 = (bf16[1,12]{1,0:T(2,128)(2,1)S(1)}, bf16[1,12]{1,0:T(2,128)(2,1)}, u32[]{:S(2)}) copy-start(bf16[1,12]{1,0:T(2,128)(2,1)} %param.15) | copy-start | bytes 76
  7.3 5.3 %copy-start.22 = (bf16[1,6,768]{2,1,0:T(8,128)(2,1)S(1)}, bf16[1,6,768]{2,1,0:T(8,128)(2,1)}, u32[]{:S(2)}) copy-start(bf16[1,6,768]{2,1,0:T(8,128)(2,1)} %param.19) | copy-start | bytes 27652
  7.3 46.9 %all-gather.6.cloned.1.call-start = ((), (), s32[]{:S(2)}) async-start(), calls=%async_computation.8 | async-start | bytes 1966080 | tf_op jit(solution)/shard_map/all_gather | solution.py:563
  13.3 10.6 %all-to-all-start = ((bf16[4,24,768]{2,1,0:T(8,128)(2,1)}), bf16[4,24,768]{2,1,0:T(8,128)(2,1)S(1)}, u32[]{:S(2)}, u32[]{:S(2)}) async-start(bf16[4,24,768]{2,1,0:T(8,128)(2,1)} %copy.213), calls=%async_computation | async-start | bytes 294912 | tf_op jit(solution)/shard_map/all_to_all | solution.py:575
  17.8 81.3 %all-gather.8.cloned.1.call-start = ((), (), s32[]{:S(2)}) async-start(), calls=%async_computation.9 | async-start | bytes 6684672 | tf_op jit(solution)/shard_map/all_gather | solution.py:604
  50.2 6.9 %copy-start.10 = (bf16[768,640]{1,0:T(8,128)(2,1)}, bf16[768,640]{1,0:T(8,128)(2,1)S(1)}, u32[]{:S(2)}) copy-start(bf16[768,640]{1,0:T(8,128)(2,1)S(1)} %all_gather.19) | copy-start | bytes 2949124
  53.4 4.7 %copy-start.28 = (f32[768]{0:T(1024)}, f32[768]{0:T(1024)S(1)}, u32[]{:S(2)}) copy-start(f32[768]{0:T(1024)S(1)} %add.181) | copy-start | bytes 9220
  54.0 4.1 %copy-start.16 = (f32[768]{0:T(1024)}, f32[768]{0:T(1024)S(1)}, u32[]{:S(2)}) copy-start(f32[768]{0:T(1024)S(1)} %mul.141) | copy-start | bytes 9220
  58.2 41.2 %copy-start.42 = (s32[1,32]{1,0:T(1,128)S(1)}, s32[1,32]{1,0:T(1,128)}, u32[]{:S(2)}) copy-start(s32[1,32]{1,0:T(1,128)} %param.14) | copy-start | bytes 388
  59.2 89.5 %all-gather.10.cloned.1.call-start = ((), (), s32[]{:S(2)}) async-start(), calls=%async_computation.10 | async-start | bytes 3649536 | tf_op jit(solution)/shard_map/all_gather | solution.py:608
  99.1 94.9 %all-gather.12.cloned.1.call-start = ((), (), s32[]{:S(2)}) async-start(), calls=%async_computation.11 | async-start | bytes 4456448 | tf_op jit(solution)/shard_map/all_gather | solution.py:614
  159.4 4.6 %copy-start.2 = (f32[128,768]{1,0:T(8,128)S(1)}, f32[128,768]{1,0:T(8,128)}, u32[]{:S(2)}) copy-start(f32[128,768]{1,0:T(8,128)} %get-tuple-element.41) | copy-start | bytes 1179652
  159.4 17.1 %all-to-all-start.2 = ((bf16[4,128,768]{2,1,0:T(8,128)(2,1)}), bf16[4,128,768]{2,1,0:T(8,128)(2,1)S(1)}, u32[]{:S(2)}, u32[]{:S(2)}) async-start(bf16[4,128,768]{2,1,0:T(8,128)(2,1)} %bitcast.99), calls=%async_computation.2 | async-start | bytes 1572864 | tf_op jit(solution)/shard_map/all_to_all | solution.py:496
  163.8 13.1 %copy-start.7 = (f32[128,768]{1,0:T(8,128)S(1)}, f32[128,768]{1,0:T(8,128)}, u32[]{:S(2)}) copy-start(f32[128,768]{1,0:T(8,128)} %param.25) | copy-start | bytes 1179652
  178.7 15.3 %all-to-all-start.3 = ((bf16[4,128,768]{2,1,0:T(8,128)(2,1)}), bf16[4,128,768]{2,1,0:T(8,128)(2,1)S(1)}, u32[]{:S(2)}, u32[]{:S(2)}) async-start(bf16[4,128,768]{2,1,0:T(8,128)(2,1)} %broadcast_in_dim.187), calls=%async_computation.3 | async-start | bytes 1572864 | tf_op jit(solution)/shard_map/all_to_all | solution.py:490
  182.3 52.2 %all-gather.14.cloned.1.call-start = ((), (), s32[]{:S(2)}) async-start(), calls=%async_computation.12 | async-start | bytes 4456448 | tf_op jit(solution)/shard_map/all_gather | solution.py:641
  194.9 4.5 %copy-start.3 = (bf16[4,192,512]{2,1,0:T(8,128)(2,1)S(1)}, bf16[4,192,512]{2,1,0:T(8,128)(2,1)}, u32[]{:S(2)}) copy-start(bf16[4,192,512]{2,1,0:T(8,128)(2,1)} %all_to_all.35) | copy-start | bytes 2359300
  199.4 127.6 %reduce-scatter.2.cloned.1.call-start = ((), (), s32[]{:S(2)}) async-start(), calls=%async_computation.13 | async-start | bytes 5677056 | tf_op jit(solution)/shard_map/reduce_scatter | solution.py:647
  234.4 3.5 %copy-start.12 = (bf16[512,192]{1,0:T(8,128)(2,1)S(1)}, bf16[512,192]{1,0:T(8,128)(2,1)}, u32[]{:S(2)}) copy-start(bf16[512,192]{1,0:T(8,128)(2,1)} %get-tuple-element.166) | copy-start | bytes 589828
  235.5 4.5 %copy-start.26 = (f32[128]{0:T(128)}, f32[128]{0:T(128)S(1)}, u32[]{:S(2)}) copy-start(f32[128]{0:T(128)S(1)} %broadcast_multiply_fusion.3) | copy-start | bytes 1540
  244.3 60.9 %collective-permute-start = (bf16[128,768]{1,0:T(8,128)(2,1)}, bf16[128,768]{1,0:T(8,128)(2,1)}, u32[]{:S(2)}, u32[]{:S(2)}) collective-permute-start(bf16[128,768]{1,0:T(8,128)(2,1)} %get-tuple-element.157), channel_id=1, source_target_pairs={{0,1},{1,2},{2,3},{3,0},{4,5},{5,6},{6,7},{7,4},{8,9},{9,10},{10,1... | collective-permute-start | bytes 589832 | tf_op jit(solution)/shard_map/ppermute | solution.py:508
  245.8 59.5 %collective-permute-start.2 = (bf16[128,768]{1,0:T(8,128)(2,1)}, bf16[128,768]{1,0:T(8,128)(2,1)}, u32[]{:S(2)}, u32[]{:S(2)}) collective-permute-start(bf16[128,768]{1,0:T(8,128)(2,1)} %get-tuple-element.158), channel_id=1, source_target_pairs={{0,3},{1,0},{2,1},{3,2},{4,7},{5,4},{6,5},{7,6},{8,11},{9,8},{10,9... | collective-permute-start | bytes 589832 | tf_op jit(solution)/shard_map/ppermute | solution.py:508
  247.5 57.7 %collective-permute-start.1 = (bf16[128,768]{1,0:T(8,128)(2,1)}, bf16[128,768]{1,0:T(8,128)(2,1)}, u32[]{:S(2)}, u32[]{:S(2)}) collective-permute-start(bf16[128,768]{1,0:T(8,128)(2,1)} %get-tuple-element.159), channel_id=1, source_target_pairs={{0,2},{1,3},{2,0},{3,1},{4,6},{5,7},{6,4},{7,5},{8,10},{9,11},{10,... | collective-permute-start | bytes 589832 | tf_op jit(solution)/shard_map/ppermute | solution.py:508
  249.3 28.0 %copy-start.1 = (bf16[512,1536]{1,0:T(8,128)(2,1)S(1)}, bf16[512,1536]{1,0:T(8,128)(2,1)}, u32[]{:S(2)}) copy-start(bf16[512,1536]{1,0:T(8,128)(2,1)} %all-gather.6.cloned.1.call-done.x.df) | copy-start | bytes 4718596
  249.3 28.0 %copy-start.11 = (bf16[768,640]{1,0:T(8,128)(2,1)S(1)}, bf16[768,640]{1,0:T(8,128)(2,1)}, u32[]{:S(2)}) copy-start(bf16[768,640]{1,0:T(8,128)(2,1)} %copy-done.10) | copy-start | bytes 2949124
  249.3 28.0 %copy-start.13 = (bf16[512,192]{1,0:T(8,128)(2,1)S(1)}, bf16[512,192]{1,0:T(8,128)(2,1)}, u32[]{:S(2)}) copy-start(bf16[512,192]{1,0:T(8,128)(2,1)} %query_grad.1) | copy-start | bytes 589828
  249.3 28.0 %copy-start.24 = (f32[512]{0:T(512)S(1)}, f32[512]{0:T(512)}, u32[]{:S(2)}) copy-start(f32[512]{0:T(512)} %copy-done.23) | copy-start | bytes 6148
  249.3 28.0 %copy-start.34 = (f32[512]{0:T(512)S(1)}, f32[512]{0:T(512)}, u32[]{:S(2)}) copy-start(f32[512]{0:T(512)} %copy-done.33) | copy-start | bytes 6148
  280.7 3.7 %copy-start.32 = (bf16[768]{0:T(1024)(128)(2,1)S(1)}, bf16[768]{0:T(1024)(128)(2,1)}, u32[]{:S(2)}) copy-start(bf16[768]{0:T(1024)(128)(2,1)} %get-tuple-element.144) | copy-start | bytes 4612
  280.7 3.8 %copy-start.31 = (bf16[768]{0:T(1024)(128)(2,1)S(1)}, bf16[768]{0:T(1024)(128)(2,1)}, u32[]{:S(2)}) copy-start(bf16[768]{0:T(1024)(128)(2,1)} %get-tuple-element.145) | copy-start | bytes 4612
  280.7 5.3 %copy-start.14 = (bf16[64,1,12]{2,0,1:T(8,128)(2,1)S(1)}, bf16[64,1,12]{2,0,1:T(8,128)(2,1)}, u32[]{:S(2)}) copy-start(bf16[64,1,12]{2,0,1:T(8,128)(2,1)} %concatenate.72) | copy-start | bytes 4612
  280.7 5.4 %copy-start.17 = (f32[768]{0:T(1024)S(1)}, f32[768]{0:T(1024)}, u32[]{:S(2)}) copy-start(f32[768]{0:T(1024)} %copy-done.16) | copy-start | bytes 9220
  280.7 5.4 %copy-start.25 = (f32[512]{0:T(512)S(1)}, f32[512]{0:T(512)}, u32[]{:S(2)}) copy-start(f32[512]{0:T(512)} %copy-done.23) | copy-start | bytes 6148
  280.7 5.4 %copy-start.29 = (f32[768]{0:T(1024)S(1)}, f32[768]{0:T(1024)}, u32[]{:S(2)}) copy-start(f32[768]{0:T(1024)} %copy-done.28) | copy-start | bytes 9220
  280.7 5.4 %copy-start.35 = (f32[512]{0:T(512)S(1)}, f32[512]{0:T(512)}, u32[]{:S(2)}) copy-start(f32[512]{0:T(512)} %copy-done.33) | copy-start | bytes 6148
  280.7 13.1 %all-to-all-start.4 = ((bf16[4,128,768]{2,1,0:T(8,128)(2,1)}), bf16[4,128,768]{2,1,0:T(8,128)(2,1)S(1)}, u32[]{:S(2)}, u32[]{:S(2)}) async-start(bf16[4,128,768]{2,1,0:T(8,128)(2,1)} %bitcast.98), calls=%async_computation.4 | async-start | bytes 1572864 | tf_op jit(solution)/shard_map/all_to_all | solution.py:496
  291.9 13.4 %copy-start.21 = (f32[768]{0:T(1024)S(1)}, f32[768]{0:T(1024)}, u32[]{:S(2)}) copy-start(f32[768]{0:T(1024)} %add.207) | copy-start | bytes 9220
  293.8 28.6 %all-to-all-start.5 = ((bf16[32,24,640]{2,1,0:T(8,128)(2,1)}), bf16[32,24,640]{2,1,0:T(8,128)(2,1)S(1)}, u32[]{:S(2)}, u32[]{:S(2)}) async-start(bf16[32,24,640]{2,1,0:T(8,128)(2,1)} %pad_maximum_fusion), calls=%async_computation.5 | async-start | bytes 1966080 | tf_op jit(solution)/shard_map/all_to_all | solution.py:496
  307.5 25.9 %copy-start.8 = (f32[128,768]{1,0:T(8,128)S(1)}, f32[128,768]{1,0:T(8,128)}, u32[]{:S(2)}) copy-start(f32[128,768]{1,0:T(8,128)} %get-tuple-element.153) | copy-start | bytes 1179652
  327.0 7.3 %slice-start = ((f32[56,768]{1,0:T(8,128)}), f32[6,768]{1,0:T(8,128)S(1)}, s32[]{:S(2)}) async-start(f32[56,768]{1,0:T(8,128)} %reduce-scatter.2.cloned.1.call-done), calls=%async_computation.14 | async-start | bytes 49152 | tf_op jit(solution)/shard_map/slice | solution.py:695
  329.3 10.3 %all-to-all-start.6 = ((f32[4,6,1408]{2,1,0:T(8,128)}), f32[4,6,1408]{2,1,0:T(8,128)S(1)}, u32[]{:S(2)}, u32[]{:S(2)}) async-start(f32[4,6,1408]{2,1,0:T(8,128)} %reshape.364), calls=%async_computation.7 | async-start | bytes 360448 | tf_op jit(solution)/shard_map/all_to_all | solution.py:684
  (11 other events, 20.0 us)
Sparse Core Ops, SparseCore 0:
  10.3 28.9 all-gather.5
  59.3 39.7 all-gather.7
  102.0 46.6 all-gather.9
  150.3 36.7 all-gather.11
  199.5 34.8 all-gather.13
  238.0 88.9 reduce-scatter.1
